TPU v7x, 32 devices: a whole 2x2x4 slice. The times are simulated.
32 devices in a mesh: dp: 4 (over y, x), row: 4 (over z), col: 2 (over core).
Axes of the slice: x: 2, y: 2, z: 4, core: 2. Of those that a mesh axis runs over, the one named last changes fastest.
Arguments:
- inputs: bfloat16 [2916, 1152], P('dp', ('row', 'col')), may hold values from -11 to 11
- cotangent: bfloat16 [2916, 1152], P('dp', ('row', 'col')), may hold values from -6 to 6
- qkv_master: float32 [288, 4, 3456], P('row', 'dp', 'col'), may hold values from -0.1875 to 0.1875
- out_master: float32 [1152, 288, 4], P('col', 'row', 'dp'), may hold values from -1 to 1
- up_master: float32 [288, 4, 4304], P('row', 'dp', 'col'), may hold values from -0.20623948 to 0.20623948
- down_master: float32 [4304, 288, 4], P('col', 'row', 'dp'), may hold values from -0.09375 to 0.09375
- qkv_first: float32 [288, 4, 3456], P('row', 'dp', 'col'), may hold values from -16 to 16
- out_first: float32 [1152, 288, 4], P('col', 'row', 'dp'), may hold values from -6 to 6
- up_first: float32 [288, 4, 4304], P('row', 'dp', 'col'), may hold values from -6 to 6
- down_first: float32 [4304, 288, 4], P('col', 'row', 'dp'), may hold values from -20 to 20
- qkv_second: float32 [288, 4, 3456], P('row', 'dp', 'col'), may hold values from 0.729 to 2.916
- out_second: float32 [1152, 288, 4], P('col', 'row', 'dp'), may hold values from 0.06561 to 0.26244
- up_second: float32 [288, 4, 4304], P('row', 'dp', 'col'), may hold values from 0.26244 to 1.04976
- down_second: float32 [4304, 288, 4], P('col', 'row', 'dp'), may hold values from 1.04976 to 4.19904
- norm_gains: float32 [2, 1152], replicated, may hold values from 0.5 to 1.5
- gain_first: float32 [2, 1152], replicated, may hold values from -32 to 32
- gain_second: float32 [2, 1152], replicated, may hold values from 2.916 to 11.664
- biases: float32 [11216], replicated, may hold values from -1.5 to 1.5
- bias_first: float32 [11216], replicated, may hold values from -32 to 32
- bias_second: float32 [11216], replicated, may hold values from 2.916 to 11.664
Outputs:
- outputs: bfloat16 [2916, 1152], P('dp', ('row', 'col'))
- input_grad: bfloat16 [2916, 1152], P('dp', ('row', 'col'))
- new_qkv: float32 [288, 4, 3456], P('row', 'dp', 'col')
- new_qkv_first: float32 [288, 4, 3456], P('row', 'dp', 'col')
- new_qkv_second: float32 [288, 4, 3456], P('row', 'dp', 'col')
- new_out: float32 [1152, 288, 4], P('col', 'row', 'dp')
- new_out_first: float32 [1152, 288, 4], P('col', 'row', 'dp')
- new_out_second: float32 [1152, 288, 4], P('col', 'row', 'dp')
- new_up: float32 [288, 4, 4304], P('row', 'dp', 'col')
- new_up_first: float32 [288, 4, 4304], P('row', 'dp', 'col')
- new_up_second: float32 [288, 4, 4304], P('row', 'dp', 'col')
- new_down: float32 [4304, 288, 4], P('col', 'row', 'dp')
- new_down_first: float32 [4304, 288, 4], P('col', 'row', 'dp')
- new_down_second: float32 [4304, 288, 4], P('col', 'row', 'dp')
- new_gains: float32 [2, 1152], replicated
- new_gain_first: float32 [2, 1152], replicated
- new_gain_second: float32 [2, 1152], replicated
- new_biases: float32 [11216], replicated
- new_bias_first: float32 [11216], replicated
- new_bias_second: float32 [11216], replicated
All inputs are finite; a program needn't handle non-finite values.
Results may differ from a plain program's by a relative error of at most 0.02.
Values may be sent and summed in bfloat16 or wider, within the bound.
No kernel may reach another device: no remote copies, remote signals or barrier semaphores. Data moves between devices by JAX's collectives and lax.ppermute only.
A program may use at most 128 MiB of HBM per device.

v0:
```python
from functools import partial

import jax
import jax.numpy as jnp
from jax import lax
from jax.experimental import pallas as pl
from jax.experimental.pallas import tpu as pltpu
from jax.sharding import PartitionSpec as P

D = 1152
FF = 4304
HEAD = 72
SEQ = 729
STEP = 10

NORM_EPS = 1e-06
ADAM_EPS = 1e-08
BETA_ONE = 0.9
BETA_TWO = 0.999
LOW = jnp.bfloat16


def dot(left, right, left_dim, right_dim, out=jnp.float32, precision=None):
    return lax.dot_general(
        left,
        right,
        (((left_dim,), (right_dim,)), ((), ())),
        precision=precision,
        preferred_element_type=out,
    )


def take(array, index, size):
    return lax.dynamic_slice_in_dim(array, index * size, size, axis=0)


def swap_cores(array):
    n_col = lax.axis_size("col")
    return lax.ppermute(array, "col", [(i, (i + 1) % n_col) for i in range(n_col)])


def both_cores(rows):
    pieces = [
        lax.all_gather(piece, "col", axis=0) for piece in jnp.split(rows, 2, axis=0)
    ]
    return jnp.concatenate(pieces, axis=1).reshape(-1, rows.shape[1])


def gather_parts(block, axis):
    size = lax.axis_size(axis)
    if size > 4:
        copies = jnp.broadcast_to(block, (size,) + block.shape)
        return [lax.all_to_all(copies, axis, 0, 0).reshape(-1, block.shape[1])]
    return [block] + [
        lax.ppermute(block, axis, [(i, i ^ step) for i in range(size)]) for step in range(1, size)
    ]


def zero_of(array):
    first = lax.slice(array, (0,) * array.ndim, (1,) * array.ndim)
    return first.reshape(()).astype(jnp.float32) * 0.0


def exchange_rows(blocks):
    return lax.all_to_all(blocks, "row", 0, 0)


def sum_blocks(blocks, axis, later):
    blocks = lax.all_to_all(blocks, axis, 0, 0)
    return jnp.sum(blocks.astype(jnp.float32) + later, axis=0).astype(LOW)


def sum_over_rows(half):
    summed = lax.psum_scatter(half.astype(LOW), "row", scatter_dimension=0, tiled=True)
    return summed.astype(jnp.float32)


def all_sum(vector):
    for axis in ("col", "row", "dp"):
        size = lax.axis_size(axis)
        if size & (size - 1) or size > 4:
            vector = lax.psum(vector, axis)
            continue
        step = 1
        while step < size:
            vector = vector + lax.ppermute(vector, axis, [(i, i ^ step) for i in range(size)])
            step *= 2
    return vector


VMEM = pl.BlockSpec(memory_space=pltpu.VMEM)
SMEM = pl.BlockSpec(memory_space=pltpu.SMEM)
ANY = pl.BlockSpec(memory_space=pl.ANY)
BIG = pltpu.CompilerParams(vmem_limit_bytes=56 * 1024 * 1024)


def prepare_kernel(parts, after_ref, wide_ref, tall_ref, out_ref):
    del after_ref
    arrays = [ref[:, 0, :].astype(LOW) for ref in (wide_ref, tall_ref)]
    for part in range(parts):
        pieces = []
        for array in arrays:
            size = array.shape[1] // parts
            pieces.append(array[:, part * size : (part + 1) * size])
        out_ref[part] = jnp.concatenate(pieces, axis=1)


def prepare(after, wide, tall, parts):
    rows = wide.shape[0]
    size = (wide.shape[2] + tall.shape[2]) // parts
    return pl.pallas_call(
        partial(prepare_kernel, parts),
        in_specs=[ANY, VMEM, VMEM],
        out_specs=VMEM,
        out_shape=jax.ShapeDtypeStruct((parts, rows, size), LOW),
        compiler_params=BIG,
        name="prepare",
    )(after, wide, tall)


def adam_kernel(rates, after_ref, blocks_ref, *refs):
    del after_ref
    parts = blocks_ref.shape[0]
    start = 0
    for index, rate in enumerate(rates):
        weight, first, second = refs[3 * index : 3 * index + 3]
        size = weight.shape[2] // parts
        gradient = jnp.concatenate(
            [blocks_ref[part, :, start : start + size] for part in range(parts)], axis=1
        ).astype(jnp.float32)
        start += size
        new = adam_update(weight[:, 0, :], first[:, 0, :], second[:, 0, :], gradient, rate, 0.1)
        for array, ref in zip(new, refs[3 * len(rates) + 3 * index :]):
            ref[:, 0, :] = array


def adam(after, blocks, rates, *arrays):
    return pl.pallas_call(
        partial(adam_kernel, rates),
        in_specs=[ANY] + [VMEM] * (1 + len(arrays)),
        out_specs=[VMEM] * len(arrays),
        out_shape=[jax.ShapeDtypeStruct(a.shape, jnp.float32) for a in arrays],
        compiler_params=BIG,
        name="adam",
    )(after, blocks, *arrays)


def assembled(place, parts, scratch):
    if len(parts) == 1:
        return parts[0][...]
    for step, part in enumerate(parts):
        scratch[place ^ step] = part[...]
    return scratch[...].reshape(-1, scratch.shape[2])


def part_scratch(parts):
    return pltpu.VMEM((len(parts),) + parts[0].shape, LOW)


def head_probs(queries, key_rows):
    scores = dot(queries, key_rows, 0, 0) * HEAD ** (-0.5)
    scores = jnp.where(lax.broadcasted_iota(jnp.int32, scores.shape, 1) < SEQ, scores, -1e30)
    exponent = jnp.exp(scores - jnp.max(scores, axis=1, keepdims=True))
    return exponent * (1.0 / jnp.sum(exponent, axis=1, keepdims=True))


def split_cores(core, first, second, theirs_ref, mine_ref):
    @pl.when(core == 0)
    def _():
        mine_ref[...] = first
        theirs_ref[...] = second

    @pl.when(core != 0)
    def _():
        mine_ref[...] = second
        theirs_ref[...] = first


def attend_kernel(place_ref, after_ref, za_ref, bias_ref, *refs):
    del after_ref
    *parts, w_ref, qkv_ref, att_ref, theirs_ref, mine_ref, scratch = refs
    w_ref[...] = assembled(place_ref[1], parts, scratch)
    heads = qkv_ref.shape[0]
    split = heads * 3 * HEAD
    qkv = dot(w_ref[:, :split], za_ref[...], 0, 0) + bias_ref[...]
    outs = []
    for head in range(heads):
        for t in range(3):
            start = (head * 3 + t) * HEAD
            qkv_ref[head, t] = qkv[start : start + HEAD].astype(LOW)
        probs = head_probs(qkv_ref[head, 0], qkv_ref[head, 1]).astype(LOW)
        outs.append(dot(qkv_ref[head, 2], probs, 1, 1))
    attended = jnp.concatenate(outs, axis=0).T.astype(LOW)
    att_ref[...] = attended
    branch = dot(attended, w_ref[:, split:], 1, 1).astype(LOW)
    half = branch.shape[0] // 2
    split_cores(place_ref[0], branch[:half], branch[half:], theirs_ref, mine_ref)


def attend(place, after, za, qkv_bias, parts, width):
    tokens = za.shape[1]
    return pl.pallas_call(
        attend_kernel,
        in_specs=[SMEM, ANY, VMEM, VMEM] + [VMEM] * len(parts),
        out_specs=[VMEM] * 5,
        out_shape=(
            jax.ShapeDtypeStruct((D, 4 * width), LOW),
            jax.ShapeDtypeStruct((width // HEAD, 3, HEAD, tokens), LOW),
            jax.ShapeDtypeStruct((tokens, width), LOW),
            jax.ShapeDtypeStruct((tokens // 2, D), LOW),
            jax.ShapeDtypeStruct((tokens // 2, D), LOW),
        ),
        scratch_shapes=[part_scratch(parts)],
        compiler_params=BIG,
        name="attend",
    )(place, after, za, qkv_bias, *parts)


def own_tokens(place_ref, chunk, tokens):
    pick = lax.broadcasted_iota(jnp.int32, (chunk, tokens), 0) + place_ref[2] * chunk
    return (lax.broadcasted_iota(jnp.int32, (chunk, tokens), 1) == pick).astype(LOW)


def beside_kernel(n_row, place_ref, after_ref, order_ref, cot_ref, w_ref, x_ref, tokens_ref, mixed_ref, mine_ref):
    del after_ref
    group, width = cot_ref.shape[:2]
    n_col = group // n_row
    order = order_ref[...]
    cot = [cot_ref[row * n_col + core] for core in range(n_col) for row in range(n_row)]
    tokens_ref[...] = dot(jnp.concatenate(cot, axis=0), order, 0, 0).astype(LOW)
    mixed_ref[...] = dot(order, w_ref[:, : 3 * width], 1, 0).astype(LOW)
    pick = own_tokens(place_ref, mine_ref.shape[0], x_ref.shape[1])
    mine_ref[...] = dot(dot(pick, x_ref[...], 1, 1).astype(LOW), order, 1, 0)


def beside(place, after, order, cot_all, w_first, x_all, n_row, chunk):
    group, width, tokens = cot_all.shape
    return pl.pallas_call(
        partial(beside_kernel, n_row),
        in_specs=[SMEM, ANY] + [VMEM] * 4,
        out_specs=[VMEM] * 3,
        out_shape=(
            jax.ShapeDtypeStruct((tokens, D), LOW),
            jax.ShapeDtypeStruct((D, 3 * width), LOW),
            jax.ShapeDtypeStruct((chunk, D), jnp.float32),
        ),
        compiler_params=BIG,
        name="beside",
    )(place, after, order, cot_all, w_first, x_all)


def before_kernel(place_ref, after_ref, order_ref, cot_ref, *refs):
    del after_ref
    *parts, up_ref, grad_ref, mixed_ref, scratch = refs
    w_rest = assembled(place_ref[1], parts, scratch)
    wide = up_ref.shape[1]
    up_ref[...] = w_rest[:, :wide]
    w_down = w_rest[:, wide:]
    grad_ref[...] = dot(cot_ref[...], w_down, 1, 0)
    mixed_ref[...] = dot(order_ref[...], w_down, 1, 0).astype(LOW)


def before(place, after, order, cot_tokens, parts):
    wide = parts[0].shape[1] // 2
    return pl.pallas_call(
        before_kernel,
        in_specs=[SMEM, ANY, VMEM, VMEM] + [VMEM] * len(parts),
        out_specs=[VMEM] * 3,
        out_shape=(
            jax.ShapeDtypeStruct((D, wide), LOW),
            jax.ShapeDtypeStruct((cot_tokens.shape[0], wide), jnp.float32),
            jax.ShapeDtypeStruct((D, wide), LOW),
        ),
        scratch_shapes=[part_scratch(parts)],
        compiler_params=BIG,
        name="before",
    )(place, after, order, cot_tokens, *parts)


def behind_kernel(
    place_ref, after_ref, zb_ref, hid_ref, cot_ref, act_ref, down_ref, mid_ref, grad_ref, theirs_ref, mine_ref
):
    del after_ref
    active = act_ref[...]
    up_grad = dot(zb_ref[...], hid_ref[...], 0, 0).astype(LOW)
    down_grad = dot(cot_ref[...], active, 0, 0).astype(LOW)
    grad_ref[...] = jnp.concatenate([up_grad, down_grad], axis=1).reshape(grad_ref.shape)
    pick = own_tokens(place_ref, mid_ref.shape[1], active.shape[0])
    result = dot(down_ref[...], active, 1, 1) + dot(mid_ref[...], pick, 1, 0)
    result = result.astype(LOW)
    half = D // 2
    split_cores(place_ref[0], result[:half], result[half:], theirs_ref, mine_ref)


def behind(place, after, zb, hidden_grad, cot_tokens, active, down_mixed, middle_mixed, n_dp):
    tokens, wide = active.shape
    return pl.pallas_call(
        behind_kernel,
        in_specs=[SMEM, ANY] + [VMEM] * 6,
        out_specs=[VMEM] * 3,
        out_shape=(
            jax.ShapeDtypeStruct((n_dp, D // n_dp, 2 * wide), LOW),
            jax.ShapeDtypeStruct((D // 2, tokens), LOW),
            jax.ShapeDtypeStruct((D // 2, tokens), LOW),
        ),
        compiler_params=BIG,
        name="behind",
    )(place, after, zb, hidden_grad, cot_tokens, active, down_mixed, middle_mixed)


def mlp_kernel(
    core_ref, zb_ref, up_ref, bias_ref, grad_ref, act_ref, hid_ref, theirs_ref, mine_ref, sum_ref
):
    step = pl.program_id(0)
    near = step >= pl.num_programs(0) // 2
    hidden = dot(zb_ref[...], up_ref[...], 1, 0) + bias_ref[...]
    square = hidden * hidden
    slope = 0.7978845608028654 * (1.0 + 0.044715 * square)
    bent = jnp.tanh(hidden * slope)
    gate = 0.5 * (1.0 + bent)
    act_ref[...] = (hidden * gate).astype(LOW)
    steep = gate + 0.5 * hidden * (1.0 - bent * bent) * (
        0.7978845608028654 * (1.0 + 3 * 0.044715 * square)
    )
    hidden_grad = (grad_ref[...] * steep).astype(LOW)
    hid_ref[...] = hidden_grad
    two_grad = dot(hidden_grad, up_ref[...], 1, 1).astype(LOW)

    @pl.when(near)
    def _():
        mine_ref[...] = two_grad

    @pl.when(jnp.logical_not(near))
    def _():
        theirs_ref[...] = two_grad

    @pl.when(step == 0)
    def _():
        sum_ref[...] = jnp.zeros(sum_ref.shape, jnp.float32)

    sum_ref[...] += jnp.sum(hidden_grad.astype(jnp.float32), axis=0, keepdims=True)


def mlp(core, zb, w_up, up_bias, active_grad):
    tokens = zb.shape[0]
    wide = w_up.shape[1]
    steps = 6
    block = tokens // steps
    turned = lambda i, c: ((i + (steps // 2) * (1 - c[0])) % steps, 0)
    whole = lambda i, c: (0, 0)
    return pl.pallas_call(
        mlp_kernel,
        grid_spec=pltpu.PrefetchScalarGridSpec(
            num_scalar_prefetch=1,
            grid=(steps,),
            in_specs=[
                pl.BlockSpec((block, D), turned),
                pl.BlockSpec((D, wide), whole),
                pl.BlockSpec((1, wide), whole),
                pl.BlockSpec((block, wide), turned),
            ],
            out_specs=[
                pl.BlockSpec((block, wide), turned),
                pl.BlockSpec((block, wide), turned),
                pl.BlockSpec((block, D), lambda i, c: (jnp.minimum(i, steps // 2 - 1), 0)),
                pl.BlockSpec((block, D), lambda i, c: (jnp.maximum(i - steps // 2, 0), 0)),
                pl.BlockSpec((1, wide), whole),
            ],
        ),
        out_shape=(
            jax.ShapeDtypeStruct((tokens, wide), LOW),
            jax.ShapeDtypeStruct((tokens, wide), LOW),
            jax.ShapeDtypeStruct((tokens // 2, D), LOW),
            jax.ShapeDtypeStruct((tokens // 2, D), LOW),
            jax.ShapeDtypeStruct((1, wide), jnp.float32),
        ),
        compiler_params=BIG,
        name="mlp",
    )(core, zb, w_up, up_bias, active_grad)


def back_kernel(bg_ref, w_ref, qkv_ref, za_ref, att_ref, grad_ref, sum_ref, wg_ref):
    heads = qkv_ref.shape[0]
    attended_grad = dot(bg_ref[...], w_ref[:, heads * 3 * HEAD :], 1, 0).T
    scale = HEAD ** (-0.5)
    parts = []
    for head in range(heads):
        queries, key_rows, values = qkv_ref[head, 0], qkv_ref[head, 1], qkv_ref[head, 2]
        grad = attended_grad[head * HEAD : (head + 1) * HEAD].astype(LOW)
        probs = head_probs(queries, key_rows)
        probs_grad = dot(grad, values, 0, 0)
        inner = jnp.sum(probs * probs_grad, axis=1, keepdims=True)
        scores_grad = (probs * (probs_grad - inner)).astype(LOW)
        parts.append(dot(key_rows, scores_grad, 1, 1) * scale)
        parts.append(dot(queries, scores_grad, 1, 0) * scale)
        parts.append(dot(grad, probs.astype(LOW), 1, 0))
    qkv_grad = jnp.concatenate(parts, axis=0).astype(LOW)
    grad_ref[...] = qkv_grad
    sum_ref[...] = jnp.sum(qkv_grad.astype(jnp.float32), axis=1, keepdims=True)
    qkv_part = dot(za_ref[...], qkv_grad, 1, 1).astype(LOW)
    out_part = dot(bg_ref[...], att_ref[...], 0, 0).astype(LOW)
    wg_ref[...] = jnp.concatenate([qkv_part, out_part], axis=1).reshape(wg_ref.shape)


def attend_back(branch_all, w_first, qkv, za, attended, n_dp):
    tokens, width = attended.shape
    return pl.pallas_call(
        back_kernel,
        in_specs=[VMEM] * 5,
        out_specs=[VMEM] * 3,
        out_shape=(
            jax.ShapeDtypeStruct((3 * width, tokens), LOW),
            jax.ShapeDtypeStruct((3 * width, 1), jnp.float32),
            jax.ShapeDtypeStruct((n_dp, D // n_dp, 4 * width), LOW),
        ),
        compiler_params=BIG,
        name="attend_back",
    )(branch_all, w_first, qkv, za, attended)


def first_kernel(core_ref, w_ref, grad_ref, x_ref, mean_ref, inv_ref, gain_ref, theirs_ref, mine_ref, sum_ref):
    n_row, rows, tokens = theirs_ref.shape
    width = rows - 16
    first = jnp.zeros((1, tokens), jnp.float32)
    second = jnp.zeros((1, tokens), jnp.float32)
    blocks = []
    for slot in range(D // width):
        here = slice(slot * width, (slot + 1) * width)
        part = dot(w_ref[here], grad_ref[...], 1, 0)
        normed = (x_ref[here].astype(jnp.float32) - mean_ref[...]) * inv_ref[...]
        product = part * normed
        sum_ref[here, 0:1] = jnp.sum(product, axis=1, keepdims=True)
        sum_ref[here, 1:2] = jnp.sum(part, axis=1, keepdims=True)
        first += jnp.sum(part * gain_ref[here], axis=0, keepdims=True)
        second += jnp.sum(product * gain_ref[here], axis=0, keepdims=True)
        blocks.append(part.astype(LOW))
    line = lax.broadcasted_iota(jnp.int32, (16, tokens), 0)
    sums = jnp.where(line == 0, first, jnp.where(line == 1, second, 0.0)).astype(LOW)
    for near, ref in ((False, theirs_ref), (True, mine_ref)):
        for core in range(2):

            @pl.when((core_ref[0] == core) == near)
            def _(core=core, ref=ref):
                for row in range(n_row):
                    ref[row, :width] = blocks[core * n_row + row]
                    ref[row, width:] = sums


def first_back(core, w_mixed, qkv_grad, x_all, x_mean, inverse, gain, width, n_row):
    tokens = x_all.shape[1]
    return pl.pallas_call(
        first_kernel,
        in_specs=[SMEM] + [VMEM] * 6,
        out_specs=[VMEM] * 3,
        out_shape=(
            jax.ShapeDtypeStruct((n_row, width + 16, tokens), LOW),
            jax.ShapeDtypeStruct((n_row, width + 16, tokens), LOW),
            jax.ShapeDtypeStruct((D, 2), jnp.float32),
        ),
        compiler_params=BIG,
        name="first_back",
    )(core, w_mixed, qkv_grad, x_all, x_mean, inverse, gain)


def adam_update(weights, moment_one, second, gradient, step_rate, weight_decay):
    moment_one = BETA_ONE * moment_one + (1.0 - BETA_ONE) * gradient
    second = BETA_TWO * second + (1.0 - BETA_TWO) * gradient * gradient
    direction = (
        moment_one / (1.0 - BETA_ONE**STEP) / (jnp.sqrt(second / (1.0 - BETA_TWO**STEP)) + ADAM_EPS)
    )
    return (weights - step_rate * (direction + weight_decay * weights), moment_one, second)


def shards(
    inputs,
    cotangent,
    qkv_master,
    out_master,
    up_master,
    down_master,
    qkv_first,
    out_first,
    up_first,
    down_first,
    qkv_second,
    out_second,
    up_second,
    down_second,
    norm_gains,
    gain_first,
    gain_second,
    biases,
    bias_first,
    bias_second,
):
    tokens, width = inputs.shape
    n_row = lax.axis_size("row")
    n_col = lax.axis_size("col")
    n_dp = lax.axis_size("dp")
    row = lax.axis_index("row")
    core = lax.axis_index("col")
    group = n_row * n_col
    heads = width // HEAD
    hidden_width = FF // group
    own = core * n_row + row
    place = jnp.stack([core, lax.axis_index("dp"), own]).astype(jnp.int32)
    chunk = -(-tokens // (group * 16)) * 16
    padded = chunk * group
    shard_rows = qkv_master.shape[0]

    index = jnp.arange(D)
    feature = (
        ((index // width) % n_row) * n_col + index // (width * n_row)
    ) * width + index % width
    index = (feature % n_dp) * (D // n_dp) + feature // n_dp
    order = (lax.broadcasted_iota(jnp.int32, (D, D), 1) == index[:, None]).astype(LOW)
    order = lax.optimization_barrier(order)

    def mixed(vector):
        return vector.reshape(n_row, n_col, width).transpose(1, 0, 2).reshape(D)

    def dealt(vector):
        return vector.reshape(D // n_dp, n_dp).T.reshape(D)

    def returned(rows):
        return exchange_rows(rows.reshape(n_row, shard_rows, -1))

    def long(array):
        return jnp.pad(array, ((0, 0), (0, padded - tokens)))

    flat = lambda array: array.transpose(1, 2, 0)
    tall = lambda array: array.transpose(2, 0, 1)
    first_rows = prepare(place, qkv_master, flat(out_master), n_row)
    first_rows = exchange_rows(first_rows).reshape(D // n_dp, -1)
    x_own = long(inputs.T)
    x_after = x_own + zero_of(first_rows).astype(LOW)
    x_rows = lax.all_gather(x_after, "row", axis=0, tiled=True)
    first_parts = gather_parts(first_rows, "dp")
    rest = prepare(x_rows, up_master, flat(down_master), n_row)
    rest = exchange_rows(rest).reshape(D // n_dp, -1)
    rest_parts = gather_parts(rest, "dp")
    x_all = both_cores(x_rows)
    cot_own = long(cotangent.T) + zero_of(rest).astype(LOW)
    cot_all = lax.all_gather(cot_own, ("row", "col"), axis=0)

    gain_one = mixed(norm_gains[0])
    gain_two = dealt(norm_gains[1])
    shift_one = mixed(biases[:D])
    shift_two = dealt(biases[D : 2 * D])
    query_bias = lax.dynamic_slice_in_dim(biases, 2 * D + own * width, width).reshape(heads, HEAD)
    value_bias = lax.dynamic_slice_in_dim(biases, 3 * D + own * width, width).reshape(heads, HEAD)
    out_bias = dealt(biases[4 * D : 5 * D])
    feature_start = (row * n_col + core) * width
    down_bias = lax.dynamic_slice_in_dim(biases, 5 * D + feature_start, width)
    up_bias = lax.dynamic_slice_in_dim(biases, 6 * D + own * hidden_width, hidden_width)
    qkv_bias = jnp.stack([query_bias, jnp.zeros_like(query_bias), value_bias], axis=1).reshape(
        3 * width, 1
    )

    x_full = x_all.astype(jnp.float32)
    x_mean = jnp.sum(x_full, axis=0, keepdims=True) / D
    center = x_full - x_mean
    inverse_one = lax.rsqrt(jnp.sum(center * center, axis=0, keepdims=True) / D + NORM_EPS)
    za = (center * inverse_one * gain_one[:, None] + shift_one[:, None]).astype(LOW)
    za = dot(order, za, 0, 0, LOW)

    w_first, qkv, attended, theirs, mine = attend(place, rest, za, qkv_bias, first_parts, width)
    pair = (mine.astype(jnp.float32) + swap_cores(theirs).astype(jnp.float32)).astype(LOW)
    branch = sum_over_rows(pair)
    cot_tokens, qkv_mixed, x_mine = beside(
        place, pair, order, cot_all, w_first, x_all, n_row, chunk
    )
    cot_mine = take(cot_tokens, own, chunk).astype(jnp.float32)

    middle = x_mine + branch + out_bias[None, :]
    center = middle - jnp.sum(middle, axis=1, keepdims=True) / D
    inverse_two = lax.rsqrt(jnp.sum(center * center, axis=1, keepdims=True) / D + NORM_EPS)
    normed_two = center * inverse_two
    zb = (normed_two * gain_two + shift_two).astype(LOW)
    zb_rows = lax.all_gather(zb, "row", axis=0, tiled=True)
    w_up, active_grad, down_mixed = before(place, zb_rows, order, cot_tokens, rest_parts)
    zb = both_cores(zb_rows)

    core_of = core.reshape(1).astype(jnp.int32)
    active, hidden_grad, theirs, mine, up_sums = mlp(
        core_of, zb, w_up, up_bias[None, :], active_grad
    )
    pair = (mine.astype(jnp.float32) + swap_cores(theirs).astype(jnp.float32)).astype(LOW)
    two_grad = sum_over_rows(pair)

    middle_mixed = dot(order, middle.astype(LOW), 1, 1, LOW)
    rest_grad, theirs, mine = behind(
        place, pair, zb, hidden_grad, cot_tokens, active, down_mixed, middle_mixed, n_dp
    )
    result = mine.astype(jnp.float32) + swap_cores(theirs).astype(jnp.float32)

    scaled = two_grad * gain_two
    first_sum = jnp.sum(scaled, axis=1, keepdims=True) / D
    second_sum = jnp.sum(scaled * normed_two, axis=1, keepdims=True) / D
    middle_grad = cot_mine + inverse_two * (scaled - first_sum - normed_two * second_sum)
    middle_grad = middle_grad.astype(LOW)
    branch_rows = lax.all_gather(middle_grad, "row", axis=0, tiled=True)
    later = zero_of(branch_rows)
    result = sum_over_rows(result + later) + down_bias[:, None]
    result = result.astype(LOW)[:, :tokens].T
    branch_all = both_cores(branch_rows)

    qkv_grad, bias_sums, first_grad = attend_back(
        branch_all, w_first, qkv, za, attended, n_dp
    )
    theirs, mine, one_sums = first_back(
        core_of, qkv_mixed, qkv_grad, x_all, x_mean, inverse_one, gain_one[:, None], width, n_row
    )
    pair = (mine.astype(jnp.float32) + swap_cores(theirs).astype(jnp.float32)).astype(LOW)
    one_grad = sum_over_rows(pair.reshape(-1, padded))
    first_rows = sum_blocks(first_grad, "dp", 0.0)
    rest_rows = sum_blocks(rest_grad, "dp", later)

    own_gain = lax.dynamic_slice_in_dim(norm_gains[0], feature_start, width)[:, None]
    own_normed = (x_own.astype(jnp.float32) - x_mean) * inverse_one
    own_order = lax.dynamic_slice_in_dim(order, own * width, width, axis=0)
    own_middle = dot(own_order, branch_all, 1, 1)
    input_grad = own_middle + inverse_one * (
        one_grad[:width] * own_gain
        - one_grad[width : width + 1] / D
        - own_normed * (one_grad[width + 1 : width + 2] / D)
    )
    input_grad = input_grad.astype(LOW)[:, :tokens].T

    later = zero_of(pair)
    bias_sums = bias_sums.reshape(heads, 3, HEAD)
    all_rows = jnp.stack(
        [
            one_sums[:, 0],
            one_sums[:, 1],
            jnp.sum(two_grad * normed_two, axis=0),
            jnp.sum(two_grad, axis=0),
            jnp.sum(middle_grad, axis=0, dtype=jnp.float32),
            jnp.sum(cot_mine, axis=0),
        ]
    )
    own_row = jnp.concatenate(
        [bias_sums[:, 0].reshape(width), bias_sums[:, 2].reshape(width), up_sums[0]]
    )
    own_row = jnp.pad(own_row, (0, D - own_row.shape[0]))
    own_rows = jnp.where(jnp.arange(group)[:, None] == own, own_row[None, :], 0.0)
    total = all_sum(jnp.concatenate([jnp.pad(all_rows, ((0, 2), (0, 0))), own_rows]) + later)
    one_rows = total[:2].reshape(2, n_col, n_row, width).transpose(0, 2, 1, 3).reshape(2, D)
    two_rows = total[2:6].reshape(4, n_dp, D // n_dp).transpose(0, 2, 1).reshape(4, D)
    own_rows = total[8:]
    gain_total = jnp.stack([one_rows[0], two_rows[0]])
    bias_total = jnp.concatenate(
        [
            one_rows[1],
            two_rows[1],
            own_rows[:, :width].reshape(D),
            own_rows[:, width : 2 * width].reshape(D),
            two_rows[2],
            two_rows[3],
            own_rows[:, 2 * width : 2 * width + hidden_width].reshape(FF),
        ]
    )

    rest_new = adam(
        pair,
        returned(rest_rows),
        (0.03, 0.02),
        up_master,
        up_first,
        up_second,
        flat(down_master),
        flat(down_first),
        flat(down_second),
    )
    first_new = adam(
        pair,
        returned(first_rows),
        (0.03, 0.12),
        qkv_master,
        qkv_first,
        qkv_second,
        flat(out_master),
        flat(out_first),
        flat(out_second),
    )
    g_new = adam_update(norm_gains, gain_first, gain_second, gain_total, 0.5, 0.0)
    b_new = adam_update(biases, bias_first, bias_second, bias_total, 0.5, 0.0)
    return (
        result,
        input_grad,
        *first_new[:3],
        *(tall(array) for array in first_new[3:]),
        *rest_new[:3],
        *(tall(array) for array in rest_new[3:]),
        *g_new,
        *b_new,
    )


def solution(mesh):
    token_spec = P("dp", ("row", "col"))
    wide = P("row", "dp", "col")
    tall = P("col", "row", "dp")
    return jax.shard_map(
        shards,
        mesh=mesh,
        in_specs=(token_spec,) * 2 + (wide, tall, wide, tall) * 3 + (P(),) * 6,
        out_specs=(token_spec,) * 2
        + (wide,) * 3
        + (tall,) * 3
        + (wide,) * 3
        + (tall,) * 3
        + (P(),) * 6,
        check_vma=False,
    )
```

profile of v0, /device:TPU:0, one launch (start us, length us, event | category | flops | bytes accessed | tf_op | source)
XLA Modules:
  0.0 348.9 jit_solution(456003958032461869)
XLA Ops:
  8.6 2.6 prepare.2
  11.2 6.4 %all-to-all-start = ((bf16[4,72,576]{2,1,0:T(8,128)(2,1)}), bf16[4,72,576]{2,1,0:T(8,128)(2,1)S(1)}, u32[]{:S(2)}, u32[]{:S(2)}) async-start(bf16[4,72,576]{2,1,0:T(8,128)(2,1)} %prepare.2), calls=%async_computation | async-start | bytes 737280 | tf_op jit(solution)/shard_map/all_to_all | solution.py:65
  19.7 9.1 %all-to-all-done = bf16[4,72,576]{2,1,0:T(8,128)(2,1)S(1)} async-done(((bf16[4,72,576]{2,1,0:T(8,128)(2,1)}), bf16[4,72,576]{2,1,0:T(8,128)(2,1)S(1)}, u32[]{:S(2)}, u32[]{:S(2)}) %all-to-all-start) | async-done | bytes 331808 | tf_op jit(solution)/shard_map/all_to_all | solution.py:65
  30.1 19.2 %all_gather.51.after_ref = bf16[576,768]{1,0:T(8,128)(2,1)} all-gather(bf16[144,768]{1,0:T(8,128)(2,1)S(1)} %pad_add_fusion.1), channel_id=1, replica_groups=mesh['dp'=4,'row'=4,'col'=2] {'row'}, dimensions={0}, use_global_device_ids=true | all-gather | bytes 1105920 | tf_op jit(solution)/shard_map/all_gather | solution.py:537
  49.3 3.5 %prepare.3 = bf16[4,72,1076]{2,1,0:T(8,128)(2,1)} custom-call(bf16[576,768]{1,0:T(8,128)(2,1)} %all_gather.51.after_ref, f32[72,1,2152]{2,1,0:T(1,128)} %refs_0_.3, f32[72,1,2152]{2,1,0:T(1,128)} %bitcast.75), custom_call_target="tpu_custom_call" | custom-call | tf_op jit(solution)/shard_map/prepare/pallas_call | solution.py:111
  52.8 4.2 %all-to-all-start.1 = ((bf16[4,72,1076]{2,1,0:T(8,128)(2,1)}), bf16[4,72,1076]{2,1,0:T(8,128)(2,1)}, u32[]{:S(2)}, u32[]{:S(2)}) async-start(bf16[4,72,1076]{2,1,0:T(8,128)(2,1)} %prepare.3), calls=%async_computation.1 | async-start | bytes 1327104 | tf_op jit(solution)/shard_map/all_to_all | solution.py:65
  74.5 3.0 all-gather
  78.6 4.1 %fusion.3.za_ref = bf16[1152,768]{1,0:T(8,128)(2,1)} fusion(bf16[1152,1152]{1,0:T(8,128)(2,1)S(1)} %fusion.order_ref, bf16[1152,768]{1,0:T(8,128)(2,1)S(1)} %bitcast.57, f32[1152]{0:T(1024)S(1)} %copy-done.33, f32[1152]{0:T(1024)S(1)} %copy-done.34, f32[768]{0:T(1024)S(1)} %add_rsqrt_fusion, f32[768]{0:T(1024)S(1)} %broadcast_multiply_fusion), kind=kOutput, calls=%fused_computation.9 | convolution fusion | flops 2043740160 | bytes 6208512 | tf_op jit(solution)/shard_map/dot_general | solution.py:24
  82.7 9.1 %attend.1 = (bf16[1152,576]{1,0:T(8,128)(2,1)}, bf16[2,3,72,768]{3,2,1,0:T(8,128)(2,1)}, bf16[768,144]{1,0:T(8,128)(2,1)}, bf16[384,1152]{1,0:T(8,128)(2,1)}, bf16[384,1152]{1,0:T(8,128)(2,1)}) custom-call(s32[3]{0:T(128)} %pad_add_fusion.2.after_ref.place_ref, bf16[288,1076]{1,0:T(8,128)(2,1)} %bitcast.8.after_ref.refs_0_, bf16[1152,768]{1,0:T(8,128)(2,1)} %fusion.3.za_ref, ...), custom_call_target="tpu_custom_call" | custom-call | tf_op jit(solution)/shard_map/attend/pallas_call | solution.py:202
  96.9 11.9 %reduce-scatter.7.cloned.1.call-start = ((), (), s32[]{:S(2)}) async-start(), calls=%async_computation.11 | async-start | bytes 1105920 | tf_op jit(solution)/shard_map/reduce_scatter | solution.py:74
  114.7 9.2 %beside.1 = (bf16[768,1152]{1,0:T(8,128)(2,1)}, bf16[1152,432]{1,0:T(8,128)(2,1)}, f32[96,1152]{1,0:T(8,128)}) custom-call(s32[3]{0:T(128)} %pad_add_fusion.2.after_ref.place_ref, bf16[384,1152]{1,0:T(8,128)(2,1)} %add_convert_fusion.5.after_ref, bf16[1152,1152]{1,0:T(8,128)(2,1)} %copy-done, bf16[8,144,768]{2,1,0:T(8,128)(2,1)} %bitcast.77, ...), custom_call_target="tpu_custom_call" | custom-call | tf_op jit(solution)/shard_map/beside/pallas_call | solution.py:238
  125.5 20.5 %all_gather.58.after_ref = bf16[384,1152]{1,0:T(8,128)(2,1)S(1)} all-gather(bf16[96,1152]{1,0:T(8,128)(2,1)S(1)} %add_convert_fusion.7), channel_id=1, replica_groups=mesh['dp'=4,'row'=4,'col'=2] {'row'}, dimensions={0}, use_global_device_ids=true | all-gather | bytes 1105920 | tf_op jit(solution)/shard_map/all_gather | solution.py:580
  153.6 8.8 %before.1 = (bf16[1152,538]{1,0:T(8,128)(2,1)}, f32[768,538]{1,0:T(8,128)}, bf16[1152,538]{1,0:T(8,128)(2,1)}) custom-call(s32[3]{0:T(128)} %pad_add_fusion.2.after_ref.place_ref, bf16[384,1152]{1,0:T(8,128)(2,1)} %copy-done.5, bf16[1152,1152]{1,0:T(8,128)(2,1)} %copy-done, bf16[768,1152]{1,0:T(8,128)(2,1)} %get-tuple-element.61.cot_ref, ...), custom_call_target="tpu_custom_call" | custom-call | tf_op jit(solution)/shard_map/before/pallas_call | solution.py:265
  162.4 9.4 %mlp.1 = (bf16[768,538]{1,0:T(8,128)(2,1)}, bf16[768,538]{1,0:T(8,128)(2,1)}, bf16[384,1152]{1,0:T(8,128)(2,1)}, bf16[384,1152]{1,0:T(8,128)(2,1)}, f32[1,538]{1,0:T(1,128)}) custom-call(s32[1]{0:T(128)} %bitcast.core_ref, bf16[768,1152]{1,0:T(8,128)(2,1)} %bitcast.62, bf16[1152,538]{1,0:T(8,128)(2,1)} %get-tuple-element.62.up_ref, ...), custom_call_target="tpu_custom_call" | custom-call | tf_op jit(solution)/shard_map/mlp/pallas_call | solution.py:351
  180.8 10.4 %behind.1 = (bf16[4,288,1076]{2,1,0:T(8,128)(2,1)}, bf16[576,768]{1,0:T(8,128)(2,1)}, bf16[576,768]{1,0:T(8,128)(2,1)}) custom-call(s32[3]{0:T(128)} %pad_add_fusion.2.after_ref.place_ref, bf16[384,1152]{1,0:T(8,128)(2,1)} %add_convert_fusion.4.after_ref, bf16[768,1152]{1,0:T(8,128)(2,1)} %bitcast.63, bf16[768,538]{1,0:T(8,128)(2,1)} %get-tuple-element.66.hid_ref, ...), custom_call_target="tpu_custom_call" | custom-call | tf_op jit(solution)/shard_map/behind/pallas_call | solution.py:297
  191.4 4.6 %all-to-all-start.4 = ((bf16[4,288,1076]{2,1,0:T(8,128)(2,1)}), bf16[4,288,1076]{2,1,0:T(8,128)(2,1)}, u32[]{:S(2)}, u32[]{:S(2)}) async-start(bf16[4,288,1076]{2,1,0:T(8,128)(2,1)} %get-tuple-element.84), calls=%async_computation.8 | async-start | bytes 5308416 | tf_op jit(solution)/shard_map/all_to_all | solution.py:69
  196.0 4.8 %reduce-scatter.7.cloned.1.call-done = bf16[96,1152]{1,0:T(8,128)(2,1)} async-done(((bf16[384,1152]{1,0:T(8,128)(2,1)}), bf16[96,1152]{1,0:T(8,128)(2,1)}) %reduce-scatter.7.cloned.1.call-update) | async-done | bytes 221200 | tf_op jit(solution)/shard_map/reduce_scatter | solution.py:74
  203.4 18.8 %all_gather.63 = bf16[384,1152]{1,0:T(8,128)(2,1)S(1)} all-gather(bf16[96,1152]{1,0:T(8,128)(2,1)S(1)} %get-tuple-element.113), channel_id=1, replica_groups=mesh['dp'=4,'row'=4,'col'=2] {'row'}, dimensions={0}, use_global_device_ids=true | all-gather | bytes 1105920 | tf_op jit(solution)/shard_map/all_gather | solution.py:602
  225.8 2.8 all-gather.5
  230.0 10.7 %attend_back.1 = (bf16[432,768]{1,0:T(8,128)(2,1)}, f32[432,1]{1,0:T(8,128)}, bf16[4,288,576]{2,1,0:T(8,128)(2,1)}) custom-call(bf16[768,1152]{1,0:T(8,128)(2,1)} %bitcast.60, bf16[1152,576]{1,0:T(8,128)(2,1)} %get-tuple-element.59.w_ref, bf16[2,3,72,768]{3,2,1,0:T(8,128)(2,1)} %get-tuple-element.72.qkv_ref, bf16[1152,768]{1,0:T(8,128)(2,1)} %fusion.3.za_ref, ...), custom_call_target="tpu_custom_call" | custom-call | tf_op jit(solution)/shard_map/attend_back/pallas_call | solution.py:407
  240.7 5.6 %first_back.1 = (bf16[4,160,768]{2,1,0:T(8,128)(2,1)}, bf16[4,160,768]{2,1,0:T(8,128)(2,1)}, f32[1152,2]{1,0:T(8,128)}) custom-call(s32[1]{0:T(128)} %bitcast.core_ref, bf16[1152,432]{1,0:T(8,128)(2,1)} %get-tuple-element.71.w_ref, bf16[432,768]{1,0:T(8,128)(2,1)} %get-tuple-element.74.grad_ref, bf16[1152,768]{1,0:T(8,128)(2,1)} %bitcast.59, ...), custom_call_target="tpu_custom_call" | custom-call | tf_op jit(solution)/shard_map/first_back/pallas_call | solution.py:451
  249.3 4.3 %all-to-all-start.2 = ((bf16[4,288,576]{2,1,0:T(8,128)(2,1)}), bf16[4,288,576]{2,1,0:T(8,128)(2,1)}, u32[]{:S(2)}, u32[]{:S(2)}) async-start(bf16[4,288,576]{2,1,0:T(8,128)(2,1)} %get-tuple-element.77), calls=%async_computation.6 | async-start | bytes 2949120 | tf_op jit(solution)/shard_map/all_to_all | solution.py:69
  259.4 3.4 add_reduce_fusion
  262.8 10.0 %all-to-all-done.2 = bf16[4,288,576]{2,1,0:T(8,128)(2,1)} async-done(((bf16[4,288,576]{2,1,0:T(8,128)(2,1)}), bf16[4,288,576]{2,1,0:T(8,128)(2,1)}, u32[]{:S(2)}, u32[]{:S(2)}) %all-to-all-start.2) | async-done | bytes 1327136 | tf_op jit(solution)/shard_map/all_to_all | solution.py:69
  272.8 3.5 all-to-all-start.5
  280.0 8.8 %collective-permute-done.11 = f32[16,1152]{1,0:T(8,128)} collective-permute-done((f32[16,1152]{1,0:T(8,128)}, f32[16,1152]{1,0:T(8,128)}, u32[]{:S(2)}, u32[]{:S(2)}) %collective-permute-start.11) | collective-permute-done | bytes 73760 | tf_op jit(solution)/shard_map/ppermute | solution.py:86
  289.8 4.6 %collective-permute-start.12 = (f32[16,1152]{1,0:T(8,128)S(1)}, f32[16,1152]{1,0:T(8,128)S(1)}, u32[]{:S(2)}, u32[]{:S(2)}) collective-permute-start(f32[16,1152]{1,0:T(8,128)S(1)} %add.322), channel_id=1, source_target_pairs={{0,4},{2,6},{4,0},{6,2},{1,5},{3,7},{5,1},{7,3},{8,12},{10,14},{12... | collective-permute-start | bytes 221192 | tf_op jit(solution)/shard_map/ppermute | solution.py:86
  303.5 2.9 fusion.21
  308.9 3.5 all-to-all-start.3
  312.4 7.2 %adam.3 = (f32[72,1,2152]{2,1,0:T(1,128)}, f32[72,1,2152]{2,1,0:T(1,128)}, f32[72,1,2152]{2,1,0:T(1,128)}, f32[72,1,2152]{2,1,0:T(1,128)}, f32[72,1,2152]{2,1,0:T(1,128)}, /*index=5*/f32[72,1,2152]{2,1,0:T(1,128)}) custom-call(bf16[4,160,768]{2,1,0:T(8,128)(2,1)} %copy-done.3, bf16[4,72,1076]{2,1,0:T(8,128)(2,1)} %copy-done.6, f32[72,1,2152]{2,1,0:T(1,128)} %refs_0_.3, ...), custom_call_target="tpu_custom_call" | custom-call | tf_op jit(solution)/shard_map/adam/pallas_call | solution.py:138
  323.2 7.9 %all-to-all-done.3.blocks_ref = bf16[4,72,576]{2,1,0:T(8,128)(2,1)S(1)} async-done(((bf16[4,72,576]{2,1,0:T(8,128)(2,1)}), bf16[4,72,576]{2,1,0:T(8,128)(2,1)S(1)}, u32[]{:S(2)}, u32[]{:S(2)}) %all-to-all-start.3) | async-done | bytes 331808 | tf_op jit(solution)/shard_map/all_to_all | solution.py:65
  331.8 4.8 %adam.2 = (f32[72,1,1728]{2,1,0:T(1,128)}, f32[72,1,1728]{2,1,0:T(1,128)}, f32[72,1,1728]{2,1,0:T(1,128)}, f32[72,1,576]{2,1,0:T(1,128)}, f32[72,1,576]{2,1,0:T(1,128)}, /*index=5*/f32[72,1,576]{2,1,0:T(1,128)}) custom-call(bf16[4,160,768]{2,1,0:T(8,128)(2,1)} %copy-done.3, bf16[4,72,576]{2,1,0:T(8,128)(2,1)} %copy-done.11, f32[72,1,1728]{2,1,0:T(1,128)} %refs_0_.2, ...), custom_call_target="tpu_custom_call" | custom-call | tf_op jit(solution)/shard_map/adam/pallas_call | solution.py:138
  (248 shorter events, 90.0 us)
Async XLA Ops:
  11.2 18.8 %copy-start.13 = (bf16[729,144]{0,1:T(8,128)(2,1)S(1)}, bf16[729,144]{0,1:T(8,128)(2,1)}, u32[]{:S(2)}) copy-start(bf16[729,144]{0,1:T(8,128)(2,1)} %param.20) | copy-start | bytes 629860
  11.2 17.6 %all-to-all-start = ((bf16[4,72,576]{2,1,0:T(8,128)(2,1)}), bf16[4,72,576]{2,1,0:T(8,128)(2,1)S(1)}, u32[]{:S(2)}, u32[]{:S(2)}) async-start(bf16[4,72,576]{2,1,0:T(8,128)(2,1)} %prepare.2), calls=%async_computation | async-start | bytes 737280 | tf_op jit(solution)/shard_map/all_to_all | solution.py:65
  18.2 60.4 %copy-start = (bf16[1152,1152]{1,0:T(8,128)(2,1)}, bf16[1152,1152]{1,0:T(8,128)(2,1)S(1)}, u32[]{:S(2)}) copy-start(bf16[1152,1152]{1,0:T(8,128)(2,1)S(1)} %fusion.order_ref) | copy-start | bytes 7962628
  28.8 20.5 %copy-start.10 = (bf16[4,72,576]{2,1,0:T(8,128)(2,1)}, bf16[4,72,576]{2,1,0:T(8,128)(2,1)S(1)}, u32[]{:S(2)}) copy-start(bf16[4,72,576]{2,1,0:T(8,128)(2,1)S(1)} %all-to-all-done) | copy-start | bytes 995332
  49.3 17.7 %copy-start.4 = (bf16[576,768]{1,0:T(8,128)(2,1)S(1)}, bf16[576,768]{1,0:T(8,128)(2,1)}, u32[]{:S(2)}) copy-start(bf16[576,768]{1,0:T(8,128)(2,1)} %all_gather.51.after_ref) | copy-start | bytes 2654212
  52.8 18.1 %all-to-all-start.1 = ((bf16[4,72,1076]{2,1,0:T(8,128)(2,1)}), bf16[4,72,1076]{2,1,0:T(8,128)(2,1)}, u32[]{:S(2)}, u32[]{:S(2)}) async-start(bf16[4,72,1076]{2,1,0:T(8,128)(2,1)} %prepare.3), calls=%async_computation.1 | async-start | bytes 1327104 | tf_op jit(solution)/shard_map/all_to_all | solution.py:65
  57.0 57.7 %all-gather.9.cloned.1.call-start = ((), (), s32[]{:S(2)}) async-start(), calls=%async_computation.14 | async-start | bytes 1990656 | tf_op jit(solution)/shard_map/all_gather | solution.py:544
  63.5 19.2 %collective-permute-start = (bf16[288,576]{1,0:T(8,128)(2,1)}, bf16[288,576]{1,0:T(8,128)(2,1)}, u32[]{:S(2)}, u32[]{:S(2)}) collective-permute-start(bf16[288,576]{1,0:T(8,128)(2,1)} %bitcast.79), channel_id=1, source_target_pairs={{0,8},{8,0},{16,24},{24,16},{1,9},{9,1},{17,25},{25,17},{2,10},{10... | collective-permute-start | bytes 995336 | tf_op jit(solution)/shard_map/ppermute | solution.py:55
  65.0 17.7 %collective-permute-start.1 = (bf16[288,576]{1,0:T(8,128)(2,1)}, bf16[288,576]{1,0:T(8,128)(2,1)}, u32[]{:S(2)}, u32[]{:S(2)}) collective-permute-start(bf16[288,576]{1,0:T(8,128)(2,1)} %bitcast.80), channel_id=1, source_target_pairs={{0,16},{8,24},{16,0},{24,8},{1,17},{9,25},{17,1},{25,9},{2,18},{10... | collective-permute-start | bytes 995336 | tf_op jit(solution)/shard_map/ppermute | solution.py:55
  66.5 16.2 %collective-permute-start.2 = (bf16[288,576]{1,0:T(8,128)(2,1)}, bf16[288,576]{1,0:T(8,128)(2,1)}, u32[]{:S(2)}, u32[]{:S(2)}) collective-permute-start(bf16[288,576]{1,0:T(8,128)(2,1)} %bitcast.81), channel_id=1, source_target_pairs={{0,24},{8,16},{16,8},{24,0},{1,25},{9,17},{17,9},{25,1},{2,26},{10... | collective-permute-start | bytes 995336 | tf_op jit(solution)/shard_map/ppermute | solution.py:55
  74.4 49.5 %reduce-scatter.5.cloned.1.call-start = ((), (), s32[]{:S(2)}) async-start(), calls=%async_computation.10 | async-start | bytes 1105920 | tf_op jit(solution)/shard_map/reduce_scatter | solution.py:74
  91.8 17.3 %copy-start.28 = (f32[1152]{0:T(1024)S(1)}, f32[1152]{0:T(1024)}, u32[]{:S(2)}) copy-start(f32[1152]{0:T(1024)} %get-tuple-element.125) | copy-start | bytes 13828
  91.8 2.7 collective-permute-start.3
  96.9 103.9 %reduce-scatter.7.cloned.1.call-start = ((), (), s32[]{:S(2)}) async-start(), calls=%async_computation.11 | async-start | bytes 1105920 | tf_op jit(solution)/shard_map/reduce_scatter | solution.py:74
  111.2 41.1 %collective-permute-start.4 = (bf16[288,1076]{1,0:T(8,128)(2,1)}, bf16[288,1076]{1,0:T(8,128)(2,1)S(1)}, u32[]{:S(2)}, u32[]{:S(2)}) collective-permute-start(bf16[288,1076]{1,0:T(8,128)(2,1)} %bitcast.8.after_ref.refs_0_), channel_id=1, source_target_pairs={{0,8},{8,0},{16,24},{24,16},{1,9},{9,1},{17,25},{25,17},{2,10},{10... | collective-permute-start | bytes 1859336 | tf_op jit(solution)/shard_map/ppermute | solution.py:55
  112.7 39.6 %collective-permute-start.5 = (bf16[288,1076]{1,0:T(8,128)(2,1)}, bf16[288,1076]{1,0:T(8,128)(2,1)S(1)}, u32[]{:S(2)}, u32[]{:S(2)}) collective-permute-start(bf16[288,1076]{1,0:T(8,128)(2,1)} %bitcast.8.after_ref.refs_0_), channel_id=1, source_target_pairs={{0,16},{8,24},{16,0},{24,8},{1,17},{9,25},{17,1},{25,9},{2,18},{10... | collective-permute-start | bytes 1859336 | tf_op jit(solution)/shard_map/ppermute | solution.py:55
  114.2 38.1 %collective-permute-start.6 = (bf16[288,1076]{1,0:T(8,128)(2,1)}, bf16[288,1076]{1,0:T(8,128)(2,1)S(1)}, u32[]{:S(2)}, u32[]{:S(2)}) collective-permute-start(bf16[288,1076]{1,0:T(8,128)(2,1)} %bitcast.8.after_ref.refs_0_), channel_id=1, source_target_pairs={{0,24},{8,16},{16,8},{24,0},{1,25},{9,17},{17,9},{25,1},{2,26},{10... | collective-permute-start | bytes 1859336 | tf_op jit(solution)/shard_map/ppermute | solution.py:55
  171.8 2.7 collective-permute-start.7
  191.2 55.1 %collective-permute-start.8 = (bf16[576,768]{1,0:T(8,128)(2,1)}, bf16[576,768]{1,0:T(8,128)(2,1)}, u32[]{:S(2)}, u32[]{:S(2)}) collective-permute-start(bf16[576,768]{1,0:T(8,128)(2,1)} %get-tuple-element.70), channel_id=1, source_target_pairs={{0,1},{1,0},{2,3},{3,2},{4,5},{5,4},{6,7},{7,6},{8,9},{9,8},{10,11... | collective-permute-start | bytes 2654216 | tf_op jit(solution)/shard_map/ppermute | solution.py:39
  191.4 57.9 %all-to-all-start.4 = ((bf16[4,288,1076]{2,1,0:T(8,128)(2,1)}), bf16[4,288,1076]{2,1,0:T(8,128)(2,1)}, u32[]{:S(2)}, u32[]{:S(2)}) async-start(bf16[4,288,1076]{2,1,0:T(8,128)(2,1)} %get-tuple-element.84), calls=%async_computation.8 | async-start | bytes 5308416 | tf_op jit(solution)/shard_map/all_to_all | solution.py:69
  196.0 140.6 %reduce-scatter.9.cloned.1.call-start = ((), (), s32[]{:S(2)}) async-start(), calls=%async_computation.12 | async-start | bytes 1105920 | tf_op jit(solution)/shard_map/reduce_scatter | solution.py:74
  246.3 8.1 %collective-permute-start.9 = (bf16[4,160,768]{2,1,0:T(8,128)(2,1)}, bf16[4,160,768]{2,1,0:T(8,128)(2,1)}, u32[]{:S(2)}, u32[]{:S(2)}) collective-permute-start(bf16[4,160,768]{2,1,0:T(8,128)(2,1)} %get-tuple-element.76), channel_id=1, source_target_pairs={{0,1},{1,0},{2,3},{3,2},{4,5},{5,4},{6,7},{7,6},{8,9},{9,8},{10,11... | collective-permute-start | bytes 2949128 | tf_op jit(solution)/shard_map/ppermute | solution.py:39
  249.3 23.5 %all-to-all-start.2 = ((bf16[4,288,576]{2,1,0:T(8,128)(2,1)}), bf16[4,288,576]{2,1,0:T(8,128)(2,1)}, u32[]{:S(2)}, u32[]{:S(2)}) async-start(bf16[4,288,576]{2,1,0:T(8,128)(2,1)} %get-tuple-element.77), calls=%async_computation.6 | async-start | bytes 2949120 | tf_op jit(solution)/shard_map/all_to_all | solution.py:69
  258.9 40.1 %copy-start.14 = (bf16[729,144]{0,1:T(8,128)(2,1)S(1)}, bf16[729,144]{0,1:T(8,128)(2,1)}, u32[]{:S(2)}) copy-start(bf16[729,144]{0,1:T(8,128)(2,1)} %param.20) | copy-start | bytes 629860
  259.0 17.5 %collective-permute-start.10 = (f32[16,1152]{1,0:T(8,128)}, f32[16,1152]{1,0:T(8,128)}, u32[]{:S(2)}, u32[]{:S(2)}) collective-permute-start(f32[16,1152]{1,0:T(8,128)} %fusion.27), channel_id=1, source_target_pairs={{0,1},{1,0},{2,3},{3,2},{4,5},{5,4},{6,7},{7,6},{8,9},{9,8},{10,11... | collective-permute-start | bytes 221192 | tf_op jit(solution)/shard_map/ppermute | solution.py:86
  272.8 36.1 %all-to-all-start.5 = ((bf16[4,72,1076]{2,1,0:T(8,128)(2,1)}), bf16[4,72,1076]{2,1,0:T(8,128)(2,1)S(1)}, u32[]{:S(2)}, u32[]{:S(2)}) async-start(bf16[4,72,1076]{2,1,0:T(8,128)(2,1)} %bitcast.37), calls=%async_computation.9 | async-start | bytes 1327104 | tf_op jit(solution)/shard_map/all_to_all | solution.py:65
  276.3 62.0 %reduce-scatter.11.cloned.1.call-start = ((), (), s32[]{:S(2)}) async-start(), calls=%async_computation.13 | async-start | bytes 1228800 | tf_op jit(solution)/shard_map/reduce_scatter | solution.py:74
  278.0 10.8 %collective-permute-start.11 = (f32[16,1152]{1,0:T(8,128)}, f32[16,1152]{1,0:T(8,128)}, u32[]{:S(2)}, u32[]{:S(2)}) collective-permute-start(f32[16,1152]{1,0:T(8,128)} %fusion.68), channel_id=1, source_target_pairs={{0,2},{2,0},{4,6},{6,4},{1,3},{3,1},{5,7},{7,5},{8,10},{10,8},{12,... | collective-permute-start | bytes 221192 | tf_op jit(solution)/shard_map/ppermute | solution.py:86
  289.8 7.7 %collective-permute-start.12 = (f32[16,1152]{1,0:T(8,128)S(1)}, f32[16,1152]{1,0:T(8,128)S(1)}, u32[]{:S(2)}, u32[]{:S(2)}) collective-permute-start(f32[16,1152]{1,0:T(8,128)S(1)} %add.322), channel_id=1, source_target_pairs={{0,4},{2,6},{4,0},{6,2},{1,5},{3,7},{5,1},{7,3},{8,12},{10,14},{12... | collective-permute-start | bytes 221192 | tf_op jit(solution)/shard_map/ppermute | solution.py:86
  297.6 4.4 %collective-permute-start.13 = (f32[16,1152]{1,0:T(8,128)S(1)}, f32[16,1152]{1,0:T(8,128)S(1)}, u32[]{:S(2)}, u32[]{:S(2)}) collective-permute-start(f32[16,1152]{1,0:T(8,128)S(1)} %add.323), channel_id=1, source_target_pairs={{0,8},{8,0},{16,24},{24,16},{1,9},{9,1},{17,25},{25,17},{2,10},{10... | collective-permute-start | bytes 221192 | tf_op jit(solution)/shard_map/ppermute | solution.py:86
  302.0 17.7 %collective-permute-start.14 = (f32[16,1152]{1,0:T(8,128)S(1)}, f32[16,1152]{1,0:T(8,128)S(1)}, u32[]{:S(2)}, u32[]{:S(2)}) collective-permute-start(f32[16,1152]{1,0:T(8,128)S(1)} %add.324), channel_id=1, source_target_pairs={{0,16},{8,24},{16,0},{24,8},{1,17},{9,25},{17,1},{25,9},{2,18},{10... | collective-permute-start | bytes 221192 | tf_op jit(solution)/shard_map/ppermute | solution.py:86
  308.9 22.2 %all-to-all-start.3 = ((bf16[4,72,576]{2,1,0:T(8,128)(2,1)}), bf16[4,72,576]{2,1,0:T(8,128)(2,1)S(1)}, u32[]{:S(2)}, u32[]{:S(2)}) async-start(bf16[4,72,576]{2,1,0:T(8,128)(2,1)} %bitcast.31), calls=%async_computation.7 | async-start | bytes 737280 | tf_op jit(solution)/shard_map/all_to_all | solution.py:65
  (32 other events, 166.5 us)
Sparse Core Ops, SparseCore 0:
  74.6 27.1 all-gather.8
Sparse Core Ops, SparseCore 1:
  97.0 25.4 reduce-scatter.4
  177.1 23.6 reduce-scatter.6
  248.8 24.4 reduce-scatter.8
  306.5 29.3 reduce-scatter.10
where the time goes:
time: 353 us; the launch traced here: 349 us
  Pallas kernels  81.3 us (23%)
  blocking collectives  74 us (21%)
  starting transfers between devices  56.3 us (16%)
  waiting for transfers between devices  50.3 us (14%)
  other arithmetic  35.4 us (10%)
  local copies, waits for them, and re-layouts  23.7 us (7%)
  between operations  19.4 us (5%)
  matrix products  8.54 us (2%)
    all_gather x1, blocking collectives, shards(): zb_rows = lax.all_gather(zb, 'row', axis=0, tiled=True)  20.5 us
    all_gather x1, blocking collectives, shards(): x_rows = lax.all_gather(x_after, 'row', axis=0, tiled=True)  19.2 us
    all_gather x1, blocking collectives, shards(): branch_rows = lax.all_gather(middle_grad, 'row', axis=0, tiled=True)  18.8 us
    all_to_all x4, waiting for transfers between devices, exchange_rows(): return lax.all_to_all(blocks, 'row', 0, 0)  17.6 us
    all_to_all x4, starting transfers between devices, exchange_rows(): return lax.all_to_all(blocks, 'row', 0, 0)  17.6 us
    all_gather x6, blocking collectives, both_cores(): lax.all_gather(piece, 'col', axis=0)  15.6 us
    ppermute x5, waiting for transfers between devices, all_sum(): lax.ppermute(vector, axis, [(i, i ^ step) for i in range(size)])  12.8 us
    reduce_scatter x4, starting transfers between devices, sum_over_rows(): lax.psum_scatter(half.astype(LOW), 'row', scatter_dimension=0, tiled=True)  12.2 us
  transfers between devices with their start and end apart: 26, of which 10 were waited for; matrix products, arithmetic and copies ran while one was open for 17% of the time, Pallas kernels for 16%

commit v1 on v0

--- a/solution.py
+++ b/solution.py
@@ -37,13 +37,6 @@
 def swap_cores(array):
     n_col = lax.axis_size("col")
     return lax.ppermute(array, "col", [(i, (i + 1) % n_col) for i in range(n_col)])
-
-
-def both_cores(rows):
-    pieces = [
-        lax.all_gather(piece, "col", axis=0) for piece in jnp.split(rows, 2, axis=0)
-    ]
-    return jnp.concatenate(pieces, axis=1).reshape(-1, rows.shape[1])
 
 
 def gather_parts(block, axis):
@@ -94,8 +87,10 @@
 BIG = pltpu.CompilerParams(vmem_limit_bytes=56 * 1024 * 1024)
 
 
-def prepare_kernel(parts, after_ref, wide_ref, tall_ref, out_ref):
+def prepare_kernel(parts, after_ref, wide_ref, tall_ref, rows_ref, out_ref, long_ref):
     del after_ref
+    long_ref[...] = jnp.zeros(long_ref.shape, long_ref.dtype)
+    long_ref[:, : rows_ref.shape[1]] = rows_ref[...]
     arrays = [ref[:, 0, :].astype(LOW) for ref in (wide_ref, tall_ref)]
     for part in range(parts):
         pieces = []
@@ -105,17 +100,50 @@
         out_ref[part] = jnp.concatenate(pieces, axis=1)
 
 
-def prepare(after, wide, tall, parts):
-    rows = wide.shape[0]
+def prepare(after, wide, tall, parts, rows, padded):
     size = (wide.shape[2] + tall.shape[2]) // parts
     return pl.pallas_call(
         partial(prepare_kernel, parts),
-        in_specs=[ANY, VMEM, VMEM],
-        out_specs=VMEM,
-        out_shape=jax.ShapeDtypeStruct((parts, rows, size), LOW),
+        in_specs=[ANY, VMEM, VMEM, VMEM],
+        out_specs=[VMEM] * 2,
+        out_shape=(
+            jax.ShapeDtypeStruct((parts, wide.shape[0], size), LOW),
+            jax.ShapeDtypeStruct((rows.shape[0], padded), LOW),
+        ),
         compiler_params=BIG,
         name="prepare",
-    )(after, wide, tall)
+    )(after, wide, tall, rows)
+
+
+def norm_kernel(place_ref, mine_ref, theirs_ref, gain_ref, shift_ref, turn_ref, x_ref, za_ref, mean_ref, inv_ref):
+    core = place_ref[0]
+    x_ref[core] = mine_ref[...]
+    x_ref[1 - core] = theirs_ref[...]
+    x_full = x_ref[...].reshape(za_ref.shape).astype(jnp.float32)
+    mean = jnp.sum(x_full, axis=0, keepdims=True) / D
+    center = x_full - mean
+    inverse = lax.rsqrt(jnp.sum(center * center, axis=0, keepdims=True) / D + NORM_EPS)
+    mean_ref[...] = mean
+    inv_ref[...] = inverse
+    z_one = (center * inverse * gain_ref[...] + shift_ref[...]).astype(LOW)
+    za_ref[...] = dot(turn_ref[...], z_one, 1, 0).astype(LOW)
+
+
+def norm_first(place, mine, theirs, gain, shift, turn):
+    rows, tokens = mine.shape
+    return pl.pallas_call(
+        norm_kernel,
+        in_specs=[SMEM] + [VMEM] * 5,
+        out_specs=[VMEM] * 4,
+        out_shape=(
+            jax.ShapeDtypeStruct((2, rows, tokens), LOW),
+            jax.ShapeDtypeStruct((2 * rows, tokens), LOW),
+            jax.ShapeDtypeStruct((1, tokens), jnp.float32),
+            jax.ShapeDtypeStruct((1, tokens), jnp.float32),
+        ),
+        compiler_params=BIG,
+        name="norm_first",
+    )(place, mine, theirs, gain, shift, turn)
 
 
 def adam_kernel(rates, after_ref, blocks_ref, *refs):
@@ -379,7 +407,8 @@
     )(core, zb, w_up, up_bias, active_grad)
 
 
-def back_kernel(bg_ref, w_ref, qkv_ref, za_ref, att_ref, grad_ref, sum_ref, wg_ref):
+def back_kernel(after_ref, bg_ref, w_ref, qkv_ref, za_ref, att_ref, grad_ref, sum_ref, wg_ref):
+    del after_ref
     heads = qkv_ref.shape[0]
     attended_grad = dot(bg_ref[...], w_ref[:, heads * 3 * HEAD :], 1, 0).T
     scale = HEAD ** (-0.5)
@@ -402,11 +431,11 @@
     wg_ref[...] = jnp.concatenate([qkv_part, out_part], axis=1).reshape(wg_ref.shape)
 
 
-def attend_back(branch_all, w_first, qkv, za, attended, n_dp):
+def attend_back(after, branch_all, w_first, qkv, za, attended, n_dp):
     tokens, width = attended.shape
     return pl.pallas_call(
         back_kernel,
-        in_specs=[VMEM] * 5,
+        in_specs=[ANY] + [VMEM] * 5,
         out_specs=[VMEM] * 3,
         out_shape=(
             jax.ShapeDtypeStruct((3 * width, tokens), LOW),
@@ -415,7 +444,7 @@
         ),
         compiler_params=BIG,
         name="attend_back",
-    )(branch_all, w_first, qkv, za, attended)
+    )(after, branch_all, w_first, qkv, za, attended)
 
 
 def first_kernel(core_ref, w_ref, grad_ref, x_ref, mean_ref, inv_ref, gain_ref, theirs_ref, mine_ref, sum_ref):
@@ -514,7 +543,8 @@
     ) * width + index % width
     index = (feature % n_dp) * (D // n_dp) + feature // n_dp
     order = (lax.broadcasted_iota(jnp.int32, (D, D), 1) == index[:, None]).astype(LOW)
-    order = lax.optimization_barrier(order)
+    turn = (lax.broadcasted_iota(jnp.int32, (D, D), 0) == index[None, :]).astype(LOW)
+    order, turn = lax.optimization_barrier((order, turn))
 
     def mixed(vector):
         return vector.reshape(n_row, n_col, width).transpose(1, 0, 2).reshape(D)
@@ -525,22 +555,17 @@
     def returned(rows):
         return exchange_rows(rows.reshape(n_row, shard_rows, -1))
 
-    def long(array):
-        return jnp.pad(array, ((0, 0), (0, padded - tokens)))
-
     flat = lambda array: array.transpose(1, 2, 0)
     tall = lambda array: array.transpose(2, 0, 1)
-    first_rows = prepare(place, qkv_master, flat(out_master), n_row)
+    first_rows, x_own = prepare(place, qkv_master, flat(out_master), n_row, inputs.T, padded)
     first_rows = exchange_rows(first_rows).reshape(D // n_dp, -1)
-    x_own = long(inputs.T)
-    x_after = x_own + zero_of(first_rows).astype(LOW)
-    x_rows = lax.all_gather(x_after, "row", axis=0, tiled=True)
+    x_rows = lax.all_gather(x_own, "row", axis=0, tiled=True)
     first_parts = gather_parts(first_rows, "dp")
-    rest = prepare(x_rows, up_master, flat(down_master), n_row)
+    rest, cot_own = prepare(
+        x_rows, up_master, flat(down_master), n_row, cotangent.T, padded
+    )
     rest = exchange_rows(rest).reshape(D // n_dp, -1)
     rest_parts = gather_parts(rest, "dp")
-    x_all = both_cores(x_rows)
-    cot_own = long(cotangent.T) + zero_of(rest).astype(LOW)
     cot_all = lax.all_gather(cot_own, ("row", "col"), axis=0)
 
     gain_one = mixed(norm_gains[0])
@@ -557,12 +582,10 @@
         3 * width, 1
     )
 
-    x_full = x_all.astype(jnp.float32)
-    x_mean = jnp.sum(x_full, axis=0, keepdims=True) / D
-    center = x_full - x_mean
-    inverse_one = lax.rsqrt(jnp.sum(center * center, axis=0, keepdims=True) / D + NORM_EPS)
-    za = (center * inverse_one * gain_one[:, None] + shift_one[:, None]).astype(LOW)
-    za = dot(order, za, 0, 0, LOW)
+    x_all, za, x_mean, inverse_one = norm_first(
+        place, x_rows, swap_cores(x_rows), gain_one[:, None], shift_one[:, None], turn
+    )
+    x_all = x_all.reshape(D, padded)
 
     w_first, qkv, attended, theirs, mine = attend(place, rest, za, qkv_bias, first_parts, width)
     pair = (mine.astype(jnp.float32) + swap_cores(theirs).astype(jnp.float32)).astype(LOW)
@@ -577,9 +600,8 @@
     inverse_two = lax.rsqrt(jnp.sum(center * center, axis=1, keepdims=True) / D + NORM_EPS)
     normed_two = center * inverse_two
     zb = (normed_two * gain_two + shift_two).astype(LOW)
-    zb_rows = lax.all_gather(zb, "row", axis=0, tiled=True)
-    w_up, active_grad, down_mixed = before(place, zb_rows, order, cot_tokens, rest_parts)
-    zb = both_cores(zb_rows)
+    w_up, active_grad, down_mixed = before(place, zb, order, cot_tokens, rest_parts)
+    zb = lax.all_gather(zb, ("col", "row"), axis=0, tiled=True)
 
     core_of = core.reshape(1).astype(jnp.int32)
     active, hidden_grad, theirs, mine, up_sums = mlp(
@@ -599,14 +621,15 @@
     second_sum = jnp.sum(scaled * normed_two, axis=1, keepdims=True) / D
     middle_grad = cot_mine + inverse_two * (scaled - first_sum - normed_two * second_sum)
     middle_grad = middle_grad.astype(LOW)
-    branch_rows = lax.all_gather(middle_grad, "row", axis=0, tiled=True)
-    later = zero_of(branch_rows)
+    branch_all = lax.all_gather(middle_grad, ("col", "row"), axis=0, tiled=True)
+    later = zero_of(middle_grad)
     result = sum_over_rows(result + later) + down_bias[:, None]
     result = result.astype(LOW)[:, :tokens].T
-    branch_all = both_cores(branch_rows)
+    rest_rows = sum_blocks(rest_grad, "dp", later)
+    rest_rows = rest_rows + zero_of(branch_all).astype(LOW)
 
     qkv_grad, bias_sums, first_grad = attend_back(
-        branch_all, w_first, qkv, za, attended, n_dp
+        rest_rows, branch_all, w_first, qkv, za, attended, n_dp
     )
     theirs, mine, one_sums = first_back(
         core_of, qkv_mixed, qkv_grad, x_all, x_mean, inverse_one, gain_one[:, None], width, n_row
@@ -614,7 +637,6 @@
     pair = (mine.astype(jnp.float32) + swap_cores(theirs).astype(jnp.float32)).astype(LOW)
     one_grad = sum_over_rows(pair.reshape(-1, padded))
     first_rows = sum_blocks(first_grad, "dp", 0.0)
-    rest_rows = sum_blocks(rest_grad, "dp", later)
 
     own_gain = lax.dynamic_slice_in_dim(norm_gains[0], feature_start, width)[:, None]
     own_normed = (x_own.astype(jnp.float32) - x_mean) * inverse_one

time: 353 us -> 394 us (1.12)
  waiting for transfers between devices: 50.3 us -> 146 us
  blocking collectives: 74 us -> 25.8 us
  starting transfers between devices: 56.3 us -> 38.8 us
  local copies, waits for them, and re-layouts: 23.7 us -> 31.8 us
  Pallas kernels: 81.3 us -> 88.3 us
  matrix products: 8.54 us -> 3.69 us
    all_gather x9 -> x1, blocking collectives: 74 us -> 25.8 us  [shards(): x_rows = lax.all_gather(x_own, 'row', axis=0, tiled=True)]
    reduce_scatter x4, waiting for transfers between devices: 4.79 us -> 37.9 us  [sum_over_rows(): lax.psum_scatter(half.astype(LOW), 'row', scatter_dimension=0, tiled=True)]
    ppermute x6, waiting for transfers between devices: 0.02 us -> 26.6 us  [gather_parts(): lax.ppermute(block, axis, [(i, i ^ step) for i in range(size)])]
    all_to_all x4, waiting for transfers between devices: 17.6 us -> 38.6 us  [exchange_rows(): return lax.all_to_all(blocks, 'row', 0, 0)]
    all_to_all x2, waiting for transfers between devices: 10 us -> 28.3 us  [sum_blocks(): blocks = lax.all_to_all(blocks, axis, 0, 0)]
    reduce_scatter x4, starting transfers between devices: 12.2 us -> 0.77 us  [sum_over_rows(): lax.psum_scatter(half.astype(LOW), 'row', scatter_dimension=0, tiled=True)]
    pallas_call x3 -> x4, Pallas kernels: 16.8 us -> 24.3 us  [the longest x1 10.7 us: attend_back(): pl.pallas_call(back_kernel, in_specs=[ANY] + [VMEM] * 5, out_specs=[VMEM]...]
    ppermute x5, starting transfers between devices: 10 us -> 3.89 us  [all_sum(): lax.ppermute(vector, axis, [(i, i ^ step) for i in range(size)])]
  transfers between devices with their start and end apart: 26 -> 29, of which waited for: 10 -> 12; matrix products, arithmetic and copies ran while one was open for 17% -> 14% of each run, Pallas kernels for 16% -> 20%
where the time goes in v1:
time: 394 us; the launch traced here: 389 us
  waiting for transfers between devices  146 us (37%)
  Pallas kernels  88.3 us (22%)
  starting transfers between devices  38.8 us (10%)
  other arithmetic  36.7 us (9%)
  local copies, waits for them, and re-layouts  31.8 us (8%)
  blocking collectives  25.8 us (7%)
  between operations  18.4 us (5%)
    all_to_all x4, waiting for transfers between devices, exchange_rows(): return lax.all_to_all(blocks, 'row', 0, 0)  38.6 us
    reduce_scatter x4, waiting for transfers between devices, sum_over_rows(): lax.psum_scatter(half.astype(LOW), 'row', scatter_dimension=0, tiled=True)  37.9 us
    all_to_all x2, waiting for transfers between devices, sum_blocks(): blocks = lax.all_to_all(blocks, axis, 0, 0)  28.3 us
    ppermute x6, waiting for transfers between devices, gather_parts(): lax.ppermute(block, axis, [(i, i ^ step) for i in range(size)])  26.6 us
    all_gather x1, blocking collectives, shards(): x_rows = lax.all_gather(x_own, 'row', axis=0, tiled=True)  25.8 us
    all_to_all x4, starting transfers between devices, exchange_rows(): return lax.all_to_all(blocks, 'row', 0, 0)  17.3 us
    pallas_call x2, Pallas kernels, adam(): pl.pallas_call(partial(adam_kernel, rates), in_specs=[ANY] + [VMEM] * (1...  11.9 us
    pallas_call x1, Pallas kernels, attend_back(): pl.pallas_call(back_kernel, in_specs=[ANY] + [VMEM] * 5, out_specs=[VMEM]...  10.7 us
  transfers between devices with their start and end apart: 29, of which 12 were waited for; matrix products, arithmetic and copies ran while one was open for 14% of the time, Pallas kernels for 20%

profile of v1, /device:TPU:0, one launch (start us, length us, event | category | flops | bytes accessed | tf_op | source)
XLA Modules:
  0.0 389.0 jit_solution(3136116336197603121)
XLA Ops:
  8.6 2.7 prepare.2
  11.4 6.3 %all-to-all-start.1 = ((bf16[4,72,576]{2,1,0:T(8,128)(2,1)}), bf16[4,72,576]{2,1,0:T(8,128)(2,1)S(1)}, u32[]{:S(2)}, u32[]{:S(2)}) async-start(bf16[4,72,576]{2,1,0:T(8,128)(2,1)} %get-tuple-element.71), calls=%async_computation.1 | async-start | bytes 737280 | tf_op jit(solution)/shard_map/all_to_all | solution.py:58
  17.7 25.8 %all_gather.15.after_ref.mine_ref = bf16[576,768]{1,0:T(8,128)(2,1)S(1)} all-gather(bf16[144,768]{1,0:T(8,128)(2,1)} %get-tuple-element.67), channel_id=1, replica_groups=mesh['dp'=4,'row'=4,'col'=2] {'row'}, dimensions={0}, use_global_device_ids=true | all-gather | bytes 1105920 | tf_op jit(solution)/shard_map/all_gather | solution.py:562
  44.4 3.6 prepare.3
  48.1 3.9 %all-to-all-start = ((bf16[4,72,1076]{2,1,0:T(8,128)(2,1)}), bf16[4,72,1076]{2,1,0:T(8,128)(2,1)S(1)}, u32[]{:S(2)}, u32[]{:S(2)}) async-start(bf16[4,72,1076]{2,1,0:T(8,128)(2,1)} %get-tuple-element.68), calls=%async_computation | async-start | bytes 1327104 | tf_op jit(solution)/shard_map/all_to_all | solution.py:58
  52.3 3.1 fusion.1
  75.7 7.3 %norm_first.1 = (bf16[2,576,768]{2,1,0:T(8,128)(2,1)}, bf16[1152,768]{1,0:T(8,128)(2,1)}, f32[1,768]{1,0:T(1,128)}, f32[1,768]{1,0:T(1,128)}) custom-call(s32[3]{0:T(128)} %pad_add_fusion.after_ref.place_ref, bf16[576,768]{1,0:T(8,128)(2,1)} %copy-done.2, bf16[576,768]{1,0:T(8,128)(2,1)} %copy-done.12, f32[1152,1]{1,0:T(8,128)} %broadcast_in_dim_reshape.14.gain_ref, ...), custom_call_target="tpu_custom_call" | custom-call | tf_op jit(solution)/shard_map/norm_first/pallas_call | solution.py:134
  84.1 8.9 %attend.1 = (bf16[1152,576]{1,0:T(8,128)(2,1)}, bf16[2,3,72,768]{3,2,1,0:T(8,128)(2,1)}, bf16[768,144]{1,0:T(8,128)(2,1)}, bf16[384,1152]{1,0:T(8,128)(2,1)}, bf16[384,1152]{1,0:T(8,128)(2,1)}) custom-call(s32[3]{0:T(128)} %pad_add_fusion.after_ref.place_ref, bf16[288,1076]{1,0:T(8,128)(2,1)} %bitcast.50, bf16[1152,768]{1,0:T(8,128)(2,1)} %get-tuple-element.70.za_ref, ...), custom_call_target="tpu_custom_call" | custom-call | tf_op jit(solution)/shard_map/attend/pallas_call | solution.py:230
  93.0 2.6 collective-permute-done.4
  99.7 9.2 %beside.1 = (bf16[768,1152]{1,0:T(8,128)(2,1)}, bf16[1152,432]{1,0:T(8,128)(2,1)}, f32[96,1152]{1,0:T(8,128)}) custom-call(s32[3]{0:T(128)} %pad_add_fusion.after_ref.place_ref, bf16[384,1152]{1,0:T(8,128)(2,1)} %add_convert_fusion.3.after_ref, bf16[1152,1152]{1,0:T(8,128)(2,1)} %get-tuple-element.74.order_ref, bf16[8,144,768]{2,1,0:T(8,128)(2,1)} %bitcast.57, ...), custom_call_target="tpu_custom_call" | custom-call | tf_op jit(solution)/shard_map/beside/pallas_call | solution.py:266
  108.9 15.3 %reduce-scatter.5.cloned.1.call-done = bf16[96,1152]{1,0:T(8,128)(2,1)} async-done(((bf16[384,1152]{1,0:T(8,128)(2,1)}), bf16[96,1152]{1,0:T(8,128)(2,1)}) %reduce-scatter.5.cloned.1.call-update) | async-done | bytes 221200 | tf_op jit(solution)/shard_map/reduce_scatter | solution.py:67
  131.5 13.0 %collective-permute-done.5.refs_1_ = bf16[288,1076]{1,0:T(8,128)(2,1)S(1)} collective-permute-done((bf16[288,1076]{1,0:T(8,128)(2,1)S(1)}, bf16[288,1076]{1,0:T(8,128)(2,1)S(1)}, u32[]{:S(2)}, u32[]{:S(2)}) %collective-permute-start.5) | collective-permute-done | bytes 619808 | tf_op jit(solution)/shard_map/ppermute | solution.py:48
  144.5 13.6 %collective-permute-done.6.refs_2_ = bf16[288,1076]{1,0:T(8,128)(2,1)S(1)} collective-permute-done((bf16[288,1076]{1,0:T(8,128)(2,1)S(1)}, bf16[288,1076]{1,0:T(8,128)(2,1)S(1)}, u32[]{:S(2)}, u32[]{:S(2)}) %collective-permute-start.6) | collective-permute-done | bytes 619808 | tf_op jit(solution)/shard_map/ppermute | solution.py:48
  159.1 8.8 %before.1 = (bf16[1152,538]{1,0:T(8,128)(2,1)}, f32[768,538]{1,0:T(8,128)}, bf16[1152,538]{1,0:T(8,128)(2,1)}) custom-call(s32[3]{0:T(128)} %pad_add_fusion.after_ref.place_ref, bf16[96,1152]{1,0:T(8,128)(2,1)} %add_convert_fusion.5.after_ref, bf16[1152,1152]{1,0:T(8,128)(2,1)} %get-tuple-element.74.order_ref, bf16[768,1152]{1,0:T(8,128)(2,1)} %get-tuple-element.79.cot_ref, ...), custom_call_target="tpu_custom_call" | custom-call | tf_op jit(solution)/shard_map/before/pallas_call | solution.py:293
  168.0 9.4 %mlp.1 = (bf16[768,538]{1,0:T(8,128)(2,1)}, bf16[768,538]{1,0:T(8,128)(2,1)}, bf16[384,1152]{1,0:T(8,128)(2,1)}, bf16[384,1152]{1,0:T(8,128)(2,1)}, f32[1,538]{1,0:T(1,128)}) custom-call(s32[1]{0:T(128)} %bitcast.core_ref, bf16[768,1152]{1,0:T(8,128)(2,1)} %all-gather.5.cloned.1.call-done.zb_ref, bf16[1152,538]{1,0:T(8,128)(2,1)} %get-tuple-element.80.up_ref, ...), custom_call_target="tpu_custom_call" | custom-call | tf_op jit(solution)/shard_map/mlp/pallas_call | solution.py:379
  177.4 2.6 collective-permute-done.8
  182.4 22.6 %reduce-scatter.7.cloned.1.call-done = bf16[96,1152]{1,0:T(8,128)(2,1)} async-done(((bf16[384,1152]{1,0:T(8,128)(2,1)}), bf16[96,1152]{1,0:T(8,128)(2,1)}) %reduce-scatter.7.cloned.1.call-update) | async-done | bytes 221200 | tf_op jit(solution)/shard_map/reduce_scatter | solution.py:67
  209.9 10.1 %behind.1 = (bf16[4,288,1076]{2,1,0:T(8,128)(2,1)}, bf16[576,768]{1,0:T(8,128)(2,1)}, bf16[576,768]{1,0:T(8,128)(2,1)}) custom-call(s32[3]{0:T(128)} %pad_add_fusion.after_ref.place_ref, bf16[384,1152]{1,0:T(8,128)(2,1)} %add_convert_fusion.2.after_ref, bf16[768,1152]{1,0:T(8,128)(2,1)} %all-gather.5.cloned.1.call-done.zb_ref, ...), custom_call_target="tpu_custom_call" | custom-call | tf_op jit(solution)/shard_map/behind/pallas_call | solution.py:325
  220.0 4.7 %all-to-all-start.2 = ((bf16[4,288,1076]{2,1,0:T(8,128)(2,1)}), bf16[4,288,1076]{2,1,0:T(8,128)(2,1)}, u32[]{:S(2)}, u32[]{:S(2)}) async-start(bf16[4,288,1076]{2,1,0:T(8,128)(2,1)} %get-tuple-element.91), calls=%async_computation.5 | async-start | bytes 5308416 | tf_op jit(solution)/shard_map/all_to_all | solution.py:62
  227.0 28.3 %all-to-all-done.2 = bf16[4,288,1076]{2,1,0:T(8,128)(2,1)} async-done(((bf16[4,288,1076]{2,1,0:T(8,128)(2,1)}), bf16[4,288,1076]{2,1,0:T(8,128)(2,1)}, u32[]{:S(2)}, u32[]{:S(2)}) %all-to-all-start.2) | async-done | bytes 2479136 | tf_op jit(solution)/shard_map/all_to_all | solution.py:62
  260.4 10.7 %attend_back.1 = (bf16[432,768]{1,0:T(8,128)(2,1)}, f32[432,1]{1,0:T(8,128)}, bf16[4,288,576]{2,1,0:T(8,128)(2,1)}) custom-call(bf16[288,1076]{1,0:T(8,128)(2,1)} %convert_add_fusion.after_ref, bf16[768,1152]{1,0:T(8,128)(2,1)} %all-gather.7.cloned.1.call-done.bg_ref, bf16[1152,576]{1,0:T(8,128)(2,1)} %get-tuple-element.76.w_ref, ...), custom_call_target="tpu_custom_call" | custom-call | tf_op jit(solution)/shard_map/attend_back/pallas_call | solution.py:436
  271.1 5.6 %first_back.1 = (bf16[4,160,768]{2,1,0:T(8,128)(2,1)}, bf16[4,160,768]{2,1,0:T(8,128)(2,1)}, f32[1152,2]{1,0:T(8,128)}) custom-call(s32[1]{0:T(128)} %bitcast.core_ref, bf16[1152,432]{1,0:T(8,128)(2,1)} %get-tuple-element.90.w_ref, bf16[432,768]{1,0:T(8,128)(2,1)} %get-tuple-element.94.grad_ref, bf16[1152,768]{1,0:T(8,128)(2,1)} %bitcast.49, ...), custom_call_target="tpu_custom_call" | custom-call | tf_op jit(solution)/shard_map/first_back/pallas_call | solution.py:480
  280.2 3.5 all-to-all-start.5
  289.5 25.1 %all-to-all-done.5.blocks_ref = bf16[4,72,1076]{2,1,0:T(8,128)(2,1)S(1)} async-done(((bf16[4,72,1076]{2,1,0:T(8,128)(2,1)}), bf16[4,72,1076]{2,1,0:T(8,128)(2,1)S(1)}, u32[]{:S(2)}, u32[]{:S(2)}) %all-to-all-start.5) | async-done | bytes 619808 | tf_op jit(solution)/shard_map/all_to_all | solution.py:58
  314.6 4.3 %all-to-all-start.3 = ((bf16[4,288,576]{2,1,0:T(8,128)(2,1)}), bf16[4,288,576]{2,1,0:T(8,128)(2,1)}, u32[]{:S(2)}, u32[]{:S(2)}) async-start(bf16[4,288,576]{2,1,0:T(8,128)(2,1)} %get-tuple-element.98), calls=%async_computation.7 | async-start | bytes 2949120 | tf_op jit(solution)/shard_map/all_to_all | solution.py:62
  322.8 2.6 collective-permute-done.12
  328.6 4.4 %collective-permute-done.13 = f32[16,1152]{1,0:T(8,128)} collective-permute-done((f32[16,1152]{1,0:T(8,128)}, f32[16,1152]{1,0:T(8,128)}, u32[]{:S(2)}, u32[]{:S(2)}) %collective-permute-start.13) | collective-permute-done | bytes 73760 | tf_op jit(solution)/shard_map/ppermute | solution.py:79
  342.8 7.2 %adam.3 = (f32[72,1,2152]{2,1,0:T(1,128)}, f32[72,1,2152]{2,1,0:T(1,128)}, f32[72,1,2152]{2,1,0:T(1,128)}, f32[72,1,2152]{2,1,0:T(1,128)}, f32[72,1,2152]{2,1,0:T(1,128)}, /*index=5*/f32[72,1,2152]{2,1,0:T(1,128)}) custom-call(bf16[4,160,768]{2,1,0:T(8,128)(2,1)} %copy-done.1, bf16[4,72,1076]{2,1,0:T(8,128)(2,1)} %copy-done.5, f32[72,1,2152]{2,1,0:T(1,128)} %refs_0_.3, ...), custom_call_target="tpu_custom_call" | custom-call | tf_op jit(solution)/shard_map/adam/pallas_call | solution.py:166
  350.0 2.4 reduce_sum.98
  352.5 3.6 all-to-all-start.4
  359.6 13.5 %all-to-all-done.4.blocks_ref = bf16[4,72,576]{2,1,0:T(8,128)(2,1)S(1)} async-done(((bf16[4,72,576]{2,1,0:T(8,128)(2,1)}), bf16[4,72,576]{2,1,0:T(8,128)(2,1)S(1)}, u32[]{:S(2)}, u32[]{:S(2)}) %all-to-all-start.4) | async-done | bytes 331808 | tf_op jit(solution)/shard_map/all_to_all | solution.py:58
  373.9 4.7 %adam.2 = (f32[72,1,1728]{2,1,0:T(1,128)}, f32[72,1,1728]{2,1,0:T(1,128)}, f32[72,1,1728]{2,1,0:T(1,128)}, f32[72,1,576]{2,1,0:T(1,128)}, f32[72,1,576]{2,1,0:T(1,128)}, /*index=5*/f32[72,1,576]{2,1,0:T(1,128)}) custom-call(bf16[4,160,768]{2,1,0:T(8,128)(2,1)} %copy-done.1, bf16[4,72,576]{2,1,0:T(8,128)(2,1)} %copy-done.9, f32[72,1,1728]{2,1,0:T(1,128)} %refs_0_.2, ...), custom_call_target="tpu_custom_call" | custom-call | tf_op jit(solution)/shard_map/adam/pallas_call | solution.py:166
  (225 shorter events, 80.9 us)
Async XLA Ops:
  11.4 36.7 %all-to-all-start.1 = ((bf16[4,72,576]{2,1,0:T(8,128)(2,1)}), bf16[4,72,576]{2,1,0:T(8,128)(2,1)S(1)}, u32[]{:S(2)}, u32[]{:S(2)}) async-start(bf16[4,72,576]{2,1,0:T(8,128)(2,1)} %get-tuple-element.71), calls=%async_computation.1 | async-start | bytes 737280 | tf_op jit(solution)/shard_map/all_to_all | solution.py:58
  17.7 82.0 %all-gather.9.cloned.1.call-start = ((), (), s32[]{:S(2)}) async-start(), calls=%async_computation.16 | async-start | bytes 1990656 | tf_op jit(solution)/shard_map/all_gather | solution.py:569
  43.5 31.2 %collective-permute-start = (bf16[576,768]{1,0:T(8,128)(2,1)S(1)}, bf16[576,768]{1,0:T(8,128)(2,1)S(1)}, u32[]{:S(2)}, u32[]{:S(2)}) collective-permute-start(bf16[576,768]{1,0:T(8,128)(2,1)S(1)} %all_gather.15.after_ref.mine_ref), channel_id=1, source_target_pairs={{0,1},{1,0},{2,3},{3,2},{4,5},{5,4},{6,7},{7,6},{8,9},{9,8},{10,11... | collective-permute-start | bytes 2654216 | tf_op jit(solution)/shard_map/ppermute | solution.py:39
  48.1 34.9 %all-to-all-start = ((bf16[4,72,1076]{2,1,0:T(8,128)(2,1)}), bf16[4,72,1076]{2,1,0:T(8,128)(2,1)S(1)}, u32[]{:S(2)}, u32[]{:S(2)}) async-start(bf16[4,72,1076]{2,1,0:T(8,128)(2,1)} %get-tuple-element.68), calls=%async_computation | async-start | bytes 1327104 | tf_op jit(solution)/shard_map/all_to_all | solution.py:58
  52.0 72.2 %reduce-scatter.5.cloned.1.call-start = ((), (), s32[]{:S(2)}) async-start(), calls=%async_computation.10 | async-start | bytes 1105920 | tf_op jit(solution)/shard_map/reduce_scatter | solution.py:67
  59.4 23.6 %collective-permute-start.1 = (bf16[288,576]{1,0:T(8,128)(2,1)S(1)}, bf16[288,576]{1,0:T(8,128)(2,1)S(1)}, u32[]{:S(2)}, u32[]{:S(2)}) collective-permute-start(bf16[288,576]{1,0:T(8,128)(2,1)S(1)} %bitcast.58), channel_id=1, source_target_pairs={{0,8},{8,0},{16,24},{24,16},{1,9},{9,1},{17,25},{25,17},{2,10},{10... | collective-permute-start | bytes 995336 | tf_op jit(solution)/shard_map/ppermute | solution.py:48
  60.9 22.1 %collective-permute-start.2 = (bf16[288,576]{1,0:T(8,128)(2,1)S(1)}, bf16[288,576]{1,0:T(8,128)(2,1)S(1)}, u32[]{:S(2)}, u32[]{:S(2)}) collective-permute-start(bf16[288,576]{1,0:T(8,128)(2,1)S(1)} %bitcast.59), channel_id=1, source_target_pairs={{0,16},{8,24},{16,0},{24,8},{1,17},{9,25},{17,1},{25,9},{2,18},{10... | collective-permute-start | bytes 995336 | tf_op jit(solution)/shard_map/ppermute | solution.py:48
  62.4 20.6 %collective-permute-start.3 = (bf16[288,576]{1,0:T(8,128)(2,1)S(1)}, bf16[288,576]{1,0:T(8,128)(2,1)}, u32[]{:S(2)}, u32[]{:S(2)}) collective-permute-start(bf16[288,576]{1,0:T(8,128)(2,1)S(1)} %bitcast.60), channel_id=1, source_target_pairs={{0,24},{8,16},{16,8},{24,0},{1,25},{9,17},{17,9},{25,1},{2,26},{10... | collective-permute-start | bytes 995336 | tf_op jit(solution)/shard_map/ppermute | solution.py:48
  93.0 2.6 collective-permute-start.4
  98.0 69.9 %all-gather.5.cloned.1.call-start = ((), (), s32[]{:S(2)}) async-start(), calls=%async_computation.11 | async-start | bytes 1990656 | tf_op jit(solution)/shard_map/all_gather | solution.py:604
  108.9 17.7 %copy-start.4 = (bf16[4,72,1076]{2,1,0:T(8,128)(2,1)S(1)}, bf16[4,72,1076]{2,1,0:T(8,128)(2,1)}, u32[]{:S(2)}) copy-start(bf16[4,72,1076]{2,1,0:T(8,128)(2,1)} %copy-done.3) | copy-start | bytes 1859332
  126.5 78.5 %reduce-scatter.7.cloned.1.call-start = ((), (), s32[]{:S(2)}) async-start(), calls=%async_computation.12 | async-start | bytes 1105920 | tf_op jit(solution)/shard_map/reduce_scatter | solution.py:67
  126.6 17.9 %collective-permute-start.5 = (bf16[288,1076]{1,0:T(8,128)(2,1)S(1)}, bf16[288,1076]{1,0:T(8,128)(2,1)S(1)}, u32[]{:S(2)}, u32[]{:S(2)}) collective-permute-start(bf16[288,1076]{1,0:T(8,128)(2,1)S(1)} %bitcast.52), channel_id=1, source_target_pairs={{0,8},{8,0},{16,24},{24,16},{1,9},{9,1},{17,25},{25,17},{2,10},{10... | collective-permute-start | bytes 1859336 | tf_op jit(solution)/shard_map/ppermute | solution.py:48
  128.1 29.9 %collective-permute-start.6 = (bf16[288,1076]{1,0:T(8,128)(2,1)S(1)}, bf16[288,1076]{1,0:T(8,128)(2,1)S(1)}, u32[]{:S(2)}, u32[]{:S(2)}) collective-permute-start(bf16[288,1076]{1,0:T(8,128)(2,1)S(1)} %bitcast.53), channel_id=1, source_target_pairs={{0,16},{8,24},{16,0},{24,8},{1,17},{9,25},{17,1},{25,9},{2,18},{10... | collective-permute-start | bytes 1859336 | tf_op jit(solution)/shard_map/ppermute | solution.py:48
  129.6 28.5 %collective-permute-start.7 = (bf16[288,1076]{1,0:T(8,128)(2,1)S(1)}, bf16[288,1076]{1,0:T(8,128)(2,1)S(1)}, u32[]{:S(2)}, u32[]{:S(2)}) collective-permute-start(bf16[288,1076]{1,0:T(8,128)(2,1)S(1)} %bitcast.54), channel_id=1, source_target_pairs={{0,24},{8,16},{16,8},{24,0},{1,25},{9,17},{17,9},{25,1},{2,26},{10... | collective-permute-start | bytes 1859336 | tf_op jit(solution)/shard_map/ppermute | solution.py:48
  177.4 2.7 collective-permute-start.8
  182.4 26.0 %copy-start = (bf16[1152,1152]{1,0:T(8,128)(2,1)S(1)}, bf16[1152,1152]{1,0:T(8,128)(2,1)}, u32[]{:S(2)}) copy-start(bf16[1152,1152]{1,0:T(8,128)(2,1)} %get-tuple-element.74.order_ref) | copy-start | bytes 7962628
  182.4 75.2 %all-gather.7.cloned.1.call-start = ((), (), s32[]{:S(2)}) async-start(), calls=%async_computation.14 | async-start | bytes 1990656 | tf_op jit(solution)/shard_map/all_gather | solution.py:624
  220.0 35.2 %all-to-all-start.2 = ((bf16[4,288,1076]{2,1,0:T(8,128)(2,1)}), bf16[4,288,1076]{2,1,0:T(8,128)(2,1)}, u32[]{:S(2)}, u32[]{:S(2)}) async-start(bf16[4,288,1076]{2,1,0:T(8,128)(2,1)} %get-tuple-element.91), calls=%async_computation.5 | async-start | bytes 5308416 | tf_op jit(solution)/shard_map/all_to_all | solution.py:62
  224.7 111.0 %reduce-scatter.9.cloned.1.call-start = ((), (), s32[]{:S(2)}) async-start(), calls=%async_computation.13 | async-start | bytes 1105920 | tf_op jit(solution)/shard_map/reduce_scatter | solution.py:67
  225.0 51.7 %collective-permute-start.9 = (bf16[576,768]{1,0:T(8,128)(2,1)}, bf16[576,768]{1,0:T(8,128)(2,1)}, u32[]{:S(2)}, u32[]{:S(2)}) collective-permute-start(bf16[576,768]{1,0:T(8,128)(2,1)} %get-tuple-element.88), channel_id=1, source_target_pairs={{0,1},{1,0},{2,3},{3,2},{4,5},{5,4},{6,7},{7,6},{8,9},{9,8},{10,11... | collective-permute-start | bytes 2654216 | tf_op jit(solution)/shard_map/ppermute | solution.py:39
  276.6 7.9 %collective-permute-start.10 = (bf16[4,160,768]{2,1,0:T(8,128)(2,1)}, bf16[4,160,768]{2,1,0:T(8,128)(2,1)}, u32[]{:S(2)}, u32[]{:S(2)}) collective-permute-start(bf16[4,160,768]{2,1,0:T(8,128)(2,1)} %get-tuple-element.97), channel_id=1, source_target_pairs={{0,1},{1,0},{2,3},{3,2},{4,5},{5,4},{6,7},{7,6},{8,9},{9,8},{10,11... | collective-permute-start | bytes 2949128 | tf_op jit(solution)/shard_map/ppermute | solution.py:39
  280.2 34.4 %all-to-all-start.5 = ((bf16[4,72,1076]{2,1,0:T(8,128)(2,1)}), bf16[4,72,1076]{2,1,0:T(8,128)(2,1)S(1)}, u32[]{:S(2)}, u32[]{:S(2)}) async-start(bf16[4,72,1076]{2,1,0:T(8,128)(2,1)} %bitcast.28), calls=%async_computation.9 | async-start | bytes 1327104 | tf_op jit(solution)/shard_map/all_to_all | solution.py:58
  288.4 38.7 %copy-start.11 = (bf16[144,768]{1,0:T(8,128)(2,1)S(1)}, bf16[144,768]{1,0:T(8,128)(2,1)}, u32[]{:S(2)}) copy-start(bf16[144,768]{1,0:T(8,128)(2,1)} %get-tuple-element.67) | copy-start | bytes 663556
  289.0 30.2 %collective-permute-start.11 = (f32[16,1152]{1,0:T(8,128)}, f32[16,1152]{1,0:T(8,128)}, u32[]{:S(2)}, u32[]{:S(2)}) collective-permute-start(f32[16,1152]{1,0:T(8,128)} %fusion.21), channel_id=1, source_target_pairs={{0,1},{1,0},{2,3},{3,2},{4,5},{5,4},{6,7},{7,6},{8,9},{9,8},{10,11... | collective-permute-start | bytes 221192 | tf_op jit(solution)/shard_map/ppermute | solution.py:79
  314.6 35.4 %all-to-all-start.3 = ((bf16[4,288,576]{2,1,0:T(8,128)(2,1)}), bf16[4,288,576]{2,1,0:T(8,128)(2,1)}, u32[]{:S(2)}, u32[]{:S(2)}) async-start(bf16[4,288,576]{2,1,0:T(8,128)(2,1)} %get-tuple-element.98), calls=%async_computation.7 | async-start | bytes 2949120 | tf_op jit(solution)/shard_map/all_to_all | solution.py:62
  318.9 59.7 %reduce-scatter.11.cloned.1.call-start = ((), (), s32[]{:S(2)}) async-start(), calls=%async_computation.15 | async-start | bytes 1228800 | tf_op jit(solution)/shard_map/reduce_scatter | solution.py:67
  320.8 4.7 %collective-permute-start.12 = (f32[16,1152]{1,0:T(8,128)}, f32[16,1152]{1,0:T(8,128)}, u32[]{:S(2)}, u32[]{:S(2)}) collective-permute-start(f32[16,1152]{1,0:T(8,128)} %fusion.58), channel_id=1, source_target_pairs={{0,2},{2,0},{4,6},{6,4},{1,3},{3,1},{5,7},{7,5},{8,10},{10,8},{12,... | collective-permute-start | bytes 221192 | tf_op jit(solution)/shard_map/ppermute | solution.py:79
  327.0 6.0 %collective-permute-start.13 = (f32[16,1152]{1,0:T(8,128)}, f32[16,1152]{1,0:T(8,128)}, u32[]{:S(2)}, u32[]{:S(2)}) collective-permute-start(f32[16,1152]{1,0:T(8,128)} %add.330), channel_id=1, source_target_pairs={{0,4},{2,6},{4,0},{6,2},{1,5},{3,7},{5,1},{7,3},{8,12},{10,14},{12... | collective-permute-start | bytes 221192 | tf_op jit(solution)/shard_map/ppermute | solution.py:79
  333.9 5.2 %collective-permute-start.14 = (f32[16,1152]{1,0:T(8,128)S(1)}, f32[16,1152]{1,0:T(8,128)S(1)}, u32[]{:S(2)}, u32[]{:S(2)}) collective-permute-start(f32[16,1152]{1,0:T(8,128)S(1)} %add.331), channel_id=1, source_target_pairs={{0,8},{8,0},{16,24},{24,16},{1,9},{9,1},{17,25},{25,17},{2,10},{10... | collective-permute-start | bytes 221192 | tf_op jit(solution)/shard_map/ppermute | solution.py:79
  339.1 17.0 %collective-permute-start.15 = (f32[16,1152]{1,0:T(8,128)S(1)}, f32[16,1152]{1,0:T(8,128)S(1)}, u32[]{:S(2)}, u32[]{:S(2)}) collective-permute-start(f32[16,1152]{1,0:T(8,128)S(1)} %add.332), channel_id=1, source_target_pairs={{0,16},{8,24},{16,0},{24,8},{1,17},{9,25},{17,1},{25,9},{2,18},{10... | collective-permute-start | bytes 221192 | tf_op jit(solution)/shard_map/ppermute | solution.py:79
  352.5 20.6 %all-to-all-start.4 = ((bf16[4,72,576]{2,1,0:T(8,128)(2,1)}), bf16[4,72,576]{2,1,0:T(8,128)(2,1)S(1)}, u32[]{:S(2)}, u32[]{:S(2)}) async-start(bf16[4,72,576]{2,1,0:T(8,128)(2,1)} %bitcast.22), calls=%async_computation.8 | async-start | bytes 737280 | tf_op jit(solution)/shard_map/all_to_all | solution.py:58
  (30 other events, 139.3 us)
Sparse Core Ops, SparseCore 0:
  48.2 36.8 all-gather.8
  126.6 25.3 all-gather.4
  208.4 25.3 all-gather.6
Sparse Core Ops, SparseCore 1:
  98.1 26.0 reduce-scatter.4
  182.5 22.5 reduce-scatter.6
  279.2 33.2 reduce-scatter.8
  342.9 29.0 reduce-scatter.10

commit v2 on v1

--- a/solution.py
+++ b/solution.py
@@ -115,35 +115,76 @@
     )(after, wide, tall, rows)
 
 
-def norm_kernel(place_ref, mine_ref, theirs_ref, gain_ref, shift_ref, turn_ref, x_ref, za_ref, mean_ref, inv_ref):
-    core = place_ref[0]
-    x_ref[core] = mine_ref[...]
-    x_ref[1 - core] = theirs_ref[...]
-    x_full = x_ref[...].reshape(za_ref.shape).astype(jnp.float32)
+def norm_kernel(n_row, vectors_ref, x_ref, turn_ref, za_ref, mean_ref, inv_ref, gain_ref):
+    columns = vectors_ref[...].T
+    gain = mixed_rows(columns[:, 0:1], n_row)
+    gain_ref[...] = gain
+    x_full = x_ref[...].astype(jnp.float32)
     mean = jnp.sum(x_full, axis=0, keepdims=True) / D
     center = x_full - mean
     inverse = lax.rsqrt(jnp.sum(center * center, axis=0, keepdims=True) / D + NORM_EPS)
     mean_ref[...] = mean
     inv_ref[...] = inverse
-    z_one = (center * inverse * gain_ref[...] + shift_ref[...]).astype(LOW)
+    z_one = (center * inverse * gain + mixed_rows(columns[:, 2:3], n_row)).astype(LOW)
     za_ref[...] = dot(turn_ref[...], z_one, 1, 0).astype(LOW)
 
 
-def norm_first(place, mine, theirs, gain, shift, turn):
-    rows, tokens = mine.shape
-    return pl.pallas_call(
-        norm_kernel,
-        in_specs=[SMEM] + [VMEM] * 5,
+def mixed_rows(column, n_row):
+    n_col = 2
+    width = D // (n_row * n_col)
+    blocks = [
+        column[(row * n_col + core) * width : (row * n_col + core + 1) * width]
+        for core in range(n_col)
+        for row in range(n_row)
+    ]
+    return jnp.concatenate(blocks, axis=0)
+
+
+def norm_first(vectors, x_all, turn, n_row):
+    tokens = x_all.shape[1]
+    return pl.pallas_call(
+        partial(norm_kernel, n_row),
+        in_specs=[VMEM] * 3,
         out_specs=[VMEM] * 4,
         out_shape=(
-            jax.ShapeDtypeStruct((2, rows, tokens), LOW),
-            jax.ShapeDtypeStruct((2 * rows, tokens), LOW),
+            jax.ShapeDtypeStruct((D, tokens), LOW),
             jax.ShapeDtypeStruct((1, tokens), jnp.float32),
             jax.ShapeDtypeStruct((1, tokens), jnp.float32),
+            jax.ShapeDtypeStruct((D, 1), jnp.float32),
         ),
         compiler_params=BIG,
         name="norm_first",
-    )(place, mine, theirs, gain, shift, turn)
+    )(vectors, x_all, turn)
+
+
+def own_kernel(n_row, place_ref, after_ref, vectors_ref, x_ref, turn_ref, mine_ref, dealt_ref):
+    del after_ref
+    pick = own_tokens(place_ref, mine_ref.shape[0], x_ref.shape[1])
+    mine_ref[...] = dot(dot(pick, x_ref[...], 1, 1).astype(LOW), turn_ref[...], 1, 1)
+    rest = mixed_rows(vectors_ref[...].T, n_row).T
+    pieces = []
+    for _ in range(3):
+        piece = rest.astype(LOW)
+        rest = rest - piece.astype(jnp.float32)
+        pieces.append(piece)
+    total = dot(pieces[0], turn_ref[...], 1, 1)
+    for piece in pieces[1:]:
+        total = total + dot(piece, turn_ref[...], 1, 1)
+    dealt_ref[...] = total
+
+
+def own_rows_of(place, after, vectors, x_all, turn, n_row, chunk):
+    return pl.pallas_call(
+        partial(own_kernel, n_row),
+        in_specs=[SMEM, ANY] + [VMEM] * 3,
+        out_specs=[VMEM] * 2,
+        out_shape=(
+            jax.ShapeDtypeStruct((chunk, D), jnp.float32),
+            jax.ShapeDtypeStruct((8, D), jnp.float32),
+        ),
+        compiler_params=BIG,
+        name="own_rows",
+    )(place, after, vectors, x_all, turn)
 
 
 def adam_kernel(rates, after_ref, blocks_ref, *refs):
@@ -249,7 +290,7 @@
     return (lax.broadcasted_iota(jnp.int32, (chunk, tokens), 1) == pick).astype(LOW)
 
 
-def beside_kernel(n_row, place_ref, after_ref, order_ref, cot_ref, w_ref, x_ref, tokens_ref, mixed_ref, mine_ref):
+def beside_kernel(n_row, after_ref, order_ref, cot_ref, w_ref, tokens_ref, mixed_ref):
     del after_ref
     group, width = cot_ref.shape[:2]
     n_col = group // n_row
@@ -257,24 +298,21 @@
     cot = [cot_ref[row * n_col + core] for core in range(n_col) for row in range(n_row)]
     tokens_ref[...] = dot(jnp.concatenate(cot, axis=0), order, 0, 0).astype(LOW)
     mixed_ref[...] = dot(order, w_ref[:, : 3 * width], 1, 0).astype(LOW)
-    pick = own_tokens(place_ref, mine_ref.shape[0], x_ref.shape[1])
-    mine_ref[...] = dot(dot(pick, x_ref[...], 1, 1).astype(LOW), order, 1, 0)
-
-
-def beside(place, after, order, cot_all, w_first, x_all, n_row, chunk):
+
+
+def beside(after, order, cot_all, w_first, n_row):
     group, width, tokens = cot_all.shape
     return pl.pallas_call(
         partial(beside_kernel, n_row),
-        in_specs=[SMEM, ANY] + [VMEM] * 4,
-        out_specs=[VMEM] * 3,
+        in_specs=[ANY] + [VMEM] * 3,
+        out_specs=[VMEM] * 2,
         out_shape=(
             jax.ShapeDtypeStruct((tokens, D), LOW),
             jax.ShapeDtypeStruct((D, 3 * width), LOW),
-            jax.ShapeDtypeStruct((chunk, D), jnp.float32),
         ),
         compiler_params=BIG,
         name="beside",
-    )(place, after, order, cot_all, w_first, x_all)
+    )(after, order, cot_all, w_first)
 
 
 def before_kernel(place_ref, after_ref, order_ref, cot_ref, *refs):
@@ -546,12 +584,6 @@
     turn = (lax.broadcasted_iota(jnp.int32, (D, D), 0) == index[None, :]).astype(LOW)
     order, turn = lax.optimization_barrier((order, turn))
 
-    def mixed(vector):
-        return vector.reshape(n_row, n_col, width).transpose(1, 0, 2).reshape(D)
-
-    def dealt(vector):
-        return vector.reshape(D // n_dp, n_dp).T.reshape(D)
-
     def returned(rows):
         return exchange_rows(rows.reshape(n_row, shard_rows, -1))
 
@@ -559,22 +591,18 @@
     tall = lambda array: array.transpose(2, 0, 1)
     first_rows, x_own = prepare(place, qkv_master, flat(out_master), n_row, inputs.T, padded)
     first_rows = exchange_rows(first_rows).reshape(D // n_dp, -1)
-    x_rows = lax.all_gather(x_own, "row", axis=0, tiled=True)
+    x_all = lax.all_gather(x_own, ("col", "row"), axis=0, tiled=True)
     first_parts = gather_parts(first_rows, "dp")
     rest, cot_own = prepare(
-        x_rows, up_master, flat(down_master), n_row, cotangent.T, padded
+        x_all, up_master, flat(down_master), n_row, cotangent.T, padded
     )
     rest = exchange_rows(rest).reshape(D // n_dp, -1)
     rest_parts = gather_parts(rest, "dp")
     cot_all = lax.all_gather(cot_own, ("row", "col"), axis=0)
 
-    gain_one = mixed(norm_gains[0])
-    gain_two = dealt(norm_gains[1])
-    shift_one = mixed(biases[:D])
-    shift_two = dealt(biases[D : 2 * D])
+    vectors = jnp.concatenate([norm_gains, biases[: 6 * D].reshape(6, D)])
     query_bias = lax.dynamic_slice_in_dim(biases, 2 * D + own * width, width).reshape(heads, HEAD)
     value_bias = lax.dynamic_slice_in_dim(biases, 3 * D + own * width, width).reshape(heads, HEAD)
-    out_bias = dealt(biases[4 * D : 5 * D])
     feature_start = (row * n_col + core) * width
     down_bias = lax.dynamic_slice_in_dim(biases, 5 * D + feature_start, width)
     up_bias = lax.dynamic_slice_in_dim(biases, 6 * D + own * hidden_width, hidden_width)
@@ -582,24 +610,21 @@
         3 * width, 1
     )
 
-    x_all, za, x_mean, inverse_one = norm_first(
-        place, x_rows, swap_cores(x_rows), gain_one[:, None], shift_one[:, None], turn
-    )
-    x_all = x_all.reshape(D, padded)
+    za, x_mean, inverse_one, gain_one = norm_first(vectors, x_all, turn, n_row)
 
     w_first, qkv, attended, theirs, mine = attend(place, rest, za, qkv_bias, first_parts, width)
     pair = (mine.astype(jnp.float32) + swap_cores(theirs).astype(jnp.float32)).astype(LOW)
     branch = sum_over_rows(pair)
-    cot_tokens, qkv_mixed, x_mine = beside(
-        place, pair, order, cot_all, w_first, x_all, n_row, chunk
-    )
-    cot_mine = take(cot_tokens, own, chunk).astype(jnp.float32)
-
-    middle = x_mine + branch + out_bias[None, :]
+    x_mine, dealt = own_rows_of(place, pair, vectors, x_all, turn, n_row, chunk)
+    gain_two, shift_two, out_bias = dealt[1], dealt[3], dealt[6]
+
+    middle = x_mine + branch + (out_bias + zero_of(rest_parts[-1]))[None, :]
     center = middle - jnp.sum(middle, axis=1, keepdims=True) / D
     inverse_two = lax.rsqrt(jnp.sum(center * center, axis=1, keepdims=True) / D + NORM_EPS)
     normed_two = center * inverse_two
     zb = (normed_two * gain_two + shift_two).astype(LOW)
+    cot_tokens, qkv_mixed = beside(zb, order, cot_all, w_first, n_row)
+    cot_mine = take(cot_tokens, own, chunk).astype(jnp.float32)
     w_up, active_grad, down_mixed = before(place, zb, order, cot_tokens, rest_parts)
     zb = lax.all_gather(zb, ("col", "row"), axis=0, tiled=True)
 
@@ -614,16 +639,16 @@
     rest_grad, theirs, mine = behind(
         place, pair, zb, hidden_grad, cot_tokens, active, down_mixed, middle_mixed, n_dp
     )
-    result = mine.astype(jnp.float32) + swap_cores(theirs).astype(jnp.float32)
+    result = (mine.astype(jnp.float32) + swap_cores(theirs).astype(jnp.float32)).astype(LOW)
 
     scaled = two_grad * gain_two
     first_sum = jnp.sum(scaled, axis=1, keepdims=True) / D
     second_sum = jnp.sum(scaled * normed_two, axis=1, keepdims=True) / D
-    middle_grad = cot_mine + inverse_two * (scaled - first_sum - normed_two * second_sum)
+    middle_grad = cot_mine + zero_of(result) + inverse_two * (scaled - first_sum - normed_two * second_sum)
     middle_grad = middle_grad.astype(LOW)
     branch_all = lax.all_gather(middle_grad, ("col", "row"), axis=0, tiled=True)
     later = zero_of(middle_grad)
-    result = sum_over_rows(result + later) + down_bias[:, None]
+    result = sum_over_rows(result) + down_bias[:, None]
     result = result.astype(LOW)[:, :tokens].T
     rest_rows = sum_blocks(rest_grad, "dp", later)
     rest_rows = rest_rows + zero_of(branch_all).astype(LOW)
@@ -632,9 +657,11 @@
         rest_rows, branch_all, w_first, qkv, za, attended, n_dp
     )
     theirs, mine, one_sums = first_back(
-        core_of, qkv_mixed, qkv_grad, x_all, x_mean, inverse_one, gain_one[:, None], width, n_row
-    )
-    pair = (mine.astype(jnp.float32) + swap_cores(theirs).astype(jnp.float32)).astype(LOW)
+        core_of, qkv_mixed, qkv_grad, x_all, x_mean, inverse_one, gain_one, width, n_row
+    )
+    rest_blocks = returned(rest_rows)
+    pair = mine.astype(jnp.float32) + zero_of(rest_blocks)
+    pair = (pair + swap_cores(theirs).astype(jnp.float32)).astype(LOW)
     one_grad = sum_over_rows(pair.reshape(-1, padded))
     first_rows = sum_blocks(first_grad, "dp", 0.0)
 
@@ -685,7 +712,7 @@
 
     rest_new = adam(
         pair,
-        returned(rest_rows),
+        rest_blocks,
         (0.03, 0.02),
         up_master,
         up_first,

time: 394 us -> 400 us (1.015)
  blocking collectives: 25.8 us -> 0 us
  Pallas kernels: 88.3 us -> 106 us
  waiting for transfers between devices: 146 us -> 163 us
  local copies, waits for them, and re-layouts: 31.8 us -> 26.7 us
    reduce_scatter x4, waiting for transfers between devices: 37.9 us -> 5.49 us  [sum_over_rows(): lax.psum_scatter(half.astype(LOW), 'row', scatter_dimension=0, tiled=True)]
    all_gather x0 -> x1, waiting for transfers between devices: none -> 26.9 us  [shards(): x_all = lax.all_gather(x_own, ('col', 'row'), axis=0, tiled=True)]
    all_gather x1 -> x0, blocking collectives: 25.8 us -> none  [shards(): x_rows = lax.all_gather(x_own, 'row', axis=0, tiled=True)]
    all_gather x1, waiting for transfers between devices: 0.01 us -> 20 us  [shards(): cot_all = lax.all_gather(cot_own, ('row', 'col'), axis=0)]
    all_to_all x4, waiting for transfers between devices: 38.6 us -> 26 us  [exchange_rows(): return lax.all_to_all(blocks, 'row', 0, 0)]
    pallas_call x1, Pallas kernels: 8.94 us -> 21.3 us  [attend(): pl.pallas_call(attend_kernel, in_specs=[SMEM, ANY, VMEM, VMEM] + [VMEM] *...]
    all_gather x1, waiting for transfers between devices: 0.01 us -> 9.99 us  [shards(): zb = lax.all_gather(zb, ('col', 'row'), axis=0, tiled=True)]
    another operation x7, local copies, waits for them, and re-layouts: 0.69 us -> 7.79 us  [shards(): jnp.stack([one_sums[:, 0], one_sums[:, 1], jnp.sum(two_grad * normed_two,...]
  transfers between devices with their start and end apart: 29 -> 29, of which waited for: 12 -> 15; matrix products, arithmetic and copies ran while one was open for 14% -> 13% of each run, Pallas kernels for 20% -> 14%
where the time goes in v2:
time: 400 us; the launch traced here: 396 us
  waiting for transfers between devices  163 us (41%)
  Pallas kernels  106 us (26%)
  other arithmetic  39 us (10%)
  starting transfers between devices  38.4 us (10%)
  local copies, waits for them, and re-layouts  26.7 us (7%)
  between operations  18.9 us (5%)
    all_to_all x2, waiting for transfers between devices, sum_blocks(): blocks = lax.all_to_all(blocks, axis, 0, 0)  29.1 us
    all_gather x1, waiting for transfers between devices, shards(): x_all = lax.all_gather(x_own, ('col', 'row'), axis=0, tiled=True)  26.9 us
    all_to_all x4, waiting for transfers between devices, exchange_rows(): return lax.all_to_all(blocks, 'row', 0, 0)  26 us
    ppermute x6, waiting for transfers between devices, gather_parts(): lax.ppermute(block, axis, [(i, i ^ step) for i in range(size)])  24.3 us
    pallas_call x1, Pallas kernels, attend(): pl.pallas_call(attend_kernel, in_specs=[SMEM, ANY, VMEM, VMEM] + [VMEM] *...  21.3 us
    all_gather x1, waiting for transfers between devices, shards(): cot_all = lax.all_gather(cot_own, ('row', 'col'), axis=0)  20 us
    all_to_all x4, starting transfers between devices, exchange_rows(): return lax.all_to_all(blocks, 'row', 0, 0)  17.1 us
    ppermute x5, waiting for transfers between devices, all_sum(): lax.ppermute(vector, axis, [(i, i ^ step) for i in range(size)])  13.3 us
  transfers between devices with their start and end apart: 29, of which 15 were waited for; matrix products, arithmetic and copies ran while one was open for 13% of the time, Pallas kernels for 14%

profile of v2, /device:TPU:0, one launch (start us, length us, event | category | flops | bytes accessed | tf_op | source)
XLA Modules:
  0.0 395.6 jit_solution(11233131140840509608)
XLA Ops:
  7.8 2.7 prepare.2
  10.6 6.4 %all-to-all-start.1 = ((bf16[4,72,576]{2,1,0:T(8,128)(2,1)}), bf16[4,72,576]{2,1,0:T(8,128)(2,1)S(1)}, u32[]{:S(2)}, u32[]{:S(2)}) async-start(bf16[4,72,576]{2,1,0:T(8,128)(2,1)} %get-tuple-element.72), calls=%async_computation.1 | async-start | bytes 737280 | tf_op jit(solution)/shard_map/all_to_all | solution.py:58
  17.0 26.9 %all-gather.6.cloned.1.call-done.after_ref.x_ref = bf16[1152,768]{1,0:T(8,128)(2,1)} async-done(((bf16[144,768]{1,0:T(8,128)(2,1)}), bf16[1152,768]{1,0:T(8,128)(2,1)}) %all-gather.6.cloned.1.call-update) | async-done | bytes 1769488 | tf_op jit(solution)/shard_map/all_gather | solution.py:594
  43.8 3.5 prepare.3
  47.4 3.5 all-to-all-start
  51.0 3.1 fusion.1
  60.0 6.9 %norm_first.1 = (bf16[1152,768]{1,0:T(8,128)(2,1)}, f32[1,768]{1,0:T(1,128)}, f32[1,768]{1,0:T(1,128)}, f32[1152,1]{1,0:T(8,128)}) custom-call(f32[8,1152]{1,0:T(8,128)} %pad_maximum_fusion.vectors_ref, bf16[1152,768]{1,0:T(8,128)(2,1)} %all-gather.6.cloned.1.call-done.after_ref.x_ref, bf16[1152,1152]{1,0:T(8,128)(2,1)} %get-tuple-element.70.turn_ref), custom_call_target="tpu_custom_call" | custom-call | tf_op jit(solution)/shard_map/norm_first/pallas_call | solution.py:145
  66.9 7.9 %collective-permute-done.1.refs_2_ = bf16[288,576]{1,0:T(8,128)(2,1)S(1)} collective-permute-done((bf16[288,576]{1,0:T(8,128)(2,1)S(1)}, bf16[288,576]{1,0:T(8,128)(2,1)S(1)}, u32[]{:S(2)}, u32[]{:S(2)}) %collective-permute-start.1) | collective-permute-done | bytes 331808 | tf_op jit(solution)/shard_map/ppermute | solution.py:48
  75.9 21.3 %attend.1 = (bf16[1152,576]{1,0:T(8,128)(2,1)}, bf16[2,3,72,768]{3,2,1,0:T(8,128)(2,1)}, bf16[768,144]{1,0:T(8,128)(2,1)}, bf16[384,1152]{1,0:T(8,128)(2,1)}, bf16[384,1152]{1,0:T(8,128)(2,1)}) custom-call(s32[3]{0:T(128)} %pad_add_fusion.after_ref.place_ref, bf16[288,1076]{1,0:T(8,128)(2,1)} %bitcast.43, bf16[1152,768]{1,0:T(8,128)(2,1)} %get-tuple-element.71.za_ref, ...), custom_call_target="tpu_custom_call" | custom-call | tf_op jit(solution)/shard_map/attend/pallas_call | solution.py:271
  104.6 16.4 %collective-permute-done.4.refs_3_ = bf16[288,1076]{1,0:T(8,128)(2,1)S(1)} collective-permute-done((bf16[288,1076]{1,0:T(8,128)(2,1)S(1)}, bf16[288,1076]{1,0:T(8,128)(2,1)S(1)}, u32[]{:S(2)}, u32[]{:S(2)}) %collective-permute-start.4) | collective-permute-done | bytes 619808 | tf_op jit(solution)/shard_map/ppermute | solution.py:48
  122.1 6.6 %own_rows.1 = (f32[96,1152]{1,0:T(8,128)}, f32[8,1152]{1,0:T(8,128)}) custom-call(s32[3]{0:T(128)} %pad_add_fusion.after_ref.place_ref, bf16[384,1152]{1,0:T(8,128)(2,1)} %add_convert_fusion.3.after_ref, f32[8,1152]{1,0:T(8,128)} %pad_maximum_fusion.vectors_ref, bf16[1152,768]{1,0:T(8,128)(2,1)} %all-gather.6.cloned.1.call-done.after_ref.x_ref, ...), custom_call_target="tpu_custom_call" | custom-call | tf_op jit(solution)/shard_map/own_rows/pallas_call | solution.py:177
  134.9 20.0 %all-gather.12.cloned.1.call-done = bf16[1152,768]{1,0:T(8,128)(2,1)} async-done(((bf16[144,768]{1,0:T(8,128)(2,1)}), bf16[1152,768]{1,0:T(8,128)(2,1)}) %all-gather.12.cloned.1.call-update) | async-done | bytes 1769488 | tf_op jit(solution)/shard_map/all_gather | solution.py:601
  154.9 8.0 %beside.1 = (bf16[768,1152]{1,0:T(8,128)(2,1)}, bf16[1152,432]{1,0:T(8,128)(2,1)}) custom-call(bf16[96,1152]{1,0:T(8,128)(2,1)} %add_convert_fusion.5.after_ref, bf16[1152,1152]{1,0:T(8,128)(2,1)} %get-tuple-element.77.order_ref, bf16[8,144,768]{2,1,0:T(8,128)(2,1)} %bitcast.50, bf16[1152,576]{1,0:T(8,128)(2,1)} %get-tuple-element.79.w_ref), custom_call_target="tpu_custom_call" | custom-call | tf_op jit(solution)/shard_map/beside/pallas_call | solution.py:305
  163.9 9.0 %before.1 = (bf16[1152,538]{1,0:T(8,128)(2,1)}, f32[768,538]{1,0:T(8,128)}, bf16[1152,538]{1,0:T(8,128)(2,1)}) custom-call(s32[3]{0:T(128)} %pad_add_fusion.after_ref.place_ref, bf16[96,1152]{1,0:T(8,128)(2,1)} %add_convert_fusion.5.after_ref, bf16[1152,1152]{1,0:T(8,128)(2,1)} %get-tuple-element.77.order_ref, bf16[768,1152]{1,0:T(8,128)(2,1)} %get-tuple-element.80.cot_ref, ...), custom_call_target="tpu_custom_call" | custom-call | tf_op jit(solution)/shard_map/before/pallas_call | solution.py:331
  172.9 10.0 %all-gather.8.cloned.1.call-done.zb_ref = bf16[768,1152]{1,0:T(8,128)(2,1)} async-done(((bf16[96,1152]{1,0:T(8,128)(2,1)}), bf16[768,1152]{1,0:T(8,128)(2,1)}) %all-gather.8.cloned.1.call-update) | async-done | bytes 1769488 | tf_op jit(solution)/shard_map/all_gather | solution.py:629
  182.9 9.4 %mlp.1 = (bf16[768,538]{1,0:T(8,128)(2,1)}, bf16[768,538]{1,0:T(8,128)(2,1)}, bf16[384,1152]{1,0:T(8,128)(2,1)}, bf16[384,1152]{1,0:T(8,128)(2,1)}, f32[1,538]{1,0:T(1,128)}) custom-call(s32[1]{0:T(128)} %bitcast.core_ref, bf16[768,1152]{1,0:T(8,128)(2,1)} %all-gather.8.cloned.1.call-done.zb_ref, bf16[1152,538]{1,0:T(8,128)(2,1)} %get-tuple-element.81.up_ref, ...), custom_call_target="tpu_custom_call" | custom-call | tf_op jit(solution)/shard_map/mlp/pallas_call | solution.py:417
  199.0 10.0 %behind.1 = (bf16[4,288,1076]{2,1,0:T(8,128)(2,1)}, bf16[576,768]{1,0:T(8,128)(2,1)}, bf16[576,768]{1,0:T(8,128)(2,1)}) custom-call(s32[3]{0:T(128)} %pad_add_fusion.after_ref.place_ref, bf16[384,1152]{1,0:T(8,128)(2,1)} %add_convert_fusion.2.after_ref, bf16[768,1152]{1,0:T(8,128)(2,1)} %all-gather.8.cloned.1.call-done.zb_ref, ...), custom_call_target="tpu_custom_call" | custom-call | tf_op jit(solution)/shard_map/behind/pallas_call | solution.py:363
  216.2 5.5 %reduce-scatter.9.cloned.1.call-done = bf16[96,1152]{1,0:T(8,128)(2,1)} async-done(((bf16[384,1152]{1,0:T(8,128)(2,1)}), bf16[96,1152]{1,0:T(8,128)(2,1)}) %reduce-scatter.9.cloned.1.call-update) | async-done | bytes 221200 | tf_op jit(solution)/shard_map/reduce_scatter | solution.py:67
  226.0 5.0 %all-to-all-start.2 = ((bf16[4,288,1076]{2,1,0:T(8,128)(2,1)}), bf16[4,288,1076]{2,1,0:T(8,128)(2,1)}, u32[]{:S(2)}, u32[]{:S(2)}) async-start(bf16[4,288,1076]{2,1,0:T(8,128)(2,1)} %get-tuple-element.92), calls=%async_computation.5 | async-start | bytes 5308416 | tf_op jit(solution)/shard_map/all_to_all | solution.py:62
  232.9 29.1 %all-to-all-done.2 = bf16[4,288,1076]{2,1,0:T(8,128)(2,1)} async-done(((bf16[4,288,1076]{2,1,0:T(8,128)(2,1)}), bf16[4,288,1076]{2,1,0:T(8,128)(2,1)}, u32[]{:S(2)}, u32[]{:S(2)}) %all-to-all-start.2) | async-done | bytes 2479136 | tf_op jit(solution)/shard_map/all_to_all | solution.py:62
  267.1 10.7 %attend_back.1 = (bf16[432,768]{1,0:T(8,128)(2,1)}, f32[432,1]{1,0:T(8,128)}, bf16[4,288,576]{2,1,0:T(8,128)(2,1)}) custom-call(bf16[288,1076]{1,0:T(8,128)(2,1)} %convert_add_fusion.after_ref, bf16[768,1152]{1,0:T(8,128)(2,1)} %all-gather.10.cloned.1.call-done.bg_ref, bf16[1152,576]{1,0:T(8,128)(2,1)} %get-tuple-element.79.w_ref, ...), custom_call_target="tpu_custom_call" | custom-call | tf_op jit(solution)/shard_map/attend_back/pallas_call | solution.py:474
  277.8 5.5 %first_back.1 = (bf16[4,160,768]{2,1,0:T(8,128)(2,1)}, bf16[4,160,768]{2,1,0:T(8,128)(2,1)}, f32[1152,2]{1,0:T(8,128)}) custom-call(s32[1]{0:T(128)} %bitcast.core_ref, bf16[1152,432]{1,0:T(8,128)(2,1)} %get-tuple-element.91.w_ref, bf16[432,768]{1,0:T(8,128)(2,1)} %get-tuple-element.95.grad_ref, ...), custom_call_target="tpu_custom_call" | custom-call | tf_op jit(solution)/shard_map/first_back/pallas_call | solution.py:518
  283.3 3.6 all-to-all-start.3
  300.9 13.3 %all-to-all-done.3.blocks_ref = bf16[4,72,1076]{2,1,0:T(8,128)(2,1)S(1)} async-done(((bf16[4,72,1076]{2,1,0:T(8,128)(2,1)}), bf16[4,72,1076]{2,1,0:T(8,128)(2,1)S(1)}, u32[]{:S(2)}, u32[]{:S(2)}) %all-to-all-start.3) | async-done | bytes 619808 | tf_op jit(solution)/shard_map/all_to_all | solution.py:58
  320.6 4.3 %all-to-all-start.4 = ((bf16[4,288,576]{2,1,0:T(8,128)(2,1)}), bf16[4,288,576]{2,1,0:T(8,128)(2,1)}, u32[]{:S(2)}, u32[]{:S(2)}) async-start(bf16[4,288,576]{2,1,0:T(8,128)(2,1)} %get-tuple-element.100), calls=%async_computation.8 | async-start | bytes 2949120 | tf_op jit(solution)/shard_map/all_to_all | solution.py:62
  327.5 3.3 collective-permute-done.11
  332.4 4.9 %collective-permute-done.12 = f32[16,1152]{1,0:T(8,128)S(1)} collective-permute-done((f32[16,1152]{1,0:T(8,128)S(1)}, f32[16,1152]{1,0:T(8,128)S(1)}, u32[]{:S(2)}, u32[]{:S(2)}) %collective-permute-start.12) | collective-permute-done | bytes 73760 | tf_op jit(solution)/shard_map/ppermute | solution.py:79
  340.6 5.1 %collective-permute-done.13 = f32[16,1152]{1,0:T(8,128)S(1)} collective-permute-done((f32[16,1152]{1,0:T(8,128)S(1)}, f32[16,1152]{1,0:T(8,128)S(1)}, u32[]{:S(2)}, u32[]{:S(2)}) %collective-permute-start.13) | collective-permute-done | bytes 73760 | tf_op jit(solution)/shard_map/ppermute | solution.py:79
  349.9 7.2 %adam.3 = (f32[72,1,2152]{2,1,0:T(1,128)}, f32[72,1,2152]{2,1,0:T(1,128)}, f32[72,1,2152]{2,1,0:T(1,128)}, f32[72,1,2152]{2,1,0:T(1,128)}, f32[72,1,2152]{2,1,0:T(1,128)}, /*index=5*/f32[72,1,2152]{2,1,0:T(1,128)}) custom-call(bf16[4,160,768]{2,1,0:T(8,128)(2,1)} %copy-done.1, bf16[4,72,1076]{2,1,0:T(8,128)(2,1)} %copy-done.4, f32[72,1,2152]{2,1,0:T(1,128)} %refs_0_.3, ...), custom_call_target="tpu_custom_call" | custom-call | tf_op jit(solution)/shard_map/adam/pallas_call | solution.py:207
  359.6 3.6 all-to-all-start.5
  367.6 12.7 %all-to-all-done.5.blocks_ref = bf16[4,72,576]{2,1,0:T(8,128)(2,1)S(1)} async-done(((bf16[4,72,576]{2,1,0:T(8,128)(2,1)}), bf16[4,72,576]{2,1,0:T(8,128)(2,1)S(1)}, u32[]{:S(2)}, u32[]{:S(2)}) %all-to-all-start.5) | async-done | bytes 331808 | tf_op jit(solution)/shard_map/all_to_all | solution.py:58
  381.1 4.7 %adam.2 = (f32[72,1,1728]{2,1,0:T(1,128)}, f32[72,1,1728]{2,1,0:T(1,128)}, f32[72,1,1728]{2,1,0:T(1,128)}, f32[72,1,576]{2,1,0:T(1,128)}, f32[72,1,576]{2,1,0:T(1,128)}, /*index=5*/f32[72,1,576]{2,1,0:T(1,128)}) custom-call(bf16[4,160,768]{2,1,0:T(8,128)(2,1)} %copy-done.1, bf16[4,72,576]{2,1,0:T(8,128)(2,1)} %copy-done.6, f32[72,1,1728]{2,1,0:T(1,128)} %refs_0_.2, ...), custom_call_target="tpu_custom_call" | custom-call | tf_op jit(solution)/shard_map/adam/pallas_call | solution.py:207
  (206 shorter events, 86.7 us)
Async XLA Ops:
  7.2 36.6 %all-gather.6.cloned.1.call-start = ((), (), s32[]{:S(2)}) async-start(), calls=%async_computation.10 | async-start | bytes 1990656 | tf_op jit(solution)/shard_map/all_gather | solution.py:594
  10.6 36.8 %all-to-all-start.1 = ((bf16[4,72,576]{2,1,0:T(8,128)(2,1)}), bf16[4,72,576]{2,1,0:T(8,128)(2,1)S(1)}, u32[]{:S(2)}, u32[]{:S(2)}) async-start(bf16[4,72,576]{2,1,0:T(8,128)(2,1)} %get-tuple-element.72), calls=%async_computation.1 | async-start | bytes 737280 | tf_op jit(solution)/shard_map/all_to_all | solution.py:58
  47.4 10.6 %copy-start.5 = (bf16[4,72,576]{2,1,0:T(8,128)(2,1)}, bf16[4,72,576]{2,1,0:T(8,128)(2,1)S(1)}, u32[]{:S(2)}) copy-start(bf16[4,72,576]{2,1,0:T(8,128)(2,1)S(1)} %all-to-all-done.1) | copy-start | bytes 995332
  47.4 27.4 %all-to-all-start = ((bf16[4,72,1076]{2,1,0:T(8,128)(2,1)}), bf16[4,72,1076]{2,1,0:T(8,128)(2,1)S(1)}, u32[]{:S(2)}, u32[]{:S(2)}) async-start(bf16[4,72,1076]{2,1,0:T(8,128)(2,1)} %get-tuple-element.69), calls=%async_computation | async-start | bytes 1327104 | tf_op jit(solution)/shard_map/all_to_all | solution.py:58
  50.9 78.8 %reduce-scatter.5.cloned.1.call-start = ((), (), s32[]{:S(2)}) async-start(), calls=%async_computation.11 | async-start | bytes 1105920 | tf_op jit(solution)/shard_map/reduce_scatter | solution.py:67
  54.9 11.9 %collective-permute-start = (bf16[288,576]{1,0:T(8,128)(2,1)S(1)}, bf16[288,576]{1,0:T(8,128)(2,1)S(1)}, u32[]{:S(2)}, u32[]{:S(2)}) collective-permute-start(bf16[288,576]{1,0:T(8,128)(2,1)S(1)} %bitcast.51), channel_id=1, source_target_pairs={{0,8},{8,0},{16,24},{24,16},{1,9},{9,1},{17,25},{25,17},{2,10},{10... | collective-permute-start | bytes 995336 | tf_op jit(solution)/shard_map/ppermute | solution.py:48
  56.4 18.3 %collective-permute-start.1 = (bf16[288,576]{1,0:T(8,128)(2,1)S(1)}, bf16[288,576]{1,0:T(8,128)(2,1)S(1)}, u32[]{:S(2)}, u32[]{:S(2)}) collective-permute-start(bf16[288,576]{1,0:T(8,128)(2,1)S(1)} %bitcast.52), channel_id=1, source_target_pairs={{0,16},{8,24},{16,0},{24,8},{1,17},{9,25},{17,1},{25,9},{2,18},{10... | collective-permute-start | bytes 995336 | tf_op jit(solution)/shard_map/ppermute | solution.py:48
  58.0 16.8 %collective-permute-start.2 = (bf16[288,576]{1,0:T(8,128)(2,1)S(1)}, bf16[288,576]{1,0:T(8,128)(2,1)S(1)}, u32[]{:S(2)}, u32[]{:S(2)}) collective-permute-start(bf16[288,576]{1,0:T(8,128)(2,1)S(1)} %bitcast.53), channel_id=1, source_target_pairs={{0,24},{8,16},{16,8},{24,0},{1,25},{9,17},{17,9},{25,1},{2,26},{10... | collective-permute-start | bytes 995336 | tf_op jit(solution)/shard_map/ppermute | solution.py:48
  97.2 2.6 collective-permute-start.3
  102.2 52.7 %all-gather.12.cloned.1.call-start = ((), (), s32[]{:S(2)}) async-start(), calls=%async_computation.17 | async-start | bytes 1990656 | tf_op jit(solution)/shard_map/all_gather | solution.py:601
  103.0 79.9 %all-gather.8.cloned.1.call-start = ((), (), s32[]{:S(2)}) async-start(), calls=%async_computation.12 | async-start | bytes 1990656 | tf_op jit(solution)/shard_map/all_gather | solution.py:629
  103.0 17.9 %collective-permute-start.4 = (bf16[288,1076]{1,0:T(8,128)(2,1)S(1)}, bf16[288,1076]{1,0:T(8,128)(2,1)S(1)}, u32[]{:S(2)}, u32[]{:S(2)}) collective-permute-start(bf16[288,1076]{1,0:T(8,128)(2,1)S(1)} %bitcast.45), channel_id=1, source_target_pairs={{0,24},{8,16},{16,8},{24,0},{1,25},{9,17},{17,9},{25,1},{2,26},{10... | collective-permute-start | bytes 1859336 | tf_op jit(solution)/shard_map/ppermute | solution.py:48
  132.1 89.6 %reduce-scatter.9.cloned.1.call-start = ((), (), s32[]{:S(2)}) async-start(), calls=%async_computation.14 | async-start | bytes 1105920 | tf_op jit(solution)/shard_map/reduce_scatter | solution.py:67
  132.1 30.8 %collective-permute-start.5 = (bf16[288,1076]{1,0:T(8,128)(2,1)S(1)}, bf16[288,1076]{1,0:T(8,128)(2,1)S(1)}, u32[]{:S(2)}, u32[]{:S(2)}) collective-permute-start(bf16[288,1076]{1,0:T(8,128)(2,1)S(1)} %bitcast.46), channel_id=1, source_target_pairs={{0,8},{8,0},{16,24},{24,16},{1,9},{9,1},{17,25},{25,17},{2,10},{10... | collective-permute-start | bytes 1859336 | tf_op jit(solution)/shard_map/ppermute | solution.py:48
  133.3 29.6 %collective-permute-start.6 = (bf16[288,1076]{1,0:T(8,128)(2,1)S(1)}, bf16[288,1076]{1,0:T(8,128)(2,1)S(1)}, u32[]{:S(2)}, u32[]{:S(2)}) collective-permute-start(bf16[288,1076]{1,0:T(8,128)(2,1)S(1)} %bitcast.47), channel_id=1, source_target_pairs={{0,16},{8,24},{16,0},{24,8},{1,17},{9,25},{17,1},{25,9},{2,18},{10... | collective-permute-start | bytes 1859336 | tf_op jit(solution)/shard_map/ppermute | solution.py:48
  192.3 2.7 collective-permute-start.7
  197.4 66.9 %all-gather.10.cloned.1.call-start = ((), (), s32[]{:S(2)}) async-start(), calls=%async_computation.15 | async-start | bytes 1990656 | tf_op jit(solution)/shard_map/all_gather | solution.py:649
  209.1 2.8 collective-permute-start.8
  226.0 36.0 %all-to-all-start.2 = ((bf16[4,288,1076]{2,1,0:T(8,128)(2,1)}), bf16[4,288,1076]{2,1,0:T(8,128)(2,1)}, u32[]{:S(2)}, u32[]{:S(2)}) async-start(bf16[4,288,1076]{2,1,0:T(8,128)(2,1)} %get-tuple-element.92), calls=%async_computation.5 | async-start | bytes 5308416 | tf_op jit(solution)/shard_map/all_to_all | solution.py:62
  283.3 13.1 %copy-start.16 = (f32[432,1]{1,0:T(8,128)S(1)}, f32[432,1]{1,0:T(8,128)}, u32[]{:S(2)}) copy-start(f32[432,1]{1,0:T(8,128)} %get-tuple-element.114) | copy-start | bytes 5188
  283.3 32.1 %collective-permute-start.9 = (bf16[4,160,768]{2,1,0:T(8,128)(2,1)}, bf16[4,160,768]{2,1,0:T(8,128)(2,1)}, u32[]{:S(2)}, u32[]{:S(2)}) collective-permute-start(bf16[4,160,768]{2,1,0:T(8,128)(2,1)} %get-tuple-element.99), channel_id=1, source_target_pairs={{0,1},{1,0},{2,3},{3,2},{4,5},{5,4},{6,7},{7,6},{8,9},{9,8},{10,11... | collective-permute-start | bytes 2949128 | tf_op jit(solution)/shard_map/ppermute | solution.py:39
  283.3 30.9 %all-to-all-start.3 = ((bf16[4,72,1076]{2,1,0:T(8,128)(2,1)}), bf16[4,72,1076]{2,1,0:T(8,128)(2,1)S(1)}, u32[]{:S(2)}, u32[]{:S(2)}) async-start(bf16[4,72,1076]{2,1,0:T(8,128)(2,1)} %bitcast.15), calls=%async_computation.6 | async-start | bytes 1327104 | tf_op jit(solution)/shard_map/all_to_all | solution.py:58
  286.9 51.9 %reduce-scatter.7.cloned.1.call-start = ((), (), s32[]{:S(2)}) async-start(), calls=%async_computation.13 | async-start | bytes 1105920 | tf_op jit(solution)/shard_map/reduce_scatter | solution.py:67
  319.3 12.3 %copy-start.7 = (bf16[144,768]{1,0:T(8,128)(2,1)S(1)}, bf16[144,768]{1,0:T(8,128)(2,1)}, u32[]{:S(2)}) copy-start(bf16[144,768]{1,0:T(8,128)(2,1)} %get-tuple-element.68) | copy-start | bytes 663556
  320.0 5.2 %collective-permute-start.10 = (f32[16,1152]{1,0:T(8,128)}, f32[16,1152]{1,0:T(8,128)}, u32[]{:S(2)}, u32[]{:S(2)}) collective-permute-start(f32[16,1152]{1,0:T(8,128)} %fusion.22), channel_id=1, source_target_pairs={{0,1},{1,0},{2,3},{3,2},{4,5},{5,4},{6,7},{7,6},{8,9},{9,8},{10,11... | collective-permute-start | bytes 221192 | tf_op jit(solution)/shard_map/ppermute | solution.py:79
  320.6 36.5 %all-to-all-start.4 = ((bf16[4,288,576]{2,1,0:T(8,128)(2,1)}), bf16[4,288,576]{2,1,0:T(8,128)(2,1)}, u32[]{:S(2)}, u32[]{:S(2)}) async-start(bf16[4,288,576]{2,1,0:T(8,128)(2,1)} %get-tuple-element.100), calls=%async_computation.8 | async-start | bytes 2949120 | tf_op jit(solution)/shard_map/all_to_all | solution.py:62
  324.9 60.8 %reduce-scatter.11.cloned.1.call-start = ((), (), s32[]{:S(2)}) async-start(), calls=%async_computation.16 | async-start | bytes 1228800 | tf_op jit(solution)/shard_map/reduce_scatter | solution.py:67
  326.1 4.7 %collective-permute-start.11 = (f32[16,1152]{1,0:T(8,128)S(1)}, f32[16,1152]{1,0:T(8,128)S(1)}, u32[]{:S(2)}, u32[]{:S(2)}) collective-permute-start(f32[16,1152]{1,0:T(8,128)S(1)} %fusion.58), channel_id=1, source_target_pairs={{0,2},{2,0},{4,6},{6,4},{1,3},{3,1},{5,7},{7,5},{8,10},{10,8},{12,... | collective-permute-start | bytes 221192 | tf_op jit(solution)/shard_map/ppermute | solution.py:79
  330.9 6.5 %collective-permute-start.12 = (f32[16,1152]{1,0:T(8,128)S(1)}, f32[16,1152]{1,0:T(8,128)S(1)}, u32[]{:S(2)}, u32[]{:S(2)}) collective-permute-start(f32[16,1152]{1,0:T(8,128)S(1)} %add.347), channel_id=1, source_target_pairs={{0,4},{2,6},{4,0},{6,2},{1,5},{3,7},{5,1},{7,3},{8,12},{10,14},{12... | collective-permute-start | bytes 221192 | tf_op jit(solution)/shard_map/ppermute | solution.py:79
  337.3 8.3 %collective-permute-start.13 = (f32[16,1152]{1,0:T(8,128)S(1)}, f32[16,1152]{1,0:T(8,128)S(1)}, u32[]{:S(2)}, u32[]{:S(2)}) collective-permute-start(f32[16,1152]{1,0:T(8,128)S(1)} %add.348), channel_id=1, source_target_pairs={{0,8},{8,0},{16,24},{24,16},{1,9},{9,1},{17,25},{25,17},{2,10},{10... | collective-permute-start | bytes 221192 | tf_op jit(solution)/shard_map/ppermute | solution.py:79
  346.3 16.9 %collective-permute-start.14 = (f32[16,1152]{1,0:T(8,128)}, f32[16,1152]{1,0:T(8,128)}, u32[]{:S(2)}, u32[]{:S(2)}) collective-permute-start(f32[16,1152]{1,0:T(8,128)} %add.349), channel_id=1, source_target_pairs={{0,16},{8,24},{16,0},{24,8},{1,17},{9,25},{17,1},{25,9},{2,18},{10... | collective-permute-start | bytes 221192 | tf_op jit(solution)/shard_map/ppermute | solution.py:79
  359.6 20.8 %all-to-all-start.5 = ((bf16[4,72,576]{2,1,0:T(8,128)(2,1)}), bf16[4,72,576]{2,1,0:T(8,128)(2,1)S(1)}, u32[]{:S(2)}, u32[]{:S(2)}) async-start(bf16[4,72,576]{2,1,0:T(8,128)(2,1)} %bitcast.20), calls=%async_computation.9 | async-start | bytes 737280 | tf_op jit(solution)/shard_map/all_to_all | solution.py:58
  (25 other events, 121.9 us)
Sparse Core Ops, SparseCore 0:
  10.7 33.0 all-gather.5
  102.4 24.7 reduce-scatter.4
  129.4 25.4 all-gather.11
  156.9 25.9 all-gather.7
  197.5 24.1 reduce-scatter.8
  226.2 25.4 all-gather.9
  290.1 30.3 reduce-scatter.6
  350.0 28.8 reduce-scatter.10

commit v3 on v2

--- a/solution.py
+++ b/solution.py
@@ -61,6 +61,17 @@
 def sum_blocks(blocks, axis, later):
     blocks = lax.all_to_all(blocks, axis, 0, 0)
     return jnp.sum(blocks.astype(jnp.float32) + later, axis=0).astype(LOW)
+
+
+def sum_parts(blocks, axis):
+    size = lax.axis_size(axis)
+    if size > 4:
+        return sum_blocks(blocks, axis, 0.0)
+    total = blocks[0].astype(jnp.float32)
+    for step in range(1, size):
+        got = lax.ppermute(blocks[step], axis, [(i, i ^ step) for i in range(size)])
+        total = total + got.astype(jnp.float32)
+    return total.astype(LOW)
 
 
 def sum_over_rows(half):
@@ -115,7 +126,8 @@
     )(after, wide, tall, rows)
 
 
-def norm_kernel(n_row, vectors_ref, x_ref, turn_ref, za_ref, mean_ref, inv_ref, gain_ref):
+def norm_kernel(n_row, vectors_ref, x_ref, index_ref, *refs):
+    za_ref, mean_ref, inv_ref, gain_ref = refs[-4:]
     columns = vectors_ref[...].T
     gain = mixed_rows(columns[:, 0:1], n_row)
     gain_ref[...] = gain
@@ -126,7 +138,8 @@
     mean_ref[...] = mean
     inv_ref[...] = inverse
     z_one = (center * inverse * gain + mixed_rows(columns[:, 2:3], n_row)).astype(LOW)
-    za_ref[...] = dot(turn_ref[...], z_one, 1, 0).astype(LOW)
+    turn = (lax.broadcasted_iota(jnp.int32, (D, D), 0) == index_ref[...]).astype(LOW)
+    za_ref[...] = dot(turn, z_one, 1, 0).astype(LOW)
 
 
 def mixed_rows(column, n_row):
@@ -140,11 +153,11 @@
     return jnp.concatenate(blocks, axis=0)
 
 
-def norm_first(vectors, x_all, turn, n_row):
+def norm_first(after, vectors, x_all, index, n_row):
     tokens = x_all.shape[1]
     return pl.pallas_call(
         partial(norm_kernel, n_row),
-        in_specs=[VMEM] * 3,
+        in_specs=[VMEM] * 3 + [ANY] * len(after),
         out_specs=[VMEM] * 4,
         out_shape=(
             jax.ShapeDtypeStruct((D, tokens), LOW),
@@ -154,29 +167,29 @@
         ),
         compiler_params=BIG,
         name="norm_first",
-    )(vectors, x_all, turn)
-
-
-def own_kernel(n_row, place_ref, after_ref, vectors_ref, x_ref, turn_ref, mine_ref, dealt_ref):
-    del after_ref
+    )(vectors, x_all, index, *after)
+
+
+def own_kernel(n_row, place_ref, after_ref, later_ref, vectors_ref, x_ref, order_ref, mine_ref, dealt_ref):
+    del after_ref, later_ref
     pick = own_tokens(place_ref, mine_ref.shape[0], x_ref.shape[1])
-    mine_ref[...] = dot(dot(pick, x_ref[...], 1, 1).astype(LOW), turn_ref[...], 1, 1)
+    mine_ref[...] = dot(dot(pick, x_ref[...], 1, 1).astype(LOW), order_ref[...], 1, 0)
     rest = mixed_rows(vectors_ref[...].T, n_row).T
     pieces = []
     for _ in range(3):
         piece = rest.astype(LOW)
         rest = rest - piece.astype(jnp.float32)
         pieces.append(piece)
-    total = dot(pieces[0], turn_ref[...], 1, 1)
+    total = dot(pieces[0], order_ref[...], 1, 0)
     for piece in pieces[1:]:
-        total = total + dot(piece, turn_ref[...], 1, 1)
+        total = total + dot(piece, order_ref[...], 1, 0)
     dealt_ref[...] = total
 
 
-def own_rows_of(place, after, vectors, x_all, turn, n_row, chunk):
+def own_rows_of(place, after, later, vectors, x_all, order, n_row, chunk):
     return pl.pallas_call(
         partial(own_kernel, n_row),
-        in_specs=[SMEM, ANY] + [VMEM] * 3,
+        in_specs=[SMEM, ANY, ANY] + [VMEM] * 3,
         out_specs=[VMEM] * 2,
         out_shape=(
             jax.ShapeDtypeStruct((chunk, D), jnp.float32),
@@ -184,7 +197,7 @@
         ),
         compiler_params=BIG,
         name="own_rows",
-    )(place, after, vectors, x_all, turn)
+    )(place, after, later, vectors, x_all, order)
 
 
 def adam_kernel(rates, after_ref, blocks_ref, *refs):
@@ -224,6 +237,15 @@
 
 def part_scratch(parts):
     return pltpu.VMEM((len(parts),) + parts[0].shape, LOW)
+
+
+def store_parts(place, array, ref):
+    count, rows = ref.shape[:2]
+    if count > 4:
+        ref[...] = array.reshape(ref.shape)
+        return
+    for index in range(count):
+        ref[place ^ index] = array[index * rows : (index + 1) * rows]
 
 
 def head_probs(queries, key_rows):
@@ -445,7 +467,7 @@
     )(core, zb, w_up, up_bias, active_grad)
 
 
-def back_kernel(after_ref, bg_ref, w_ref, qkv_ref, za_ref, att_ref, grad_ref, sum_ref, wg_ref):
+def back_kernel(place_ref, after_ref, bg_ref, w_ref, qkv_ref, za_ref, att_ref, grad_ref, sum_ref, wg_ref):
     del after_ref
     heads = qkv_ref.shape[0]
     attended_grad = dot(bg_ref[...], w_ref[:, heads * 3 * HEAD :], 1, 0).T
@@ -466,14 +488,14 @@
     sum_ref[...] = jnp.sum(qkv_grad.astype(jnp.float32), axis=1, keepdims=True)
     qkv_part = dot(za_ref[...], qkv_grad, 1, 1).astype(LOW)
     out_part = dot(bg_ref[...], att_ref[...], 0, 0).astype(LOW)
-    wg_ref[...] = jnp.concatenate([qkv_part, out_part], axis=1).reshape(wg_ref.shape)
-
-
-def attend_back(after, branch_all, w_first, qkv, za, attended, n_dp):
+    store_parts(place_ref[1], jnp.concatenate([qkv_part, out_part], axis=1), wg_ref)
+
+
+def attend_back(place, after, branch_all, w_first, qkv, za, attended, n_dp):
     tokens, width = attended.shape
     return pl.pallas_call(
         back_kernel,
-        in_specs=[ANY] + [VMEM] * 5,
+        in_specs=[SMEM, ANY] + [VMEM] * 5,
         out_specs=[VMEM] * 3,
         out_shape=(
             jax.ShapeDtypeStruct((3 * width, tokens), LOW),
@@ -482,7 +504,7 @@
         ),
         compiler_params=BIG,
         name="attend_back",
-    )(after, branch_all, w_first, qkv, za, attended)
+    )(place, after, branch_all, w_first, qkv, za, attended)
 
 
 def first_kernel(core_ref, w_ref, grad_ref, x_ref, mean_ref, inv_ref, gain_ref, theirs_ref, mine_ref, sum_ref):
@@ -581,8 +603,7 @@
     ) * width + index % width
     index = (feature % n_dp) * (D // n_dp) + feature // n_dp
     order = (lax.broadcasted_iota(jnp.int32, (D, D), 1) == index[:, None]).astype(LOW)
-    turn = (lax.broadcasted_iota(jnp.int32, (D, D), 0) == index[None, :]).astype(LOW)
-    order, turn = lax.optimization_barrier((order, turn))
+    order = lax.optimization_barrier(order)
 
     def returned(rows):
         return exchange_rows(rows.reshape(n_row, shard_rows, -1))
@@ -593,12 +614,11 @@
     first_rows = exchange_rows(first_rows).reshape(D // n_dp, -1)
     x_all = lax.all_gather(x_own, ("col", "row"), axis=0, tiled=True)
     first_parts = gather_parts(first_rows, "dp")
-    rest, cot_own = prepare(
-        x_all, up_master, flat(down_master), n_row, cotangent.T, padded
-    )
-    rest = exchange_rows(rest).reshape(D // n_dp, -1)
-    rest_parts = gather_parts(rest, "dp")
-    cot_all = lax.all_gather(cot_own, ("row", "col"), axis=0)
+    rest, cot_own = prepare(place, up_master, flat(down_master), n_row, cotangent.T, padded)
+    once = zero_of(x_all).astype(LOW)
+    sent = exchange_rows(rest + once).reshape(D // n_dp, -1)
+    rest_parts = gather_parts(sent, "dp")
+    cot_all = lax.all_gather(cot_own + once, ("row", "col"), axis=0)
 
     vectors = jnp.concatenate([norm_gains, biases[: 6 * D].reshape(6, D)])
     query_bias = lax.dynamic_slice_in_dim(biases, 2 * D + own * width, width).reshape(heads, HEAD)
@@ -610,12 +630,16 @@
         3 * width, 1
     )
 
-    za, x_mean, inverse_one, gain_one = norm_first(vectors, x_all, turn, n_row)
-
-    w_first, qkv, attended, theirs, mine = attend(place, rest, za, qkv_bias, first_parts, width)
+    za, x_mean, inverse_one, gain_one = norm_first(
+        (*first_parts[1:], rest), vectors, x_all, index[None, :], n_row
+    )
+
+    w_first, qkv, attended, theirs, mine = attend(place, sent, za, qkv_bias, first_parts, width)
     pair = (mine.astype(jnp.float32) + swap_cores(theirs).astype(jnp.float32)).astype(LOW)
     branch = sum_over_rows(pair)
-    x_mine, dealt = own_rows_of(place, pair, vectors, x_all, turn, n_row, chunk)
+    x_mine, dealt = own_rows_of(
+        place, pair, cot_all, vectors, x_all, order, n_row, chunk
+    )
     gain_two, shift_two, out_bias = dealt[1], dealt[3], dealt[6]
 
     middle = x_mine + branch + (out_bias + zero_of(rest_parts[-1]))[None, :]
@@ -648,13 +672,14 @@
     middle_grad = middle_grad.astype(LOW)
     branch_all = lax.all_gather(middle_grad, ("col", "row"), axis=0, tiled=True)
     later = zero_of(middle_grad)
-    result = sum_over_rows(result) + down_bias[:, None]
+    summed = lax.psum_scatter(result, "row", scatter_dimension=0, tiled=True)
+    result = summed.astype(jnp.float32) + down_bias[:, None]
     result = result.astype(LOW)[:, :tokens].T
     rest_rows = sum_blocks(rest_grad, "dp", later)
     rest_rows = rest_rows + zero_of(branch_all).astype(LOW)
 
     qkv_grad, bias_sums, first_grad = attend_back(
-        rest_rows, branch_all, w_first, qkv, za, attended, n_dp
+        place, summed, branch_all, w_first, qkv, za, attended, n_dp
     )
     theirs, mine, one_sums = first_back(
         core_of, qkv_mixed, qkv_grad, x_all, x_mean, inverse_one, gain_one, width, n_row
@@ -663,7 +688,7 @@
     pair = mine.astype(jnp.float32) + zero_of(rest_blocks)
     pair = (pair + swap_cores(theirs).astype(jnp.float32)).astype(LOW)
     one_grad = sum_over_rows(pair.reshape(-1, padded))
-    first_rows = sum_blocks(first_grad, "dp", 0.0)
+    first_rows = sum_parts(first_grad, "dp")
 
     own_gain = lax.dynamic_slice_in_dim(norm_gains[0], feature_start, width)[:, None]
     own_normed = (x_own.astype(jnp.float32) - x_mean) * inverse_one

time: 400 us -> 393 us (0.983)
  Pallas kernels: 106 us -> 91 us
  starting transfers between devices: 38.4 us -> 48.4 us
  waiting for transfers between devices: 163 us -> 157 us
    all_gather x1, waiting for transfers between devices: 20 us -> 0.02 us  [shards(): cot_all = lax.all_gather(cot_own + once, ('row', 'col'), axis=0)]
    pallas_call x1, Pallas kernels: 21.3 us -> 9 us  [attend(): pl.pallas_call(attend_kernel, in_specs=[SMEM, ANY, VMEM, VMEM] + [VMEM] *...]
    all_gather x1, starting transfers between devices: 0.04 us -> 12.3 us  [shards(): zb = lax.all_gather(zb, ('col', 'row'), axis=0, tiled=True)]
    reduce_scatter x4 -> x3, waiting for transfers between devices: 5.49 us -> 17.2 us  [sum_over_rows(): lax.psum_scatter(half.astype(LOW), 'row', scatter_dimension=0, tiled=True)]
    ppermute x0 -> x3, waiting for transfers between devices: none -> 10.9 us  [sum_parts(): got = lax.ppermute(blocks[step], axis, [(i, i ^ step) for i in range(size)])]
    all_gather x1, waiting for transfers between devices: 0.02 us -> 10.8 us  [shards(): branch_all = lax.all_gather(middle_grad, ('col', 'row'), axis=0, tiled=True)]
    all_gather x1, waiting for transfers between devices: 9.99 us -> 0.42 us  [shards(): zb = lax.all_gather(zb, ('col', 'row'), axis=0, tiled=True)]
    ppermute x5, waiting for transfers between devices: 13.3 us -> 4.68 us  [all_sum(): lax.ppermute(vector, axis, [(i, i ^ step) for i in range(size)])]
  transfers between devices with their start and end apart: 29 -> 31, of which waited for: 15 -> 21; matrix products, arithmetic and copies ran while one was open for 13% -> 14% of each run, Pallas kernels for 14% -> 16%
where the time goes in v3:
time: 393 us; the launch traced here: 389 us
  waiting for transfers between devices  157 us (40%)
  Pallas kernels  91 us (23%)
  starting transfers between devices  48.4 us (12%)
  other arithmetic  40.3 us (10%)
  local copies, waits for them, and re-layouts  28.7 us (7%)
  between operations  19.8 us (5%)
    ppermute x6, waiting for transfers between devices, gather_parts(): lax.ppermute(block, axis, [(i, i ^ step) for i in range(size)])  31.4 us
    all_to_all x1, waiting for transfers between devices, sum_blocks(): blocks = lax.all_to_all(blocks, axis, 0, 0)  29 us
    all_gather x1, waiting for transfers between devices, shards(): x_all = lax.all_gather(x_own, ('col', 'row'), axis=0, tiled=True)  25.6 us
    all_to_all x4, waiting for transfers between devices, exchange_rows(): return lax.all_to_all(blocks, 'row', 0, 0)  19.1 us
    reduce_scatter x3, waiting for transfers between devices, sum_over_rows(): lax.psum_scatter(half.astype(LOW), 'row', scatter_dimension=0, tiled=True)  17.2 us
    all_to_all x4, starting transfers between devices, exchange_rows(): return lax.all_to_all(blocks, 'row', 0, 0)  14.5 us
    all_gather x1, starting transfers between devices, shards(): zb = lax.all_gather(zb, ('col', 'row'), axis=0, tiled=True)  12.3 us
    pallas_call x2, Pallas kernels, adam(): pl.pallas_call(partial(adam_kernel, rates), in_specs=[ANY] + [VMEM] * (1...  11.9 us
  transfers between devices with their start and end apart: 31, of which 21 were waited for; matrix products, arithmetic and copies ran while one was open for 14% of the time, Pallas kernels for 16%

profile of v3, /device:TPU:0, one launch (start us, length us, event | category | flops | bytes accessed | tf_op | source)
XLA Modules:
  0.0 388.7 jit_solution(8387739750641706362)
XLA Ops:
  7.8 2.7 prepare.3
  10.6 3.6 prepare.2
  14.2 25.6 %all-gather.6.cloned.1.call-done.x_ref = bf16[1152,768]{1,0:T(8,128)(2,1)} async-done(((bf16[144,768]{1,0:T(8,128)(2,1)}), bf16[1152,768]{1,0:T(8,128)(2,1)}) %all-gather.6.cloned.1.call-update) | async-done | bytes 1769488 | tf_op jit(solution)/shard_map/all_gather | solution.py:615
  43.4 3.5 all-to-all-start.1
  47.8 17.5 %all-to-all-done.1 = bf16[4,72,576]{2,1,0:T(8,128)(2,1)S(1)} async-done(((bf16[4,72,576]{2,1,0:T(8,128)(2,1)}), bf16[4,72,576]{2,1,0:T(8,128)(2,1)S(1)}, u32[]{:S(2)}, u32[]{:S(2)}) %all-to-all-start.1) | async-done | bytes 331808 | tf_op jit(solution)/shard_map/all_to_all | solution.py:58
  65.2 3.5 all-to-all-start
  75.4 6.2 %collective-permute-done.refs_0_.refs_1_ = bf16[288,576]{1,0:T(8,128)(2,1)S(1)} collective-permute-done((bf16[288,576]{1,0:T(8,128)(2,1)S(1)}, bf16[288,576]{1,0:T(8,128)(2,1)S(1)}, u32[]{:S(2)}, u32[]{:S(2)}) %collective-permute-start) | collective-permute-done | bytes 331808 | tf_op jit(solution)/shard_map/ppermute | solution.py:48
  81.6 5.1 %collective-permute-done.1.refs_1_.refs_2_ = bf16[288,576]{1,0:T(8,128)(2,1)S(1)} collective-permute-done((bf16[288,576]{1,0:T(8,128)(2,1)S(1)}, bf16[288,576]{1,0:T(8,128)(2,1)S(1)}, u32[]{:S(2)}, u32[]{:S(2)}) %collective-permute-start.1) | collective-permute-done | bytes 331808 | tf_op jit(solution)/shard_map/ppermute | solution.py:48
  88.2 6.3 %norm_first.1 = (bf16[1152,768]{1,0:T(8,128)(2,1)}, f32[1,768]{1,0:T(1,128)}, f32[1,768]{1,0:T(1,128)}, f32[1152,1]{1,0:T(8,128)}) custom-call(f32[8,1152]{1,0:T(8,128)} %pad_maximum_fusion.vectors_ref, bf16[1152,768]{1,0:T(8,128)(2,1)} %all-gather.6.cloned.1.call-done.x_ref, s32[1,1152]{1,0:T(1,128)} %fusion.52.index_ref, bf16[288,576]{1,0:T(8,128)(2,1)} %copy-done.8, ...), custom_call_target="tpu_custom_call" | custom-call | tf_op jit(solution)/shard_map/norm_first/pallas_call | solution.py:158
  95.4 9.0 %attend.1 = (bf16[1152,576]{1,0:T(8,128)(2,1)}, bf16[2,3,72,768]{3,2,1,0:T(8,128)(2,1)}, bf16[768,144]{1,0:T(8,128)(2,1)}, bf16[384,1152]{1,0:T(8,128)(2,1)}, bf16[384,1152]{1,0:T(8,128)(2,1)}) custom-call(s32[3]{0:T(128)} %pad_add_fusion.after_ref.place_ref, bf16[288,1076]{1,0:T(8,128)(2,1)} %bitcast.55, bf16[1152,768]{1,0:T(8,128)(2,1)} %get-tuple-element.69.za_ref, ...), custom_call_target="tpu_custom_call" | custom-call | tf_op jit(solution)/shard_map/attend/pallas_call | solution.py:293
  109.5 12.3 %all-gather.8.cloned.1.call-start = ((), (), s32[]{:S(2)}) async-start(), calls=%async_computation.11 | async-start | bytes 1990656 | tf_op jit(solution)/shard_map/all_gather | solution.py:653
  125.4 14.4 %collective-permute-done.4.refs_3_ = bf16[288,1076]{1,0:T(8,128)(2,1)S(1)} collective-permute-done((bf16[288,1076]{1,0:T(8,128)(2,1)S(1)}, bf16[288,1076]{1,0:T(8,128)(2,1)S(1)}, u32[]{:S(2)}, u32[]{:S(2)}) %collective-permute-start.4) | collective-permute-done | bytes 619808 | tf_op jit(solution)/shard_map/ppermute | solution.py:48
  140.9 5.1 %own_rows.1 = (f32[96,1152]{1,0:T(8,128)}, f32[8,1152]{1,0:T(8,128)}) custom-call(s32[3]{0:T(128)} %pad_add_fusion.after_ref.place_ref, bf16[384,1152]{1,0:T(8,128)(2,1)} %add_convert_fusion.3.after_ref, bf16[8,144,768]{2,1,0:T(8,128)(2,1)} %bitcast.53, f32[8,1152]{1,0:T(8,128)} %pad_maximum_fusion.vectors_ref, ...), custom_call_target="tpu_custom_call" | custom-call | tf_op jit(solution)/shard_map/own_rows/pallas_call | solution.py:190
  152.1 7.9 %beside.1 = (bf16[768,1152]{1,0:T(8,128)(2,1)}, bf16[1152,432]{1,0:T(8,128)(2,1)}) custom-call(bf16[96,1152]{1,0:T(8,128)(2,1)} %add_convert_fusion.5.after_ref, bf16[1152,1152]{1,0:T(8,128)(2,1)} %fusion.order_ref, bf16[8,144,768]{2,1,0:T(8,128)(2,1)} %bitcast.54, bf16[1152,576]{1,0:T(8,128)(2,1)} %get-tuple-element.75.w_ref), custom_call_target="tpu_custom_call" | custom-call | tf_op jit(solution)/shard_map/beside/pallas_call | solution.py:327
  160.1 5.5 %collective-permute-done.5.refs_1_ = bf16[288,1076]{1,0:T(8,128)(2,1)S(1)} collective-permute-done((bf16[288,1076]{1,0:T(8,128)(2,1)S(1)}, bf16[288,1076]{1,0:T(8,128)(2,1)S(1)}, u32[]{:S(2)}, u32[]{:S(2)}) %collective-permute-start.5) | collective-permute-done | bytes 619808 | tf_op jit(solution)/shard_map/ppermute | solution.py:48
  166.6 8.9 %before.1 = (bf16[1152,538]{1,0:T(8,128)(2,1)}, f32[768,538]{1,0:T(8,128)}, bf16[1152,538]{1,0:T(8,128)(2,1)}) custom-call(s32[3]{0:T(128)} %pad_add_fusion.after_ref.place_ref, bf16[96,1152]{1,0:T(8,128)(2,1)} %add_convert_fusion.5.after_ref, bf16[1152,1152]{1,0:T(8,128)(2,1)} %fusion.order_ref, bf16[768,1152]{1,0:T(8,128)(2,1)} %get-tuple-element.76.cot_ref, ...), custom_call_target="tpu_custom_call" | custom-call | tf_op jit(solution)/shard_map/before/pallas_call | solution.py:353
  176.0 9.4 %mlp.1 = (bf16[768,538]{1,0:T(8,128)(2,1)}, bf16[768,538]{1,0:T(8,128)(2,1)}, bf16[384,1152]{1,0:T(8,128)(2,1)}, bf16[384,1152]{1,0:T(8,128)(2,1)}, f32[1,538]{1,0:T(1,128)}) custom-call(s32[1]{0:T(128)} %bitcast.core_ref, bf16[768,1152]{1,0:T(8,128)(2,1)} %all-gather.8.cloned.1.call-done.zb_ref, bf16[1152,538]{1,0:T(8,128)(2,1)} %get-tuple-element.77.up_ref, ...), custom_call_target="tpu_custom_call" | custom-call | tf_op jit(solution)/shard_map/mlp/pallas_call | solution.py:439
  192.2 10.1 %behind.1 = (bf16[4,288,1076]{2,1,0:T(8,128)(2,1)}, bf16[576,768]{1,0:T(8,128)(2,1)}, bf16[576,768]{1,0:T(8,128)(2,1)}) custom-call(s32[3]{0:T(128)} %pad_add_fusion.after_ref.place_ref, bf16[384,1152]{1,0:T(8,128)(2,1)} %add_convert_fusion.2.after_ref, bf16[768,1152]{1,0:T(8,128)(2,1)} %all-gather.8.cloned.1.call-done.zb_ref, ...), custom_call_target="tpu_custom_call" | custom-call | tf_op jit(solution)/shard_map/behind/pallas_call | solution.py:385
  209.1 6.9 %reduce-scatter.9.cloned.1.call-done = bf16[96,1152]{1,0:T(8,128)(2,1)} async-done(((bf16[384,1152]{1,0:T(8,128)(2,1)}), bf16[96,1152]{1,0:T(8,128)(2,1)}) %reduce-scatter.9.cloned.1.call-update) | async-done | bytes 221200 | tf_op jit(solution)/shard_map/reduce_scatter | solution.py:78
  220.3 5.0 %all-to-all-start.2 = ((bf16[4,288,1076]{2,1,0:T(8,128)(2,1)}), bf16[4,288,1076]{2,1,0:T(8,128)(2,1)}, u32[]{:S(2)}, u32[]{:S(2)}) async-start(bf16[4,288,1076]{2,1,0:T(8,128)(2,1)} %get-tuple-element.94), calls=%async_computation.5 | async-start | bytes 5308416 | tf_op jit(solution)/shard_map/all_to_all | solution.py:62
  227.2 29.0 %all-to-all-done.2 = bf16[4,288,1076]{2,1,0:T(8,128)(2,1)} async-done(((bf16[4,288,1076]{2,1,0:T(8,128)(2,1)}), bf16[4,288,1076]{2,1,0:T(8,128)(2,1)}, u32[]{:S(2)}, u32[]{:S(2)}) %all-to-all-start.2) | async-done | bytes 2479136 | tf_op jit(solution)/shard_map/all_to_all | solution.py:62
  258.6 10.8 %all-gather.10.cloned.1.call-done.bg_ref = bf16[768,1152]{1,0:T(8,128)(2,1)} async-done(((bf16[96,1152]{1,0:T(8,128)(2,1)}), bf16[768,1152]{1,0:T(8,128)(2,1)}) %all-gather.10.cloned.1.call-update) | async-done | bytes 1769488 | tf_op jit(solution)/shard_map/all_gather | solution.py:673
  269.4 10.7 %attend_back.1 = (bf16[432,768]{1,0:T(8,128)(2,1)}, f32[432,1]{1,0:T(8,128)}, bf16[4,288,576]{2,1,0:T(8,128)(2,1)}) custom-call(s32[3]{0:T(128)} %pad_add_fusion.after_ref.place_ref, bf16[144,768]{1,0:T(8,128)(2,1)} %reduce-scatter.7.cloned.1.call-done.after_ref, bf16[768,1152]{1,0:T(8,128)(2,1)} %all-gather.10.cloned.1.call-done.bg_ref, ...), custom_call_target="tpu_custom_call" | custom-call | tf_op jit(solution)/shard_map/attend_back/pallas_call | solution.py:496
  280.1 5.5 %first_back.1 = (bf16[4,160,768]{2,1,0:T(8,128)(2,1)}, bf16[4,160,768]{2,1,0:T(8,128)(2,1)}, f32[1152,2]{1,0:T(8,128)}) custom-call(s32[1]{0:T(128)} %bitcast.core_ref, bf16[1152,432]{1,0:T(8,128)(2,1)} %get-tuple-element.87.w_ref, bf16[432,768]{1,0:T(8,128)(2,1)} %get-tuple-element.90.grad_ref, bf16[1152,768]{1,0:T(8,128)(2,1)} %all-gather.6.cloned.1.call-done.x_ref, ...), custom_call_target="tpu_custom_call" | custom-call | tf_op jit(solution)/shard_map/first_back/pallas_call | solution.py:540
  288.6 3.5 all-to-all-start.3
  321.4 3.3 collective-permute-done.14
  326.0 3.4 collective-permute-done.12
  329.4 7.5 %collective-permute-done.11 = bf16[288,576]{1,0:T(8,128)(2,1)} collective-permute-done((bf16[288,576]{1,0:T(8,128)(2,1)}, bf16[288,576]{1,0:T(8,128)(2,1)}, u32[]{:S(2)}, u32[]{:S(2)}) %collective-permute-start.11) | collective-permute-done | bytes 331808 | tf_op jit(solution)/shard_map/ppermute | solution.py:72
  339.1 4.1 %all-to-all-start.4 = ((bf16[4,72,576]{2,1,0:T(8,128)(2,1)}), bf16[4,72,576]{2,1,0:T(8,128)(2,1)}, u32[]{:S(2)}, u32[]{:S(2)}) async-start(bf16[4,72,576]{2,1,0:T(8,128)(2,1)} %bitcast.25), calls=%async_computation.8 | async-start | bytes 737280 | tf_op jit(solution)/shard_map/all_to_all | solution.py:58
  352.2 7.2 %adam.3 = (f32[72,1,2152]{2,1,0:T(1,128)}, f32[72,1,2152]{2,1,0:T(1,128)}, f32[72,1,2152]{2,1,0:T(1,128)}, f32[72,1,2152]{2,1,0:T(1,128)}, f32[72,1,2152]{2,1,0:T(1,128)}, /*index=5*/f32[72,1,2152]{2,1,0:T(1,128)}) custom-call(bf16[4,160,768]{2,1,0:T(8,128)(2,1)} %copy-done.1, bf16[4,72,1076]{2,1,0:T(8,128)(2,1)} %copy-done.5, f32[72,1,2152]{2,1,0:T(1,128)} %refs_0_.3, ...), custom_call_target="tpu_custom_call" | custom-call | tf_op jit(solution)/shard_map/adam/pallas_call | solution.py:220
  359.4 4.7 %adam.2 = (f32[72,1,1728]{2,1,0:T(1,128)}, f32[72,1,1728]{2,1,0:T(1,128)}, f32[72,1,1728]{2,1,0:T(1,128)}, f32[72,1,576]{2,1,0:T(1,128)}, f32[72,1,576]{2,1,0:T(1,128)}, /*index=5*/f32[72,1,576]{2,1,0:T(1,128)}) custom-call(bf16[4,160,768]{2,1,0:T(8,128)(2,1)} %copy-done.1, bf16[4,72,576]{2,1,0:T(8,128)(2,1)} %all-to-all-done.4.blocks_ref, ...), custom_call_target="tpu_custom_call" | custom-call | tf_op jit(solution)/shard_map/adam/pallas_call | solution.py:220
  368.6 10.3 %reduce-scatter.11.cloned.1.call-done = bf16[160,768]{1,0:T(8,128)(2,1)} async-done(((bf16[640,768]{1,0:T(8,128)(2,1)}), bf16[160,768]{1,0:T(8,128)(2,1)}) %reduce-scatter.11.cloned.1.call-update) | async-done | bytes 245776 | tf_op jit(solution)/shard_map/reduce_scatter | solution.py:78
  (213 shorter events, 100.6 us)
Async XLA Ops:
  7.2 32.6 %all-gather.6.cloned.1.call-start = ((), (), s32[]{:S(2)}) async-start(), calls=%async_computation.9 | async-start | bytes 1990656 | tf_op jit(solution)/shard_map/all_gather | solution.py:615
  10.6 130.3 %all-gather.12.cloned.1.call-start = ((), (), s32[]{:S(2)}) async-start(), calls=%async_computation.16 | async-start | bytes 1990656 | tf_op jit(solution)/shard_map/all_gather | solution.py:621
  14.2 32.6 %copy-start.4 = (bf16[4,72,1076]{2,1,0:T(8,128)(2,1)S(1)}, bf16[4,72,1076]{2,1,0:T(8,128)(2,1)}, u32[]{:S(2)}) copy-start(bf16[4,72,1076]{2,1,0:T(8,128)(2,1)} %get-tuple-element.66.refs_3_) | copy-start | bytes 1859332
  43.4 21.8 %all-to-all-start.1 = ((bf16[4,72,576]{2,1,0:T(8,128)(2,1)}), bf16[4,72,576]{2,1,0:T(8,128)(2,1)S(1)}, u32[]{:S(2)}, u32[]{:S(2)}) async-start(bf16[4,72,576]{2,1,0:T(8,128)(2,1)} %get-tuple-element.68), calls=%async_computation.1 | async-start | bytes 737280 | tf_op jit(solution)/shard_map/all_to_all | solution.py:58
  65.2 29.4 %all-to-all-start = ((bf16[4,72,1076]{2,1,0:T(8,128)(2,1)}), bf16[4,72,1076]{2,1,0:T(8,128)(2,1)S(1)}, u32[]{:S(2)}, u32[]{:S(2)}) async-start(bf16[4,72,1076]{2,1,0:T(8,128)(2,1)} %broadcast_add_fusion), calls=%async_computation | async-start | bytes 1327104 | tf_op jit(solution)/shard_map/all_to_all | solution.py:58
  68.7 78.3 %reduce-scatter.5.cloned.1.call-start = ((), (), s32[]{:S(2)}) async-start(), calls=%async_computation.10 | async-start | bytes 1105920 | tf_op jit(solution)/shard_map/reduce_scatter | solution.py:78
  70.3 11.3 %collective-permute-start = (bf16[288,576]{1,0:T(8,128)(2,1)S(1)}, bf16[288,576]{1,0:T(8,128)(2,1)S(1)}, u32[]{:S(2)}, u32[]{:S(2)}) collective-permute-start(bf16[288,576]{1,0:T(8,128)(2,1)S(1)} %bitcast.62), channel_id=1, source_target_pairs={{0,8},{8,0},{16,24},{24,16},{1,9},{9,1},{17,25},{25,17},{2,10},{10... | collective-permute-start | bytes 995336 | tf_op jit(solution)/shard_map/ppermute | solution.py:48
  71.8 15.0 %collective-permute-start.1 = (bf16[288,576]{1,0:T(8,128)(2,1)S(1)}, bf16[288,576]{1,0:T(8,128)(2,1)S(1)}, u32[]{:S(2)}, u32[]{:S(2)}) collective-permute-start(bf16[288,576]{1,0:T(8,128)(2,1)S(1)} %bitcast.63), channel_id=1, source_target_pairs={{0,16},{8,24},{16,0},{24,8},{1,17},{9,25},{17,1},{25,9},{2,18},{10... | collective-permute-start | bytes 995336 | tf_op jit(solution)/shard_map/ppermute | solution.py:48
  73.3 13.5 %collective-permute-start.2 = (bf16[288,576]{1,0:T(8,128)(2,1)S(1)}, bf16[288,576]{1,0:T(8,128)(2,1)S(1)}, u32[]{:S(2)}, u32[]{:S(2)}) collective-permute-start(bf16[288,576]{1,0:T(8,128)(2,1)S(1)} %bitcast.64), channel_id=1, source_target_pairs={{0,24},{8,16},{16,8},{24,0},{1,25},{9,17},{17,9},{25,1},{2,26},{10... | collective-permute-start | bytes 995336 | tf_op jit(solution)/shard_map/ppermute | solution.py:48
  104.4 2.6 collective-permute-start.3
  109.5 66.5 %all-gather.8.cloned.1.call-start = ((), (), s32[]{:S(2)}) async-start(), calls=%async_computation.11 | async-start | bytes 1990656 | tf_op jit(solution)/shard_map/all_gather | solution.py:653
  121.8 17.9 %collective-permute-start.4 = (bf16[288,1076]{1,0:T(8,128)(2,1)S(1)}, bf16[288,1076]{1,0:T(8,128)(2,1)S(1)}, u32[]{:S(2)}, u32[]{:S(2)}) collective-permute-start(bf16[288,1076]{1,0:T(8,128)(2,1)S(1)} %bitcast.57), channel_id=1, source_target_pairs={{0,24},{8,16},{16,8},{24,0},{1,25},{9,17},{17,9},{25,1},{2,26},{10... | collective-permute-start | bytes 1859336 | tf_op jit(solution)/shard_map/ppermute | solution.py:48
  149.3 66.6 %reduce-scatter.9.cloned.1.call-start = ((), (), s32[]{:S(2)}) async-start(), calls=%async_computation.13 | async-start | bytes 1105920 | tf_op jit(solution)/shard_map/reduce_scatter | solution.py:78
  149.4 16.2 %collective-permute-start.5 = (bf16[288,1076]{1,0:T(8,128)(2,1)S(1)}, bf16[288,1076]{1,0:T(8,128)(2,1)S(1)}, u32[]{:S(2)}, u32[]{:S(2)}) collective-permute-start(bf16[288,1076]{1,0:T(8,128)(2,1)S(1)} %bitcast.58), channel_id=1, source_target_pairs={{0,8},{8,0},{16,24},{24,16},{1,9},{9,1},{17,25},{25,17},{2,10},{10... | collective-permute-start | bytes 1859336 | tf_op jit(solution)/shard_map/ppermute | solution.py:48
  149.9 15.8 %collective-permute-start.6 = (bf16[288,1076]{1,0:T(8,128)(2,1)S(1)}, bf16[288,1076]{1,0:T(8,128)(2,1)S(1)}, u32[]{:S(2)}, u32[]{:S(2)}) collective-permute-start(bf16[288,1076]{1,0:T(8,128)(2,1)S(1)} %bitcast.59), channel_id=1, source_target_pairs={{0,16},{8,24},{16,0},{24,8},{1,17},{9,25},{17,1},{25,9},{2,18},{10... | collective-permute-start | bytes 1859336 | tf_op jit(solution)/shard_map/ppermute | solution.py:48
  185.3 2.7 collective-permute-start.7
  190.5 68.0 %reduce-scatter.7.cloned.1.call-start = ((), (), s32[]{:S(2)}) async-start(), calls=%async_computation.12 | async-start | bytes 1105920 | tf_op jit(solution)/shard_map/reduce_scatter | solution.py:675
  202.2 2.6 collective-permute-start.8
  207.2 62.2 %all-gather.10.cloned.1.call-start = ((), (), s32[]{:S(2)}) async-start(), calls=%async_computation.14 | async-start | bytes 1990656 | tf_op jit(solution)/shard_map/all_gather | solution.py:673
  220.3 35.9 %all-to-all-start.2 = ((bf16[4,288,1076]{2,1,0:T(8,128)(2,1)}), bf16[4,288,1076]{2,1,0:T(8,128)(2,1)}, u32[]{:S(2)}, u32[]{:S(2)}) async-start(bf16[4,288,1076]{2,1,0:T(8,128)(2,1)} %get-tuple-element.94), calls=%async_computation.5 | async-start | bytes 5308416 | tf_op jit(solution)/shard_map/all_to_all | solution.py:62
  285.6 26.0 %collective-permute-start.9 = (bf16[4,160,768]{2,1,0:T(8,128)(2,1)}, bf16[4,160,768]{2,1,0:T(8,128)(2,1)}, u32[]{:S(2)}, u32[]{:S(2)}) collective-permute-start(bf16[4,160,768]{2,1,0:T(8,128)(2,1)} %get-tuple-element.95), channel_id=1, source_target_pairs={{0,1},{1,0},{2,3},{3,2},{4,5},{5,4},{6,7},{7,6},{8,9},{9,8},{10,11... | collective-permute-start | bytes 2949128 | tf_op jit(solution)/shard_map/ppermute | solution.py:39
  288.6 21.7 %all-to-all-start.3 = ((bf16[4,72,1076]{2,1,0:T(8,128)(2,1)}), bf16[4,72,1076]{2,1,0:T(8,128)(2,1)S(1)}, u32[]{:S(2)}, u32[]{:S(2)}) async-start(bf16[4,72,1076]{2,1,0:T(8,128)(2,1)} %bitcast.16), calls=%async_computation.6 | async-start | bytes 1327104 | tf_op jit(solution)/shard_map/all_to_all | solution.py:58
  315.6 4.6 %collective-permute-start.13 = (f32[16,1152]{1,0:T(8,128)S(1)}, f32[16,1152]{1,0:T(8,128)S(1)}, u32[]{:S(2)}, u32[]{:S(2)}) collective-permute-start(f32[16,1152]{1,0:T(8,128)S(1)} %fusion.24), channel_id=1, source_target_pairs={{0,1},{1,0},{2,3},{3,2},{4,5},{5,4},{6,7},{7,6},{8,9},{9,8},{10,11... | collective-permute-start | bytes 221192 | tf_op jit(solution)/shard_map/ppermute | solution.py:90
  316.7 12.6 %collective-permute-start.12 = (bf16[288,576]{1,0:T(8,128)(2,1)}, bf16[288,576]{1,0:T(8,128)(2,1)}, u32[]{:S(2)}, u32[]{:S(2)}) collective-permute-start(bf16[288,576]{1,0:T(8,128)(2,1)} %get-tuple-element.137), channel_id=1, source_target_pairs={{0,24},{8,16},{16,8},{24,0},{1,25},{9,17},{17,9},{25,1},{2,26},{10... | collective-permute-start | bytes 995336 | tf_op jit(solution)/shard_map/ppermute | solution.py:72
  319.1 17.7 %collective-permute-start.11 = (bf16[288,576]{1,0:T(8,128)(2,1)}, bf16[288,576]{1,0:T(8,128)(2,1)}, u32[]{:S(2)}, u32[]{:S(2)}) collective-permute-start(bf16[288,576]{1,0:T(8,128)(2,1)} %get-tuple-element.138), channel_id=1, source_target_pairs={{0,16},{8,24},{16,0},{24,8},{1,17},{9,25},{17,1},{25,9},{2,18},{10... | collective-permute-start | bytes 995336 | tf_op jit(solution)/shard_map/ppermute | solution.py:72
  319.7 17.2 %collective-permute-start.10 = (bf16[288,576]{1,0:T(8,128)(2,1)}, bf16[288,576]{1,0:T(8,128)(2,1)}, u32[]{:S(2)}, u32[]{:S(2)}) collective-permute-start(bf16[288,576]{1,0:T(8,128)(2,1)} %get-tuple-element.136), channel_id=1, source_target_pairs={{0,8},{8,0},{16,24},{24,16},{1,9},{9,1},{17,25},{25,17},{2,10},{10... | collective-permute-start | bytes 995336 | tf_op jit(solution)/shard_map/ppermute | solution.py:72
  320.3 4.4 %collective-permute-start.14 = (f32[16,1152]{1,0:T(8,128)S(1)}, f32[16,1152]{1,0:T(8,128)S(1)}, u32[]{:S(2)}, u32[]{:S(2)}) collective-permute-start(f32[16,1152]{1,0:T(8,128)S(1)} %fusion.67), channel_id=1, source_target_pairs={{0,2},{2,0},{4,6},{6,4},{1,3},{3,1},{5,7},{7,5},{8,10},{10,8},{12,... | collective-permute-start | bytes 221192 | tf_op jit(solution)/shard_map/ppermute | solution.py:90
  324.7 18.8 %collective-permute-start.15 = (f32[16,1152]{1,0:T(8,128)S(1)}, f32[16,1152]{1,0:T(8,128)S(1)}, u32[]{:S(2)}, u32[]{:S(2)}) collective-permute-start(f32[16,1152]{1,0:T(8,128)S(1)} %add.410), channel_id=1, source_target_pairs={{0,4},{2,6},{4,0},{6,2},{1,5},{3,7},{5,1},{7,3},{8,12},{10,14},{12... | collective-permute-start | bytes 221192 | tf_op jit(solution)/shard_map/ppermute | solution.py:90
  339.1 20.2 %all-to-all-start.4 = ((bf16[4,72,576]{2,1,0:T(8,128)(2,1)}), bf16[4,72,576]{2,1,0:T(8,128)(2,1)}, u32[]{:S(2)}, u32[]{:S(2)}) async-start(bf16[4,72,576]{2,1,0:T(8,128)(2,1)} %bitcast.25), calls=%async_computation.8 | async-start | bytes 737280 | tf_op jit(solution)/shard_map/all_to_all | solution.py:58
  343.3 35.6 %reduce-scatter.11.cloned.1.call-start = ((), (), s32[]{:S(2)}) async-start(), calls=%async_computation.15 | async-start | bytes 1228800 | tf_op jit(solution)/shard_map/reduce_scatter | solution.py:78
  343.5 4.4 %collective-permute-start.16 = (f32[16,1152]{1,0:T(8,128)S(1)}, f32[16,1152]{1,0:T(8,128)S(1)}, u32[]{:S(2)}, u32[]{:S(2)}) collective-permute-start(f32[16,1152]{1,0:T(8,128)S(1)} %add.411), channel_id=1, source_target_pairs={{0,8},{8,0},{16,24},{24,16},{1,9},{9,1},{17,25},{25,17},{2,10},{10... | collective-permute-start | bytes 221192 | tf_op jit(solution)/shard_map/ppermute | solution.py:90
  348.6 15.5 %collective-permute-start.17 = (f32[16,1152]{1,0:T(8,128)}, f32[16,1152]{1,0:T(8,128)}, u32[]{:S(2)}, u32[]{:S(2)}) collective-permute-start(f32[16,1152]{1,0:T(8,128)} %add.412), channel_id=1, source_target_pairs={{0,16},{8,24},{16,0},{24,8},{1,17},{9,25},{17,1},{25,9},{2,18},{10... | collective-permute-start | bytes 221192 | tf_op jit(solution)/shard_map/ppermute | solution.py:90
  (26 other events, 246.9 us)
Sparse Core Ops, SparseCore 0:
  10.7 29.0 all-gather.5
  43.5 35.4 all-gather.11
  109.6 24.6 reduce-scatter.4
  149.4 26.4 all-gather.7
  190.7 25.2 reduce-scatter.8
  218.1 23.5 reduce-scatter.6
  243.9 25.4 all-gather.9
  352.3 26.5 reduce-scatter.10

commit v4 on v0

--- a/solution.py
+++ b/solution.py
@@ -174,6 +174,11 @@
     def _():
         mine_ref[...] = second
         theirs_ref[...] = first
+
+
+def join_cores(core, near_ref, far_ref, ref):
+    ref[core] = near_ref[...]
+    ref[1 - core] = far_ref[...]
 
 
 def attend_kernel(place_ref, after_ref, za_ref, bias_ref, *refs):
@@ -249,9 +254,9 @@
     )(place, after, order, cot_all, w_first, x_all)
 
 
-def before_kernel(place_ref, after_ref, order_ref, cot_ref, *refs):
-    del after_ref
-    *parts, up_ref, grad_ref, mixed_ref, scratch = refs
+def before_kernel(place_ref, near_ref, far_ref, order_ref, cot_ref, *refs):
+    *parts, zb_ref, up_ref, grad_ref, mixed_ref, scratch = refs
+    join_cores(place_ref[0], near_ref, far_ref, zb_ref)
     w_rest = assembled(place_ref[1], parts, scratch)
     wide = up_ref.shape[1]
     up_ref[...] = w_rest[:, :wide]
@@ -260,13 +265,14 @@
     mixed_ref[...] = dot(order_ref[...], w_down, 1, 0).astype(LOW)
 
 
-def before(place, after, order, cot_tokens, parts):
+def before(place, near, far, order, cot_tokens, parts):
     wide = parts[0].shape[1] // 2
     return pl.pallas_call(
         before_kernel,
-        in_specs=[SMEM, ANY, VMEM, VMEM] + [VMEM] * len(parts),
-        out_specs=[VMEM] * 3,
+        in_specs=[SMEM] + [VMEM] * (4 + len(parts)),
+        out_specs=[VMEM] * 4,
         out_shape=(
+            jax.ShapeDtypeStruct((2,) + near.shape, LOW),
             jax.ShapeDtypeStruct((D, wide), LOW),
             jax.ShapeDtypeStruct((cot_tokens.shape[0], wide), jnp.float32),
             jax.ShapeDtypeStruct((D, wide), LOW),
@@ -274,7 +280,7 @@
         scratch_shapes=[part_scratch(parts)],
         compiler_params=BIG,
         name="before",
-    )(place, after, order, cot_tokens, *parts)
+    )(place, near, far, order, cot_tokens, *parts)
 
 
 def behind_kernel(
@@ -379,9 +385,14 @@
     )(core, zb, w_up, up_bias, active_grad)
 
 
-def back_kernel(bg_ref, w_ref, qkv_ref, za_ref, att_ref, grad_ref, sum_ref, wg_ref):
+def back_kernel(
+    place_ref, after_ref, near_ref, far_ref, w_ref, qkv_ref, za_ref, att_ref, all_ref, grad_ref, sum_ref, wg_ref
+):
+    del after_ref
+    join_cores(place_ref[0], near_ref, far_ref, all_ref)
+    branch_all = all_ref[...].reshape(att_ref.shape[0], D)
     heads = qkv_ref.shape[0]
-    attended_grad = dot(bg_ref[...], w_ref[:, heads * 3 * HEAD :], 1, 0).T
+    attended_grad = dot(branch_all, w_ref[:, heads * 3 * HEAD :], 1, 0).T
     scale = HEAD ** (-0.5)
     parts = []
     for head in range(heads):
@@ -398,24 +409,25 @@
     grad_ref[...] = qkv_grad
     sum_ref[...] = jnp.sum(qkv_grad.astype(jnp.float32), axis=1, keepdims=True)
     qkv_part = dot(za_ref[...], qkv_grad, 1, 1).astype(LOW)
-    out_part = dot(bg_ref[...], att_ref[...], 0, 0).astype(LOW)
+    out_part = dot(branch_all, att_ref[...], 0, 0).astype(LOW)
     wg_ref[...] = jnp.concatenate([qkv_part, out_part], axis=1).reshape(wg_ref.shape)
 
 
-def attend_back(branch_all, w_first, qkv, za, attended, n_dp):
+def attend_back(place, after, near, far, w_first, qkv, za, attended, n_dp):
     tokens, width = attended.shape
     return pl.pallas_call(
         back_kernel,
-        in_specs=[VMEM] * 5,
-        out_specs=[VMEM] * 3,
+        in_specs=[SMEM, ANY] + [VMEM] * 6,
+        out_specs=[VMEM] * 4,
         out_shape=(
+            jax.ShapeDtypeStruct((2,) + near.shape, LOW),
             jax.ShapeDtypeStruct((3 * width, tokens), LOW),
             jax.ShapeDtypeStruct((3 * width, 1), jnp.float32),
             jax.ShapeDtypeStruct((n_dp, D // n_dp, 4 * width), LOW),
         ),
         compiler_params=BIG,
         name="attend_back",
-    )(branch_all, w_first, qkv, za, attended)
+    )(place, after, near, far, w_first, qkv, za, attended)
 
 
 def first_kernel(core_ref, w_ref, grad_ref, x_ref, mean_ref, inv_ref, gain_ref, theirs_ref, mine_ref, sum_ref):
@@ -578,8 +590,10 @@
     normed_two = center * inverse_two
     zb = (normed_two * gain_two + shift_two).astype(LOW)
     zb_rows = lax.all_gather(zb, "row", axis=0, tiled=True)
-    w_up, active_grad, down_mixed = before(place, zb_rows, order, cot_tokens, rest_parts)
-    zb = both_cores(zb_rows)
+    zb, w_up, active_grad, down_mixed = before(
+        place, zb_rows, swap_cores(zb_rows), order, cot_tokens, rest_parts
+    )
+    zb = zb.reshape(padded, D)
 
     core_of = core.reshape(1).astype(jnp.int32)
     active, hidden_grad, theirs, mine, up_sums = mlp(
@@ -600,21 +614,22 @@
     middle_grad = cot_mine + inverse_two * (scaled - first_sum - normed_two * second_sum)
     middle_grad = middle_grad.astype(LOW)
     branch_rows = lax.all_gather(middle_grad, "row", axis=0, tiled=True)
-    later = zero_of(branch_rows)
+    rest_rows = sum_blocks(rest_grad, "dp", zero_of(branch_rows))
+    rest_blocks = returned(rest_rows)
+    branch_all, qkv_grad, bias_sums, first_grad = attend_back(
+        place, rest_rows, branch_rows, swap_cores(branch_rows), w_first, qkv, za, attended, n_dp
+    )
+    branch_all = branch_all.reshape(padded, D)
+    theirs, mine, one_sums = first_back(
+        core_of, qkv_mixed, qkv_grad, x_all, x_mean, inverse_one, gain_one[:, None], width, n_row
+    )
+    pair = mine.astype(jnp.float32) + zero_of(rest_blocks)
+    pair = (pair + swap_cores(theirs).astype(jnp.float32)).astype(LOW)
+    one_grad = sum_over_rows(pair.reshape(-1, padded))
+    later = zero_of(one_grad)
     result = sum_over_rows(result + later) + down_bias[:, None]
     result = result.astype(LOW)[:, :tokens].T
-    branch_all = both_cores(branch_rows)
-
-    qkv_grad, bias_sums, first_grad = attend_back(
-        branch_all, w_first, qkv, za, attended, n_dp
-    )
-    theirs, mine, one_sums = first_back(
-        core_of, qkv_mixed, qkv_grad, x_all, x_mean, inverse_one, gain_one[:, None], width, n_row
-    )
-    pair = (mine.astype(jnp.float32) + swap_cores(theirs).astype(jnp.float32)).astype(LOW)
-    one_grad = sum_over_rows(pair.reshape(-1, padded))
     first_rows = sum_blocks(first_grad, "dp", 0.0)
-    rest_rows = sum_blocks(rest_grad, "dp", later)
 
     own_gain = lax.dynamic_slice_in_dim(norm_gains[0], feature_start, width)[:, None]
     own_normed = (x_own.astype(jnp.float32) - x_mean) * inverse_one
@@ -627,7 +642,6 @@
     )
     input_grad = input_grad.astype(LOW)[:, :tokens].T
 
-    later = zero_of(pair)
     bias_sums = bias_sums.reshape(heads, 3, HEAD)
     all_rows = jnp.stack(
         [
@@ -663,7 +677,7 @@
 
     rest_new = adam(
         pair,
-        returned(rest_rows),
+        rest_blocks,
         (0.03, 0.02),
         up_master,
         up_first,

time: 353 us -> 389 us (1.10)
  waiting for transfers between devices: 50.3 us -> 86.5 us
  blocking collectives: 74 us -> 83.7 us
  starting transfers between devices: 56.3 us -> 50.7 us
  other arithmetic: 35.4 us -> 30.8 us
    reduce_scatter x4, waiting for transfers between devices: 4.79 us -> 36.9 us  [sum_over_rows(): lax.psum_scatter(half.astype(LOW), 'row', scatter_dimension=0, tiled=True)]
    ppermute x6, waiting for transfers between devices: 0.02 us -> 28.2 us  [gather_parts(): lax.ppermute(block, axis, [(i, i ^ step) for i in range(size)])]
    all_to_all x0 -> x1, blocking collectives: none -> 21.2 us  [exchange_rows(): return lax.all_to_all(blocks, 'row', 0, 0)]
    all_gather x6 -> x2, blocking collectives: 15.6 us -> 5.45 us  [both_cores(): lax.all_gather(piece, 'col', axis=0)]
    all_to_all x2, waiting for transfers between devices: 10 us -> 0.01 us  [sum_blocks(): blocks = lax.all_to_all(blocks, axis, 0, 0)]
    all_to_all x4 -> x3, waiting for transfers between devices: 17.6 us -> 9.72 us  [exchange_rows(): return lax.all_to_all(blocks, 'row', 0, 0)]
    ppermute x5, waiting for transfers between devices: 12.8 us -> 6.44 us  [all_sum(): lax.ppermute(vector, axis, [(i, i ^ step) for i in range(size)])]
    all_to_all x4 -> x3, starting transfers between devices: 17.6 us -> 14.7 us  [exchange_rows(): return lax.all_to_all(blocks, 'row', 0, 0)]
  transfers between devices with their start and end apart: 26 -> 27, of which waited for: 10 -> 13; matrix products, arithmetic and copies ran while one was open for 17% -> 13% of each run, Pallas kernels for 16% -> 11%
where the time goes in v4:
time: 389 us; the launch traced here: 384 us
  waiting for transfers between devices  86.5 us (22%)
  blocking collectives  83.7 us (22%)
  Pallas kernels  82.8 us (21%)
  starting transfers between devices  50.7 us (13%)
  other arithmetic  30.8 us (8%)
  local copies, waits for them, and re-layouts  21.9 us (6%)
  between operations  20.2 us (5%)
  matrix products  7.7 us (2%)
    reduce_scatter x4, waiting for transfers between devices, sum_over_rows(): lax.psum_scatter(half.astype(LOW), 'row', scatter_dimension=0, tiled=True)  36.9 us
    ppermute x6, waiting for transfers between devices, gather_parts(): lax.ppermute(block, axis, [(i, i ^ step) for i in range(size)])  28.2 us
    all_to_all x1, blocking collectives, exchange_rows(): return lax.all_to_all(blocks, 'row', 0, 0)  21.2 us
    all_gather x1, blocking collectives, shards(): x_rows = lax.all_gather(x_after, 'row', axis=0, tiled=True)  19.2 us
    all_gather x1, blocking collectives, shards(): branch_rows = lax.all_gather(middle_grad, 'row', axis=0, tiled=True)  19.1 us
    all_gather x1, blocking collectives, shards(): zb_rows = lax.all_gather(zb, 'row', axis=0, tiled=True)  18.8 us
    all_to_all x3, starting transfers between devices, exchange_rows(): return lax.all_to_all(blocks, 'row', 0, 0)  14.7 us
    pallas_call x2, Pallas kernels, adam(): pl.pallas_call(partial(adam_kernel, rates), in_specs=[ANY] + [VMEM] * (1...  11.9 us
  transfers between devices with their start and end apart: 27, of which 13 were waited for; matrix products, arithmetic and copies ran while one was open for 13% of the time, Pallas kernels for 11%

profile of v4, /device:TPU:0, one launch (start us, length us, event | category | flops | bytes accessed | tf_op | source)
XLA Modules:
  0.0 384.3 jit_solution(3185749590498737313)
XLA Ops:
  11.2 6.4 %all-to-all-start = ((bf16[4,72,576]{2,1,0:T(8,128)(2,1)}), bf16[4,72,576]{2,1,0:T(8,128)(2,1)S(1)}, u32[]{:S(2)}, u32[]{:S(2)}) async-start(bf16[4,72,576]{2,1,0:T(8,128)(2,1)} %prepare.2), calls=%async_computation | async-start | bytes 737280 | tf_op jit(solution)/shard_map/all_to_all | solution.py:65
  19.7 9.1 %all-to-all-done = bf16[4,72,576]{2,1,0:T(8,128)(2,1)S(1)} async-done(((bf16[4,72,576]{2,1,0:T(8,128)(2,1)}), bf16[4,72,576]{2,1,0:T(8,128)(2,1)S(1)}, u32[]{:S(2)}, u32[]{:S(2)}) %all-to-all-start) | async-done | bytes 331808 | tf_op jit(solution)/shard_map/all_to_all | solution.py:65
  30.1 19.2 %all_gather.27.after_ref = bf16[576,768]{1,0:T(8,128)(2,1)} all-gather(bf16[144,768]{1,0:T(8,128)(2,1)S(1)} %pad_add_fusion.1), channel_id=1, replica_groups=mesh['dp'=4,'row'=4,'col'=2] {'row'}, dimensions={0}, use_global_device_ids=true | all-gather | bytes 1105920 | tf_op jit(solution)/shard_map/all_gather | solution.py:549
  49.3 3.6 prepare.3
  52.8 4.2 %all-to-all-start.1 = ((bf16[4,72,1076]{2,1,0:T(8,128)(2,1)}), bf16[4,72,1076]{2,1,0:T(8,128)(2,1)}, u32[]{:S(2)}, u32[]{:S(2)}) async-start(bf16[4,72,1076]{2,1,0:T(8,128)(2,1)} %prepare.3), calls=%async_computation.1 | async-start | bytes 1327104 | tf_op jit(solution)/shard_map/all_to_all | solution.py:65
  74.5 3.0 all-gather
  78.6 4.0 %fusion.3.za_ref = bf16[1152,768]{1,0:T(8,128)(2,1)} fusion(bf16[1152,1152]{1,0:T(8,128)(2,1)S(1)} %fusion.order_ref, bf16[1152,768]{1,0:T(8,128)(2,1)S(1)} %bitcast.54, f32[1152]{0:T(1024)S(1)} %copy-done.33, f32[1152]{0:T(1024)S(1)} %copy-done.34, f32[768]{0:T(1024)S(1)} %add_rsqrt_fusion, f32[768]{0:T(1024)S(1)} %broadcast_multiply_fusion), kind=kOutput, calls=%fused_computation.9 | convolution fusion | flops 2043740160 | bytes 6208512 | tf_op jit(solution)/shard_map/dot_general | solution.py:24
  82.6 9.1 %attend.1 = (bf16[1152,576]{1,0:T(8,128)(2,1)}, bf16[2,3,72,768]{3,2,1,0:T(8,128)(2,1)}, bf16[768,144]{1,0:T(8,128)(2,1)}, bf16[384,1152]{1,0:T(8,128)(2,1)}, bf16[384,1152]{1,0:T(8,128)(2,1)}) custom-call(s32[3]{0:T(128)} %pad_add_fusion.2.after_ref.place_ref, bf16[288,1076]{1,0:T(8,128)(2,1)} %bitcast.8.after_ref.refs_0_, bf16[1152,768]{1,0:T(8,128)(2,1)} %fusion.3.za_ref, ...), custom_call_target="tpu_custom_call" | custom-call | tf_op jit(solution)/shard_map/attend/pallas_call | solution.py:207
  96.8 11.4 %reduce-scatter.7.cloned.1.call-start = ((), (), s32[]{:S(2)}) async-start(), calls=%async_computation.11 | async-start | bytes 1105920 | tf_op jit(solution)/shard_map/reduce_scatter | solution.py:74
  109.3 9.2 %beside.1 = (bf16[768,1152]{1,0:T(8,128)(2,1)}, bf16[1152,432]{1,0:T(8,128)(2,1)}, f32[96,1152]{1,0:T(8,128)}) custom-call(s32[3]{0:T(128)} %pad_add_fusion.2.after_ref.place_ref, bf16[384,1152]{1,0:T(8,128)(2,1)} %add_convert_fusion.5.after_ref, bf16[1152,1152]{1,0:T(8,128)(2,1)} %copy-done, bf16[8,144,768]{2,1,0:T(8,128)(2,1)} %bitcast.69, ...), custom_call_target="tpu_custom_call" | custom-call | tf_op jit(solution)/shard_map/beside/pallas_call | solution.py:243
  118.5 3.8 reduce-scatter.5.cloned.1.call-done
  123.9 18.8 %all_gather.34.near_ref = bf16[384,1152]{1,0:T(8,128)(2,1)S(1)} all-gather(bf16[96,1152]{1,0:T(8,128)(2,1)S(1)} %add_convert_fusion.7), channel_id=1, replica_groups=mesh['dp'=4,'row'=4,'col'=2] {'row'}, dimensions={0}, use_global_device_ids=true | all-gather | bytes 1105920 | tf_op jit(solution)/shard_map/all_gather | solution.py:592
  147.5 13.1 %collective-permute-done.5.refs_1_ = bf16[288,1076]{1,0:T(8,128)(2,1)S(1)} collective-permute-done((bf16[288,1076]{1,0:T(8,128)(2,1)}, bf16[288,1076]{1,0:T(8,128)(2,1)S(1)}, u32[]{:S(2)}, u32[]{:S(2)}) %collective-permute-start.5) | collective-permute-done | bytes 619808 | tf_op jit(solution)/shard_map/ppermute | solution.py:55
  160.6 15.1 %collective-permute-done.6.refs_2_ = bf16[288,1076]{1,0:T(8,128)(2,1)} collective-permute-done((bf16[288,1076]{1,0:T(8,128)(2,1)}, bf16[288,1076]{1,0:T(8,128)(2,1)}, u32[]{:S(2)}, u32[]{:S(2)}) %collective-permute-start.6) | collective-permute-done | bytes 619808 | tf_op jit(solution)/shard_map/ppermute | solution.py:55
  176.7 10.5 %before.1 = (bf16[2,384,1152]{2,1,0:T(8,128)(2,1)}, bf16[1152,538]{1,0:T(8,128)(2,1)}, f32[768,538]{1,0:T(8,128)}, bf16[1152,538]{1,0:T(8,128)(2,1)}) custom-call(s32[3]{0:T(128)} %pad_add_fusion.2.after_ref.place_ref, bf16[384,1152]{1,0:T(8,128)(2,1)} %copy-done.5, bf16[384,1152]{1,0:T(8,128)(2,1)} %copy-done.12, bf16[1152,1152]{1,0:T(8,128)(2,1)} %copy-done, ...), custom_call_target="tpu_custom_call" | custom-call | tf_op jit(solution)/shard_map/before/pallas_call | solution.py:270
  187.2 9.4 %mlp.1 = (bf16[768,538]{1,0:T(8,128)(2,1)}, bf16[768,538]{1,0:T(8,128)(2,1)}, bf16[384,1152]{1,0:T(8,128)(2,1)}, bf16[384,1152]{1,0:T(8,128)(2,1)}, f32[1,538]{1,0:T(1,128)}) custom-call(s32[1]{0:T(128)} %bitcast.core_ref, bf16[768,1152]{1,0:T(8,128)(2,1)} %bitcast.64, bf16[1152,538]{1,0:T(8,128)(2,1)} %get-tuple-element.65.up_ref, ...), custom_call_target="tpu_custom_call" | custom-call | tf_op jit(solution)/shard_map/mlp/pallas_call | solution.py:357
  196.7 2.6 collective-permute-done.8
  203.3 10.1 %behind.1 = (bf16[4,288,1076]{2,1,0:T(8,128)(2,1)}, bf16[576,768]{1,0:T(8,128)(2,1)}, bf16[576,768]{1,0:T(8,128)(2,1)}) custom-call(s32[3]{0:T(128)} %pad_add_fusion.2.after_ref.place_ref, bf16[384,1152]{1,0:T(8,128)(2,1)} %add_convert_fusion.4.after_ref, bf16[768,1152]{1,0:T(8,128)(2,1)} %bitcast.65, bf16[768,538]{1,0:T(8,128)(2,1)} %get-tuple-element.69.hid_ref, ...), custom_call_target="tpu_custom_call" | custom-call | tf_op jit(solution)/shard_map/behind/pallas_call | solution.py:303
  213.4 4.6 %all-to-all-start.2 = ((bf16[4,288,1076]{2,1,0:T(8,128)(2,1)}), bf16[4,288,1076]{2,1,0:T(8,128)(2,1)}, u32[]{:S(2)}, u32[]{:S(2)}) async-start(bf16[4,288,1076]{2,1,0:T(8,128)(2,1)} %get-tuple-element.75), calls=%async_computation.3 | async-start | bytes 5308416 | tf_op jit(solution)/shard_map/all_to_all | solution.py:69
  218.0 7.3 %reduce-scatter.7.cloned.1.call-done = bf16[96,1152]{1,0:T(8,128)(2,1)} async-done(((bf16[384,1152]{1,0:T(8,128)(2,1)}), bf16[96,1152]{1,0:T(8,128)(2,1)}) %reduce-scatter.7.cloned.1.call-update) | async-done | bytes 221200 | tf_op jit(solution)/shard_map/reduce_scatter | solution.py:74
  228.9 19.1 %all_gather.35.near_ref = bf16[384,1152]{1,0:T(8,128)(2,1)S(1)} all-gather(bf16[96,1152]{1,0:T(8,128)(2,1)S(1)} %get-tuple-element.117), channel_id=1, replica_groups=mesh['dp'=4,'row'=4,'col'=2] {'row'}, dimensions={0}, use_global_device_ids=true | all-gather | bytes 1105920 | tf_op jit(solution)/shard_map/all_gather | solution.py:616
  251.5 3.4 add_reduce_fusion.after_ref
  254.9 10.8 %attend_back.1 = (bf16[2,384,1152]{2,1,0:T(8,128)(2,1)}, bf16[432,768]{1,0:T(8,128)(2,1)}, f32[432,1]{1,0:T(8,128)}, bf16[4,288,576]{2,1,0:T(8,128)(2,1)}) custom-call(s32[3]{0:T(128)} %pad_add_fusion.2.after_ref.place_ref, bf16[288,1076]{1,0:T(8,128)(2,1)} %add_reduce_fusion.after_ref, bf16[384,1152]{1,0:T(8,128)(2,1)} %copy-done.6, ...), custom_call_target="tpu_custom_call" | custom-call | tf_op jit(solution)/shard_map/attend_back/pallas_call | solution.py:418
  265.6 5.5 %first_back.1 = (bf16[4,160,768]{2,1,0:T(8,128)(2,1)}, bf16[4,160,768]{2,1,0:T(8,128)(2,1)}, f32[1152,2]{1,0:T(8,128)}) custom-call(s32[1]{0:T(128)} %bitcast.core_ref, bf16[1152,432]{1,0:T(8,128)(2,1)} %get-tuple-element.74.w_ref, bf16[432,768]{1,0:T(8,128)(2,1)} %get-tuple-element.78.grad_ref, bf16[1152,768]{1,0:T(8,128)(2,1)} %bitcast.56, ...), custom_call_target="tpu_custom_call" | custom-call | tf_op jit(solution)/shard_map/first_back/pallas_call | solution.py:463
  271.6 21.2 %all_to_all.30.blocks_ref = bf16[4,72,1076]{2,1,0:T(8,128)(2,1)S(1)} all-to-all(bf16[4,72,1076]{2,1,0:T(8,128)(2,1)S(1)} %bitcast.66), channel_id=1, replica_groups=mesh['dp'=4,'row'=4,'col'=2] {'row'}, dimensions={0} | all-to-all | bytes 1239552 | tf_op jit(solution)/shard_map/all_to_all | solution.py:65
  297.0 4.5 %all-to-all-start.4 = ((bf16[4,288,576]{2,1,0:T(8,128)(2,1)}), bf16[4,288,576]{2,1,0:T(8,128)(2,1)}, u32[]{:S(2)}, u32[]{:S(2)}) async-start(bf16[4,288,576]{2,1,0:T(8,128)(2,1)} %get-tuple-element.82), calls=%async_computation.8 | async-start | bytes 2949120 | tf_op jit(solution)/shard_map/all_to_all | solution.py:69
  303.6 17.0 %reduce-scatter.9.cloned.1.call-done = bf16[160,768]{1,0:T(8,128)(2,1)} async-done(((bf16[640,768]{1,0:T(8,128)(2,1)}), bf16[160,768]{1,0:T(8,128)(2,1)}) %reduce-scatter.9.cloned.1.call-update) | async-done | bytes 245776 | tf_op jit(solution)/shard_map/reduce_scatter | solution.py:74
  325.1 4.1 %all-to-all-start.5 = ((bf16[4,72,576]{2,1,0:T(8,128)(2,1)}), bf16[4,72,576]{2,1,0:T(8,128)(2,1)}, u32[]{:S(2)}, u32[]{:S(2)}) async-start(bf16[4,72,576]{2,1,0:T(8,128)(2,1)} %bitcast.30), calls=%async_computation.9 | async-start | bytes 737280 | tf_op jit(solution)/shard_map/all_to_all | solution.py:65
  334.2 7.2 %adam.3 = (f32[72,1,2152]{2,1,0:T(1,128)}, f32[72,1,2152]{2,1,0:T(1,128)}, f32[72,1,2152]{2,1,0:T(1,128)}, f32[72,1,2152]{2,1,0:T(1,128)}, f32[72,1,2152]{2,1,0:T(1,128)}, /*index=5*/f32[72,1,2152]{2,1,0:T(1,128)}) custom-call(bf16[4,160,768]{2,1,0:T(8,128)(2,1)} %add_convert_fusion.1.after_ref, bf16[4,72,1076]{2,1,0:T(8,128)(2,1)} %copy-done.7, ...), custom_call_target="tpu_custom_call" | custom-call | tf_op jit(solution)/shard_map/adam/pallas_call | solution.py:138
  341.4 4.7 %adam.2 = (f32[72,1,1728]{2,1,0:T(1,128)}, f32[72,1,1728]{2,1,0:T(1,128)}, f32[72,1,1728]{2,1,0:T(1,128)}, f32[72,1,576]{2,1,0:T(1,128)}, f32[72,1,576]{2,1,0:T(1,128)}, /*index=5*/f32[72,1,576]{2,1,0:T(1,128)}) custom-call(bf16[4,160,768]{2,1,0:T(8,128)(2,1)} %add_convert_fusion.1.after_ref, bf16[4,72,576]{2,1,0:T(8,128)(2,1)} %all-to-all-done.5.blocks_ref, ...), custom_call_target="tpu_custom_call" | custom-call | tf_op jit(solution)/shard_map/adam/pallas_call | solution.py:138
  355.2 2.9 collective-permute-done.15
  366.0 8.7 %reduce-scatter.11.cloned.1.call-done = bf16[144,768]{1,0:T(8,128)(2,1)} async-done(((bf16[576,768]{1,0:T(8,128)(2,1)}), bf16[144,768]{1,0:T(8,128)(2,1)}) %reduce-scatter.11.cloned.1.call-update) | async-done | bytes 221200 | tf_op jit(solution)/shard_map/reduce_scatter | solution.py:74
  (244 shorter events, 80.4 us)
Async XLA Ops:
  11.2 17.6 %all-to-all-start = ((bf16[4,72,576]{2,1,0:T(8,128)(2,1)}), bf16[4,72,576]{2,1,0:T(8,128)(2,1)S(1)}, u32[]{:S(2)}, u32[]{:S(2)}) async-start(bf16[4,72,576]{2,1,0:T(8,128)(2,1)} %prepare.2), calls=%async_computation | async-start | bytes 737280 | tf_op jit(solution)/shard_map/all_to_all | solution.py:65
  18.2 60.4 %copy-start = (bf16[1152,1152]{1,0:T(8,128)(2,1)}, bf16[1152,1152]{1,0:T(8,128)(2,1)S(1)}, u32[]{:S(2)}) copy-start(bf16[1152,1152]{1,0:T(8,128)(2,1)S(1)} %fusion.order_ref) | copy-start | bytes 7962628
  28.8 20.5 %copy-start.10 = (bf16[4,72,576]{2,1,0:T(8,128)(2,1)}, bf16[4,72,576]{2,1,0:T(8,128)(2,1)S(1)}, u32[]{:S(2)}) copy-start(bf16[4,72,576]{2,1,0:T(8,128)(2,1)S(1)} %all-to-all-done) | copy-start | bytes 995332
  52.8 18.1 %all-to-all-start.1 = ((bf16[4,72,1076]{2,1,0:T(8,128)(2,1)}), bf16[4,72,1076]{2,1,0:T(8,128)(2,1)}, u32[]{:S(2)}, u32[]{:S(2)}) async-start(bf16[4,72,1076]{2,1,0:T(8,128)(2,1)} %prepare.3), calls=%async_computation.1 | async-start | bytes 1327104 | tf_op jit(solution)/shard_map/all_to_all | solution.py:65
  57.0 52.3 %all-gather.5.cloned.1.call-start = ((), (), s32[]{:S(2)}) async-start(), calls=%async_computation.14 | async-start | bytes 1990656 | tf_op jit(solution)/shard_map/all_gather | solution.py:556
  63.6 19.0 %collective-permute-start = (bf16[288,576]{1,0:T(8,128)(2,1)}, bf16[288,576]{1,0:T(8,128)(2,1)}, u32[]{:S(2)}, u32[]{:S(2)}) collective-permute-start(bf16[288,576]{1,0:T(8,128)(2,1)} %bitcast.72), channel_id=1, source_target_pairs={{0,8},{8,0},{16,24},{24,16},{1,9},{9,1},{17,25},{25,17},{2,10},{10... | collective-permute-start | bytes 995336 | tf_op jit(solution)/shard_map/ppermute | solution.py:55
  65.1 17.5 %collective-permute-start.1 = (bf16[288,576]{1,0:T(8,128)(2,1)}, bf16[288,576]{1,0:T(8,128)(2,1)}, u32[]{:S(2)}, u32[]{:S(2)}) collective-permute-start(bf16[288,576]{1,0:T(8,128)(2,1)} %bitcast.73), channel_id=1, source_target_pairs={{0,16},{8,24},{16,0},{24,8},{1,17},{9,25},{17,1},{25,9},{2,18},{10... | collective-permute-start | bytes 995336 | tf_op jit(solution)/shard_map/ppermute | solution.py:55
  66.6 16.0 %collective-permute-start.2 = (bf16[288,576]{1,0:T(8,128)(2,1)}, bf16[288,576]{1,0:T(8,128)(2,1)}, u32[]{:S(2)}, u32[]{:S(2)}) collective-permute-start(bf16[288,576]{1,0:T(8,128)(2,1)} %bitcast.74), channel_id=1, source_target_pairs={{0,24},{8,16},{16,8},{24,0},{1,25},{9,17},{17,9},{25,1},{2,26},{10... | collective-permute-start | bytes 995336 | tf_op jit(solution)/shard_map/ppermute | solution.py:55
  74.5 47.9 %reduce-scatter.5.cloned.1.call-start = ((), (), s32[]{:S(2)}) async-start(), calls=%async_computation.10 | async-start | bytes 1105920 | tf_op jit(solution)/shard_map/reduce_scatter | solution.py:74
  91.8 2.7 collective-permute-start.3
  96.8 128.5 %reduce-scatter.7.cloned.1.call-start = ((), (), s32[]{:S(2)}) async-start(), calls=%async_computation.11 | async-start | bytes 1105920 | tf_op jit(solution)/shard_map/reduce_scatter | solution.py:74
  142.7 33.1 %copy-start.5 = (bf16[384,1152]{1,0:T(8,128)(2,1)}, bf16[384,1152]{1,0:T(8,128)(2,1)S(1)}, u32[]{:S(2)}) copy-start(bf16[384,1152]{1,0:T(8,128)(2,1)S(1)} %all_gather.34.near_ref) | copy-start | bytes 2654212
  142.7 33.1 %collective-permute-start.4 = (bf16[384,1152]{1,0:T(8,128)(2,1)S(1)}, bf16[384,1152]{1,0:T(8,128)(2,1)S(1)}, u32[]{:S(2)}, u32[]{:S(2)}) collective-permute-start(bf16[384,1152]{1,0:T(8,128)(2,1)S(1)} %all_gather.34.near_ref), channel_id=1, source_target_pairs={{0,1},{1,0},{2,3},{3,2},{4,5},{5,4},{6,7},{7,6},{8,9},{9,8},{10,11... | collective-permute-start | bytes 2654216 | tf_op jit(solution)/shard_map/ppermute | solution.py:39
  142.7 17.9 %collective-permute-start.5 = (bf16[288,1076]{1,0:T(8,128)(2,1)}, bf16[288,1076]{1,0:T(8,128)(2,1)S(1)}, u32[]{:S(2)}, u32[]{:S(2)}) collective-permute-start(bf16[288,1076]{1,0:T(8,128)(2,1)} %bitcast.8.after_ref.refs_0_), channel_id=1, source_target_pairs={{0,8},{8,0},{16,24},{24,16},{1,9},{9,1},{17,25},{25,17},{2,10},{10... | collective-permute-start | bytes 1859336 | tf_op jit(solution)/shard_map/ppermute | solution.py:55
  144.2 31.6 %collective-permute-start.6 = (bf16[288,1076]{1,0:T(8,128)(2,1)}, bf16[288,1076]{1,0:T(8,128)(2,1)}, u32[]{:S(2)}, u32[]{:S(2)}) collective-permute-start(bf16[288,1076]{1,0:T(8,128)(2,1)} %bitcast.8.after_ref.refs_0_), channel_id=1, source_target_pairs={{0,16},{8,24},{16,0},{24,8},{1,17},{9,25},{17,1},{25,9},{2,18},{10... | collective-permute-start | bytes 1859336 | tf_op jit(solution)/shard_map/ppermute | solution.py:55
  145.6 30.1 %collective-permute-start.7 = (bf16[288,1076]{1,0:T(8,128)(2,1)}, bf16[288,1076]{1,0:T(8,128)(2,1)}, u32[]{:S(2)}, u32[]{:S(2)}) collective-permute-start(bf16[288,1076]{1,0:T(8,128)(2,1)} %bitcast.8.after_ref.refs_0_), channel_id=1, source_target_pairs={{0,24},{8,16},{16,8},{24,0},{1,25},{9,17},{17,9},{25,1},{2,26},{10... | collective-permute-start | bytes 1859336 | tf_op jit(solution)/shard_map/ppermute | solution.py:55
  196.6 2.7 collective-permute-start.8
  213.4 38.1 %all-to-all-start.2 = ((bf16[4,288,1076]{2,1,0:T(8,128)(2,1)}), bf16[4,288,1076]{2,1,0:T(8,128)(2,1)}, u32[]{:S(2)}, u32[]{:S(2)}) async-start(bf16[4,288,1076]{2,1,0:T(8,128)(2,1)} %get-tuple-element.75), calls=%async_computation.3 | async-start | bytes 5308416 | tf_op jit(solution)/shard_map/all_to_all | solution.py:69
  218.0 102.7 %reduce-scatter.9.cloned.1.call-start = ((), (), s32[]{:S(2)}) async-start(), calls=%async_computation.12 | async-start | bytes 1228800 | tf_op jit(solution)/shard_map/reduce_scatter | solution.py:74
  248.1 6.8 %collective-permute-start.10 = (bf16[384,1152]{1,0:T(8,128)(2,1)S(1)}, bf16[384,1152]{1,0:T(8,128)(2,1)}, u32[]{:S(2)}, u32[]{:S(2)}) collective-permute-start(bf16[384,1152]{1,0:T(8,128)(2,1)S(1)} %all_gather.35.near_ref), channel_id=1, source_target_pairs={{0,1},{1,0},{2,3},{3,2},{4,5},{5,4},{6,7},{7,6},{8,9},{9,8},{10,11... | collective-permute-start | bytes 2654216 | tf_op jit(solution)/shard_map/ppermute | solution.py:39
  271.2 22.8 %copy-start.11 = (bf16[4,160,768]{2,1,0:T(8,128)(2,1)S(1)}, bf16[4,160,768]{2,1,0:T(8,128)(2,1)}, u32[]{:S(2)}) copy-start(bf16[4,160,768]{2,1,0:T(8,128)(2,1)} %get-tuple-element.79) | copy-start | bytes 2949124
  271.2 22.8 %collective-permute-start.11 = (bf16[4,160,768]{2,1,0:T(8,128)(2,1)}, bf16[4,160,768]{2,1,0:T(8,128)(2,1)S(1)}, u32[]{:S(2)}, u32[]{:S(2)}) collective-permute-start(bf16[4,160,768]{2,1,0:T(8,128)(2,1)} %get-tuple-element.80), channel_id=1, source_target_pairs={{0,1},{1,0},{2,3},{3,2},{4,5},{5,4},{6,7},{7,6},{8,9},{9,8},{10,11... | collective-permute-start | bytes 2949128 | tf_op jit(solution)/shard_map/ppermute | solution.py:39
  296.8 52.8 %collective-permute-start.9 = (bf16[576,768]{1,0:T(8,128)(2,1)}, bf16[576,768]{1,0:T(8,128)(2,1)}, u32[]{:S(2)}, u32[]{:S(2)}) collective-permute-start(bf16[576,768]{1,0:T(8,128)(2,1)} %get-tuple-element.73), channel_id=1, source_target_pairs={{0,1},{1,0},{2,3},{3,2},{4,5},{5,4},{6,7},{7,6},{8,9},{9,8},{10,11... | collective-permute-start | bytes 2654216 | tf_op jit(solution)/shard_map/ppermute | solution.py:39
  297.0 25.6 %copy-start.15 = (bf16[729,144]{0,1:T(8,128)(2,1)S(1)}, bf16[729,144]{0,1:T(8,128)(2,1)}, u32[]{:S(2)}) copy-start(bf16[729,144]{0,1:T(8,128)(2,1)} %param.20) | copy-start | bytes 629860
  297.0 25.7 %all-to-all-start.4 = ((bf16[4,288,576]{2,1,0:T(8,128)(2,1)}), bf16[4,288,576]{2,1,0:T(8,128)(2,1)}, u32[]{:S(2)}, u32[]{:S(2)}) async-start(bf16[4,288,576]{2,1,0:T(8,128)(2,1)} %get-tuple-element.82), calls=%async_computation.8 | async-start | bytes 2949120 | tf_op jit(solution)/shard_map/all_to_all | solution.py:69
  322.5 6.9 %collective-permute-start.12 = (f32[16,1152]{1,0:T(8,128)S(1)}, f32[16,1152]{1,0:T(8,128)S(1)}, u32[]{:S(2)}, u32[]{:S(2)}) collective-permute-start(f32[16,1152]{1,0:T(8,128)S(1)} %fusion.27), channel_id=1, source_target_pairs={{0,1},{1,0},{2,3},{3,2},{4,5},{5,4},{6,7},{7,6},{8,9},{9,8},{10,11... | collective-permute-start | bytes 221192 | tf_op jit(solution)/shard_map/ppermute | solution.py:86
  325.1 16.3 %all-to-all-start.5 = ((bf16[4,72,576]{2,1,0:T(8,128)(2,1)}), bf16[4,72,576]{2,1,0:T(8,128)(2,1)}, u32[]{:S(2)}, u32[]{:S(2)}) async-start(bf16[4,72,576]{2,1,0:T(8,128)(2,1)} %bitcast.30), calls=%async_computation.9 | async-start | bytes 737280 | tf_op jit(solution)/shard_map/all_to_all | solution.py:65
  329.2 45.5 %reduce-scatter.11.cloned.1.call-start = ((), (), s32[]{:S(2)}) async-start(), calls=%async_computation.13 | async-start | bytes 1105920 | tf_op jit(solution)/shard_map/reduce_scatter | solution.py:74
  330.1 16.0 %collective-permute-start.13 = (f32[16,1152]{1,0:T(8,128)}, f32[16,1152]{1,0:T(8,128)}, u32[]{:S(2)}, u32[]{:S(2)}) collective-permute-start(f32[16,1152]{1,0:T(8,128)} %fusion.66), channel_id=1, source_target_pairs={{0,2},{2,0},{4,6},{6,4},{1,3},{3,1},{5,7},{7,5},{8,10},{10,8},{12,... | collective-permute-start | bytes 221192 | tf_op jit(solution)/shard_map/ppermute | solution.py:86
  347.1 6.5 %collective-permute-start.14 = (f32[16,1152]{1,0:T(8,128)S(1)}, f32[16,1152]{1,0:T(8,128)S(1)}, u32[]{:S(2)}, u32[]{:S(2)}) collective-permute-start(f32[16,1152]{1,0:T(8,128)S(1)} %add.330), channel_id=1, source_target_pairs={{0,4},{2,6},{4,0},{6,2},{1,5},{3,7},{5,1},{7,3},{8,12},{10,14},{12... | collective-permute-start | bytes 221192 | tf_op jit(solution)/shard_map/ppermute | solution.py:86
  353.6 4.4 %collective-permute-start.15 = (f32[16,1152]{1,0:T(8,128)S(1)}, f32[16,1152]{1,0:T(8,128)S(1)}, u32[]{:S(2)}, u32[]{:S(2)}) collective-permute-start(f32[16,1152]{1,0:T(8,128)S(1)} %add.331), channel_id=1, source_target_pairs={{0,8},{8,0},{16,24},{24,16},{1,9},{9,1},{17,25},{25,17},{2,10},{10... | collective-permute-start | bytes 221192 | tf_op jit(solution)/shard_map/ppermute | solution.py:86
  358.1 4.4 %collective-permute-start.16 = (f32[16,1152]{1,0:T(8,128)S(1)}, f32[16,1152]{1,0:T(8,128)S(1)}, u32[]{:S(2)}, u32[]{:S(2)}) collective-permute-start(f32[16,1152]{1,0:T(8,128)S(1)} %add.332), channel_id=1, source_target_pairs={{0,16},{8,24},{16,0},{24,8},{1,17},{9,25},{17,1},{25,9},{2,18},{10... | collective-permute-start | bytes 221192 | tf_op jit(solution)/shard_map/ppermute | solution.py:86
  (33 other events, 279.8 us)
Sparse Core Ops, SparseCore 0:
  74.6 27.1 all-gather.4
Sparse Core Ops, SparseCore 1:
  96.9 25.3 reduce-scatter.4
  201.8 23.5 reduce-scatter.6
  295.4 25.2 reduce-scatter.8
  352.0 22.7 reduce-scatter.10

commit v5 on v4

--- a/solution.py
+++ b/solution.py
@@ -584,7 +584,8 @@
     )
     cot_mine = take(cot_tokens, own, chunk).astype(jnp.float32)
 
-    middle = x_mine + branch + out_bias[None, :]
+    flown = sum(zero_of(part) for part in rest_parts[1:]) if len(rest_parts) > 1 else 0.0
+    middle = x_mine + branch + (out_bias + flown)[None, :]
     center = middle - jnp.sum(middle, axis=1, keepdims=True) / D
     inverse_two = lax.rsqrt(jnp.sum(center * center, axis=1, keepdims=True) / D + NORM_EPS)
     normed_two = center * inverse_two
@@ -617,14 +618,13 @@
     rest_rows = sum_blocks(rest_grad, "dp", zero_of(branch_rows))
     rest_blocks = returned(rest_rows)
     branch_all, qkv_grad, bias_sums, first_grad = attend_back(
-        place, rest_rows, branch_rows, swap_cores(branch_rows), w_first, qkv, za, attended, n_dp
+        place, branch_rows, branch_rows, swap_cores(branch_rows), w_first, qkv, za, attended, n_dp
     )
     branch_all = branch_all.reshape(padded, D)
     theirs, mine, one_sums = first_back(
         core_of, qkv_mixed, qkv_grad, x_all, x_mean, inverse_one, gain_one[:, None], width, n_row
     )
-    pair = mine.astype(jnp.float32) + zero_of(rest_blocks)
-    pair = (pair + swap_cores(theirs).astype(jnp.float32)).astype(LOW)
+    pair = (mine.astype(jnp.float32) + swap_cores(theirs).astype(jnp.float32)).astype(LOW)
     one_grad = sum_over_rows(pair.reshape(-1, padded))
     later = zero_of(one_grad)
     result = sum_over_rows(result + later) + down_bias[:, None]

time: 389 us -> 412 us (1.059)
  blocking collectives: 83.7 us -> 62.1 us
  waiting for transfers between devices: 86.5 us -> 104 us
  local copies, waits for them, and re-layouts: 21.9 us -> 32.8 us
  other arithmetic: 30.8 us -> 38.5 us
  starting transfers between devices: 50.7 us -> 56.2 us
    all_to_all x1 -> x0, blocking collectives: 21.2 us -> none  [exchange_rows(): return lax.all_to_all(blocks, 'row', 0, 0)]
    all_to_all x2, waiting for transfers between devices: 0.01 us -> 12.4 us  [sum_blocks(): blocks = lax.all_to_all(blocks, axis, 0, 0)]
    another operation x7, local copies, waits for them, and re-layouts: 0.09 us -> 5.7 us  [shards(): jnp.stack([one_sums[:, 0], one_sums[:, 1], jnp.sum(two_grad * normed_two,...]
    all_to_all x3 -> x4, starting transfers between devices: 14.7 us -> 18.2 us  [exchange_rows(): return lax.all_to_all(blocks, 'row', 0, 0)]
    all_to_all x3 -> x4, waiting for transfers between devices: 9.72 us -> 13.1 us  [exchange_rows(): return lax.all_to_all(blocks, 'row', 0, 0)]
  transfers between devices with their start and end apart: 27 -> 28, of which waited for: 13 -> 17; matrix products, arithmetic and copies ran while one was open for 13% -> 16% of each run, Pallas kernels for 11% -> 14%
where the time goes in v5:
time: 412 us; the launch traced here: 407 us
  waiting for transfers between devices  104 us (25%)
  Pallas kernels  82.3 us (20%)
  blocking collectives  62.1 us (15%)
  starting transfers between devices  56.2 us (14%)
  other arithmetic  38.5 us (9%)
  local copies, waits for them, and re-layouts  32.8 us (8%)
  between operations  21.3 us (5%)
  matrix products  9.95 us (2%)
    reduce_scatter x4, waiting for transfers between devices, sum_over_rows(): lax.psum_scatter(half.astype(LOW), 'row', scatter_dimension=0, tiled=True)  36.6 us
    ppermute x6, waiting for transfers between devices, gather_parts(): lax.ppermute(block, axis, [(i, i ^ step) for i in range(size)])  27 us
    all_gather x1, blocking collectives, shards(): branch_rows = lax.all_gather(middle_grad, 'row', axis=0, tiled=True)  19.3 us
    all_gather x1, blocking collectives, shards(): x_rows = lax.all_gather(x_after, 'row', axis=0, tiled=True)  19.2 us
    all_gather x1, blocking collectives, shards(): zb_rows = lax.all_gather(zb, 'row', axis=0, tiled=True)  18.8 us
    all_to_all x4, starting transfers between devices, exchange_rows(): return lax.all_to_all(blocks, 'row', 0, 0)  18.2 us
    all_to_all x4, waiting for transfers between devices, exchange_rows(): return lax.all_to_all(blocks, 'row', 0, 0)  13.1 us
    reduce_scatter x4, starting transfers between devices, sum_over_rows(): lax.psum_scatter(half.astype(LOW), 'row', scatter_dimension=0, tiled=True)  12.4 us
  transfers between devices with their start and end apart: 28, of which 17 were waited for; matrix products, arithmetic and copies ran while one was open for 16% of the time, Pallas kernels for 14%

profile of v5, /device:TPU:0, one launch (start us, length us, event | category | flops | bytes accessed | tf_op | source)
XLA Modules:
  0.0 406.8 jit_solution(14109812689227174514)
XLA Ops:
  11.2 6.4 %all-to-all-start = ((bf16[4,72,576]{2,1,0:T(8,128)(2,1)}), bf16[4,72,576]{2,1,0:T(8,128)(2,1)}, u32[]{:S(2)}, u32[]{:S(2)}) async-start(bf16[4,72,576]{2,1,0:T(8,128)(2,1)} %prepare.2), calls=%async_computation | async-start | bytes 737280 | tf_op jit(solution)/shard_map/all_to_all | solution.py:65
  23.2 5.7 %all-to-all-done = bf16[4,72,576]{2,1,0:T(8,128)(2,1)} async-done(((bf16[4,72,576]{2,1,0:T(8,128)(2,1)}), bf16[4,72,576]{2,1,0:T(8,128)(2,1)}, u32[]{:S(2)}, u32[]{:S(2)}) %all-to-all-start) | async-done | bytes 331808 | tf_op jit(solution)/shard_map/all_to_all | solution.py:65
  30.8 19.2 %all_gather.27.after_ref = bf16[576,768]{1,0:T(8,128)(2,1)} all-gather(bf16[144,768]{1,0:T(8,128)(2,1)S(1)} %pad_add_fusion.1), channel_id=1, replica_groups=mesh['dp'=4,'row'=4,'col'=2] {'row'}, dimensions={0}, use_global_device_ids=true | all-gather | bytes 1105920 | tf_op jit(solution)/shard_map/all_gather | solution.py:549
  50.0 3.6 prepare.3
  53.6 4.2 %all-to-all-start.1 = ((bf16[4,72,1076]{2,1,0:T(8,128)(2,1)}), bf16[4,72,1076]{2,1,0:T(8,128)(2,1)}, u32[]{:S(2)}, u32[]{:S(2)}) async-start(bf16[4,72,1076]{2,1,0:T(8,128)(2,1)} %prepare.3), calls=%async_computation.1 | async-start | bytes 1327104 | tf_op jit(solution)/shard_map/all_to_all | solution.py:65
  82.2 11.5 %collective-permute-done.4.refs_1_ = bf16[288,1076]{1,0:T(8,128)(2,1)S(1)} collective-permute-done((bf16[288,1076]{1,0:T(8,128)(2,1)}, bf16[288,1076]{1,0:T(8,128)(2,1)S(1)}, u32[]{:S(2)}, u32[]{:S(2)}) %collective-permute-start.4) | collective-permute-done | bytes 619808 | tf_op jit(solution)/shard_map/ppermute | solution.py:55
  96.7 15.5 %collective-permute-done.5.refs_2_ = bf16[288,1076]{1,0:T(8,128)(2,1)S(1)} collective-permute-done((bf16[288,1076]{1,0:T(8,128)(2,1)}, bf16[288,1076]{1,0:T(8,128)(2,1)S(1)}, u32[]{:S(2)}, u32[]{:S(2)}) %collective-permute-start.5) | collective-permute-done | bytes 619808 | tf_op jit(solution)/shard_map/ppermute | solution.py:55
  117.1 5.5 %fusion.3.za_ref = bf16[1152,768]{1,0:T(8,128)(2,1)} fusion(bf16[1152,1152]{1,0:T(8,128)(2,1)S(1)} %fusion.order_ref, bf16[1152,768]{1,0:T(8,128)(2,1)} %bitcast.54, f32[1152]{0:T(1024)S(1)} %add.312, f32[1152]{0:T(1024)} %mul.271, f32[768]{0:T(1024)S(1)} %add_rsqrt_fusion, f32[768]{0:T(1024)S(1)} %broadcast_multiply_fusion), kind=kOutput, calls=%fused_computation.9 | convolution fusion | flops 2043740160 | bytes 6208512 | tf_op jit(solution)/shard_map/dot_general | solution.py:24
  123.3 8.9 %attend.1 = (bf16[1152,576]{1,0:T(8,128)(2,1)}, bf16[2,3,72,768]{3,2,1,0:T(8,128)(2,1)}, bf16[768,144]{1,0:T(8,128)(2,1)}, bf16[384,1152]{1,0:T(8,128)(2,1)}, bf16[384,1152]{1,0:T(8,128)(2,1)}) custom-call(s32[3]{0:T(128)} %pad_add_fusion.2.after_ref.place_ref, bf16[288,1076]{1,0:T(8,128)(2,1)} %bitcast.8.after_ref.refs_0_, bf16[1152,768]{1,0:T(8,128)(2,1)} %fusion.3.za_ref, ...), custom_call_target="tpu_custom_call" | custom-call | tf_op jit(solution)/shard_map/attend/pallas_call | solution.py:207
  137.3 11.3 %reduce-scatter.7.cloned.1.call-start = ((), (), s32[]{:S(2)}) async-start(), calls=%async_computation.11 | async-start | bytes 1105920 | tf_op jit(solution)/shard_map/reduce_scatter | solution.py:74
  149.7 9.2 %beside.1 = (bf16[768,1152]{1,0:T(8,128)(2,1)}, bf16[1152,432]{1,0:T(8,128)(2,1)}, f32[96,1152]{1,0:T(8,128)}) custom-call(s32[3]{0:T(128)} %pad_add_fusion.2.after_ref.place_ref, bf16[384,1152]{1,0:T(8,128)(2,1)} %add_convert_fusion.5.after_ref, bf16[1152,1152]{1,0:T(8,128)(2,1)} %copy-done, bf16[8,144,768]{2,1,0:T(8,128)(2,1)} %bitcast.68, ...), custom_call_target="tpu_custom_call" | custom-call | tf_op jit(solution)/shard_map/beside/pallas_call | solution.py:243
  158.9 3.5 reduce-scatter.5.cloned.1.call-done
  164.0 18.8 %all_gather.34.near_ref = bf16[384,1152]{1,0:T(8,128)(2,1)S(1)} all-gather(bf16[96,1152]{1,0:T(8,128)(2,1)S(1)} %add_convert_fusion.7), channel_id=1, replica_groups=mesh['dp'=4,'row'=4,'col'=2] {'row'}, dimensions={0}, use_global_device_ids=true | all-gather | bytes 1105920 | tf_op jit(solution)/shard_map/all_gather | solution.py:593
  186.1 10.4 %before.1 = (bf16[2,384,1152]{2,1,0:T(8,128)(2,1)}, bf16[1152,538]{1,0:T(8,128)(2,1)}, f32[768,538]{1,0:T(8,128)}, bf16[1152,538]{1,0:T(8,128)(2,1)}) custom-call(s32[3]{0:T(128)} %pad_add_fusion.2.after_ref.place_ref, bf16[384,1152]{1,0:T(8,128)(2,1)} %copy-done.5, bf16[384,1152]{1,0:T(8,128)(2,1)} %copy-done.11, bf16[1152,1152]{1,0:T(8,128)(2,1)} %copy-done, ...), custom_call_target="tpu_custom_call" | custom-call | tf_op jit(solution)/shard_map/before/pallas_call | solution.py:270
  196.5 9.4 %mlp.1 = (bf16[768,538]{1,0:T(8,128)(2,1)}, bf16[768,538]{1,0:T(8,128)(2,1)}, bf16[384,1152]{1,0:T(8,128)(2,1)}, bf16[384,1152]{1,0:T(8,128)(2,1)}, f32[1,538]{1,0:T(1,128)}) custom-call(s32[1]{0:T(128)} %bitcast.core_ref, bf16[768,1152]{1,0:T(8,128)(2,1)} %bitcast.64, bf16[1152,538]{1,0:T(8,128)(2,1)} %get-tuple-element.65.up_ref, ...), custom_call_target="tpu_custom_call" | custom-call | tf_op jit(solution)/shard_map/mlp/pallas_call | solution.py:357
  211.0 24.5 %reduce-scatter.7.cloned.1.call-done = bf16[96,1152]{1,0:T(8,128)(2,1)} async-done(((bf16[384,1152]{1,0:T(8,128)(2,1)}), bf16[96,1152]{1,0:T(8,128)(2,1)}) %reduce-scatter.7.cloned.1.call-update) | async-done | bytes 221200 | tf_op jit(solution)/shard_map/reduce_scatter | solution.py:74
  238.1 19.3 %all_gather.35.after_ref.near_ref = bf16[384,1152]{1,0:T(8,128)(2,1)} all-gather(bf16[96,1152]{1,0:T(8,128)(2,1)S(1)} %get-tuple-element.117), channel_id=1, replica_groups=mesh['dp'=4,'row'=4,'col'=2] {'row'}, dimensions={0}, use_global_device_ids=true | all-gather | bytes 1105920 | tf_op jit(solution)/shard_map/all_gather | solution.py:617
  259.0 10.0 %behind.1 = (bf16[4,288,1076]{2,1,0:T(8,128)(2,1)}, bf16[576,768]{1,0:T(8,128)(2,1)}, bf16[576,768]{1,0:T(8,128)(2,1)}) custom-call(s32[3]{0:T(128)} %pad_add_fusion.2.after_ref.place_ref, bf16[384,1152]{1,0:T(8,128)(2,1)} %add_convert_fusion.4.after_ref, bf16[768,1152]{1,0:T(8,128)(2,1)} %bitcast.65, bf16[768,538]{1,0:T(8,128)(2,1)} %get-tuple-element.69.hid_ref, ...), custom_call_target="tpu_custom_call" | custom-call | tf_op jit(solution)/shard_map/behind/pallas_call | solution.py:303
  269.0 4.6 %all-to-all-start.4 = ((bf16[4,288,1076]{2,1,0:T(8,128)(2,1)}), bf16[4,288,1076]{2,1,0:T(8,128)(2,1)}, u32[]{:S(2)}, u32[]{:S(2)}) async-start(bf16[4,288,1076]{2,1,0:T(8,128)(2,1)} %get-tuple-element.88), calls=%async_computation.8 | async-start | bytes 5308416 | tf_op jit(solution)/shard_map/all_to_all | solution.py:69
  276.2 10.8 %attend_back.1 = (bf16[2,384,1152]{2,1,0:T(8,128)(2,1)}, bf16[432,768]{1,0:T(8,128)(2,1)}, f32[432,1]{1,0:T(8,128)}, bf16[4,288,576]{2,1,0:T(8,128)(2,1)}) custom-call(s32[3]{0:T(128)} %pad_add_fusion.2.after_ref.place_ref, bf16[384,1152]{1,0:T(8,128)(2,1)} %all_gather.35.after_ref.near_ref, bf16[384,1152]{1,0:T(8,128)(2,1)} %all_gather.35.after_ref.near_ref, ...), custom_call_target="tpu_custom_call" | custom-call | tf_op jit(solution)/shard_map/attend_back/pallas_call | solution.py:418
  287.0 5.5 %first_back.1 = (bf16[4,160,768]{2,1,0:T(8,128)(2,1)}, bf16[4,160,768]{2,1,0:T(8,128)(2,1)}, f32[1152,2]{1,0:T(8,128)}) custom-call(s32[1]{0:T(128)} %bitcast.core_ref, bf16[1152,432]{1,0:T(8,128)(2,1)} %get-tuple-element.74.w_ref, bf16[432,768]{1,0:T(8,128)(2,1)} %get-tuple-element.77.grad_ref, bf16[1152,768]{1,0:T(8,128)(2,1)} %bitcast.56, ...), custom_call_target="tpu_custom_call" | custom-call | tf_op jit(solution)/shard_map/first_back/pallas_call | solution.py:463
  297.8 7.6 %all-to-all-done.4 = bf16[4,288,1076]{2,1,0:T(8,128)(2,1)} async-done(((bf16[4,288,1076]{2,1,0:T(8,128)(2,1)}), bf16[4,288,1076]{2,1,0:T(8,128)(2,1)}, u32[]{:S(2)}, u32[]{:S(2)}) %all-to-all-start.4) | async-done | bytes 2479136 | tf_op jit(solution)/shard_map/all_to_all | solution.py:69
  305.4 4.3 %all-to-all-start.2 = ((bf16[4,288,576]{2,1,0:T(8,128)(2,1)}), bf16[4,288,576]{2,1,0:T(8,128)(2,1)}, u32[]{:S(2)}, u32[]{:S(2)}) async-start(bf16[4,288,576]{2,1,0:T(8,128)(2,1)} %get-tuple-element.81), calls=%async_computation.6 | async-start | bytes 2949120 | tf_op jit(solution)/shard_map/all_to_all | solution.py:69
  316.4 3.4 add_reduce_fusion
  323.4 4.7 %all-to-all-done.2 = bf16[4,288,576]{2,1,0:T(8,128)(2,1)} async-done(((bf16[4,288,576]{2,1,0:T(8,128)(2,1)}), bf16[4,288,576]{2,1,0:T(8,128)(2,1)}, u32[]{:S(2)}, u32[]{:S(2)}) %all-to-all-start.2) | async-done | bytes 1327136 | tf_op jit(solution)/shard_map/all_to_all | solution.py:69
  328.2 3.5 all-to-all-start.5
  344.3 4.3 %all-to-all-done.5.blocks_ref = bf16[4,72,1076]{2,1,0:T(8,128)(2,1)S(1)} async-done(((bf16[4,72,1076]{2,1,0:T(8,128)(2,1)}), bf16[4,72,1076]{2,1,0:T(8,128)(2,1)S(1)}, u32[]{:S(2)}, u32[]{:S(2)}) %all-to-all-start.5) | async-done | bytes 619808 | tf_op jit(solution)/shard_map/all_to_all | solution.py:65
  348.6 4.1 %all-to-all-start.3 = ((bf16[4,72,576]{2,1,0:T(8,128)(2,1)}), bf16[4,72,576]{2,1,0:T(8,128)(2,1)}, u32[]{:S(2)}, u32[]{:S(2)}) async-start(bf16[4,72,576]{2,1,0:T(8,128)(2,1)} %bitcast.70), calls=%async_computation.7 | async-start | bytes 737280 | tf_op jit(solution)/shard_map/all_to_all | solution.py:65
  358.7 7.2 %adam.3 = (f32[72,1,2152]{2,1,0:T(1,128)}, f32[72,1,2152]{2,1,0:T(1,128)}, f32[72,1,2152]{2,1,0:T(1,128)}, f32[72,1,2152]{2,1,0:T(1,128)}, f32[72,1,2152]{2,1,0:T(1,128)}, /*index=5*/f32[72,1,2152]{2,1,0:T(1,128)}) custom-call(bf16[4,160,768]{2,1,0:T(8,128)(2,1)} %add_convert_fusion.1.after_ref, bf16[4,72,1076]{2,1,0:T(8,128)(2,1)} %copy-done.6, ...), custom_call_target="tpu_custom_call" | custom-call | tf_op jit(solution)/shard_map/adam/pallas_call | solution.py:138
  365.9 4.7 %adam.2 = (f32[72,1,1728]{2,1,0:T(1,128)}, f32[72,1,1728]{2,1,0:T(1,128)}, f32[72,1,1728]{2,1,0:T(1,128)}, f32[72,1,576]{2,1,0:T(1,128)}, f32[72,1,576]{2,1,0:T(1,128)}, /*index=5*/f32[72,1,576]{2,1,0:T(1,128)}) custom-call(bf16[4,160,768]{2,1,0:T(8,128)(2,1)} %add_convert_fusion.1.after_ref, bf16[4,72,576]{2,1,0:T(8,128)(2,1)} %all-to-all-done.3.blocks_ref, ...), custom_call_target="tpu_custom_call" | custom-call | tf_op jit(solution)/shard_map/adam/pallas_call | solution.py:138
  377.7 3.1 collective-permute-done.15
  388.8 8.5 %reduce-scatter.11.cloned.1.call-done = bf16[144,768]{1,0:T(8,128)(2,1)} async-done(((bf16[576,768]{1,0:T(8,128)(2,1)}), bf16[144,768]{1,0:T(8,128)(2,1)}) %reduce-scatter.11.cloned.1.call-update) | async-done | bytes 221200 | tf_op jit(solution)/shard_map/reduce_scatter | solution.py:74
  (239 shorter events, 112.4 us)
Async XLA Ops:
  11.2 17.7 %all-to-all-start = ((bf16[4,72,576]{2,1,0:T(8,128)(2,1)}), bf16[4,72,576]{2,1,0:T(8,128)(2,1)}, u32[]{:S(2)}, u32[]{:S(2)}) async-start(bf16[4,72,576]{2,1,0:T(8,128)(2,1)} %prepare.2), calls=%async_computation | async-start | bytes 737280 | tf_op jit(solution)/shard_map/all_to_all | solution.py:65
  18.2 98.9 %copy-start = (bf16[1152,1152]{1,0:T(8,128)(2,1)}, bf16[1152,1152]{1,0:T(8,128)(2,1)S(1)}, u32[]{:S(2)}) copy-start(bf16[1152,1152]{1,0:T(8,128)(2,1)S(1)} %fusion.order_ref) | copy-start | bytes 7962628
  53.6 18.1 %all-to-all-start.1 = ((bf16[4,72,1076]{2,1,0:T(8,128)(2,1)}), bf16[4,72,1076]{2,1,0:T(8,128)(2,1)}, u32[]{:S(2)}, u32[]{:S(2)}) async-start(bf16[4,72,1076]{2,1,0:T(8,128)(2,1)} %prepare.3), calls=%async_computation.1 | async-start | bytes 1327104 | tf_op jit(solution)/shard_map/all_to_all | solution.py:65
  57.7 91.9 %all-gather.5.cloned.1.call-start = ((), (), s32[]{:S(2)}) async-start(), calls=%async_computation.14 | async-start | bytes 1990656 | tf_op jit(solution)/shard_map/all_gather | solution.py:556
  59.4 63.2 %collective-permute-start = (bf16[288,576]{1,0:T(8,128)(2,1)}, bf16[288,576]{1,0:T(8,128)(2,1)}, u32[]{:S(2)}, u32[]{:S(2)}) collective-permute-start(bf16[288,576]{1,0:T(8,128)(2,1)} %bitcast.5.refs_0_), channel_id=1, source_target_pairs={{0,8},{8,0},{16,24},{24,16},{1,9},{9,1},{17,25},{25,17},{2,10},{10... | collective-permute-start | bytes 995336 | tf_op jit(solution)/shard_map/ppermute | solution.py:55
  60.9 61.7 %collective-permute-start.1 = (bf16[288,576]{1,0:T(8,128)(2,1)}, bf16[288,576]{1,0:T(8,128)(2,1)}, u32[]{:S(2)}, u32[]{:S(2)}) collective-permute-start(bf16[288,576]{1,0:T(8,128)(2,1)} %bitcast.5.refs_0_), channel_id=1, source_target_pairs={{0,16},{8,24},{16,0},{24,8},{1,17},{9,25},{17,1},{25,9},{2,18},{10... | collective-permute-start | bytes 995336 | tf_op jit(solution)/shard_map/ppermute | solution.py:55
  75.1 87.3 %reduce-scatter.5.cloned.1.call-start = ((), (), s32[]{:S(2)}) async-start(), calls=%async_computation.10 | async-start | bytes 1105920 | tf_op jit(solution)/shard_map/reduce_scatter | solution.py:74
  75.6 41.3 %copy-start.21 = (f32[11216]{0:T(1024)S(1)}, f32[11216]{0:T(1024)}, u32[]{:S(2)}) copy-start(f32[11216]{0:T(1024)} %param.37) | copy-start | bytes 134596
  75.6 18.1 %collective-permute-start.4 = (bf16[288,1076]{1,0:T(8,128)(2,1)}, bf16[288,1076]{1,0:T(8,128)(2,1)S(1)}, u32[]{:S(2)}, u32[]{:S(2)}) collective-permute-start(bf16[288,1076]{1,0:T(8,128)(2,1)} %bitcast.8.after_ref.refs_0_), channel_id=1, source_target_pairs={{0,8},{8,0},{16,24},{24,16},{1,9},{9,1},{17,25},{25,17},{2,10},{10... | collective-permute-start | bytes 1859336 | tf_op jit(solution)/shard_map/ppermute | solution.py:55
  77.1 35.0 %collective-permute-start.5 = (bf16[288,1076]{1,0:T(8,128)(2,1)}, bf16[288,1076]{1,0:T(8,128)(2,1)S(1)}, u32[]{:S(2)}, u32[]{:S(2)}) collective-permute-start(bf16[288,1076]{1,0:T(8,128)(2,1)} %bitcast.8.after_ref.refs_0_), channel_id=1, source_target_pairs={{0,16},{8,24},{16,0},{24,8},{1,17},{9,25},{17,1},{25,9},{2,18},{10... | collective-permute-start | bytes 1859336 | tf_op jit(solution)/shard_map/ppermute | solution.py:55
  78.7 36.2 %collective-permute-start.6 = (bf16[288,1076]{1,0:T(8,128)(2,1)}, bf16[288,1076]{1,0:T(8,128)(2,1)S(1)}, u32[]{:S(2)}, u32[]{:S(2)}) collective-permute-start(bf16[288,1076]{1,0:T(8,128)(2,1)} %bitcast.8.after_ref.refs_0_), channel_id=1, source_target_pairs={{0,24},{8,16},{16,8},{24,0},{1,25},{9,17},{17,9},{25,1},{2,26},{10... | collective-permute-start | bytes 1859336 | tf_op jit(solution)/shard_map/ppermute | solution.py:55
  93.7 28.9 %collective-permute-start.2 = (bf16[288,576]{1,0:T(8,128)(2,1)}, bf16[288,576]{1,0:T(8,128)(2,1)S(1)}, u32[]{:S(2)}, u32[]{:S(2)}) collective-permute-start(bf16[288,576]{1,0:T(8,128)(2,1)} %bitcast.5.refs_0_), channel_id=1, source_target_pairs={{0,24},{8,16},{16,8},{24,0},{1,25},{9,17},{17,9},{25,1},{2,26},{10... | collective-permute-start | bytes 995336 | tf_op jit(solution)/shard_map/ppermute | solution.py:55
  132.3 2.6 collective-permute-start.3
  137.3 98.2 %reduce-scatter.7.cloned.1.call-start = ((), (), s32[]{:S(2)}) async-start(), calls=%async_computation.11 | async-start | bytes 1105920 | tf_op jit(solution)/shard_map/reduce_scatter | solution.py:74
  182.8 2.4 collective-permute-start.7
  205.9 2.7 collective-permute-start.8
  210.9 46.5 %copy-start.1 = (bf16[1152,1152]{1,0:T(8,128)(2,1)S(1)}, bf16[1152,1152]{1,0:T(8,128)(2,1)}, u32[]{:S(2)}) copy-start(bf16[1152,1152]{1,0:T(8,128)(2,1)} %copy-done) | copy-start | bytes 7962628
  257.4 18.9 %collective-permute-start.10 = (bf16[384,1152]{1,0:T(8,128)(2,1)}, bf16[384,1152]{1,0:T(8,128)(2,1)}, u32[]{:S(2)}, u32[]{:S(2)}) collective-permute-start(bf16[384,1152]{1,0:T(8,128)(2,1)} %all_gather.35.after_ref.near_ref), channel_id=1, source_target_pairs={{0,1},{1,0},{2,3},{3,2},{4,5},{5,4},{6,7},{7,6},{8,9},{9,8},{10,11... | collective-permute-start | bytes 2654216 | tf_op jit(solution)/shard_map/ppermute | solution.py:39
  269.0 36.4 %all-to-all-start.4 = ((bf16[4,288,1076]{2,1,0:T(8,128)(2,1)}), bf16[4,288,1076]{2,1,0:T(8,128)(2,1)}, u32[]{:S(2)}, u32[]{:S(2)}) async-start(bf16[4,288,1076]{2,1,0:T(8,128)(2,1)} %get-tuple-element.88), calls=%async_computation.8 | async-start | bytes 5308416 | tf_op jit(solution)/shard_map/all_to_all | solution.py:69
  273.6 64.2 %reduce-scatter.9.cloned.1.call-start = ((), (), s32[]{:S(2)}) async-start(), calls=%async_computation.12 | async-start | bytes 1228800 | tf_op jit(solution)/shard_map/reduce_scatter | solution.py:74
  292.5 2.8 collective-permute-start.11
  305.4 22.7 %all-to-all-start.2 = ((bf16[4,288,576]{2,1,0:T(8,128)(2,1)}), bf16[4,288,576]{2,1,0:T(8,128)(2,1)}, u32[]{:S(2)}, u32[]{:S(2)}) async-start(bf16[4,288,576]{2,1,0:T(8,128)(2,1)} %get-tuple-element.81), calls=%async_computation.6 | async-start | bytes 2949120 | tf_op jit(solution)/shard_map/all_to_all | solution.py:69
  312.2 60.9 %collective-permute-start.9 = (bf16[576,768]{1,0:T(8,128)(2,1)}, bf16[576,768]{1,0:T(8,128)(2,1)}, u32[]{:S(2)}, u32[]{:S(2)}) collective-permute-start(bf16[576,768]{1,0:T(8,128)(2,1)} %get-tuple-element.73), channel_id=1, source_target_pairs={{0,1},{1,0},{2,3},{3,2},{4,5},{5,4},{6,7},{7,6},{8,9},{9,8},{10,11... | collective-permute-start | bytes 2654216 | tf_op jit(solution)/shard_map/ppermute | solution.py:39
  319.8 21.3 %copy-start.14 = (bf16[729,144]{0,1:T(8,128)(2,1)S(1)}, bf16[729,144]{0,1:T(8,128)(2,1)}, u32[]{:S(2)}) copy-start(bf16[729,144]{0,1:T(8,128)(2,1)} %param.20) | copy-start | bytes 629860
  328.2 20.4 %all-to-all-start.5 = ((bf16[4,72,1076]{2,1,0:T(8,128)(2,1)}), bf16[4,72,1076]{2,1,0:T(8,128)(2,1)S(1)}, u32[]{:S(2)}, u32[]{:S(2)}) async-start(bf16[4,72,1076]{2,1,0:T(8,128)(2,1)} %bitcast.35), calls=%async_computation.9 | async-start | bytes 1327104 | tf_op jit(solution)/shard_map/all_to_all | solution.py:65
  341.0 11.9 %collective-permute-start.12 = (f32[16,1152]{1,0:T(8,128)}, f32[16,1152]{1,0:T(8,128)}, u32[]{:S(2)}, u32[]{:S(2)}) collective-permute-start(f32[16,1152]{1,0:T(8,128)} %fusion.27), channel_id=1, source_target_pairs={{0,1},{1,0},{2,3},{3,2},{4,5},{5,4},{6,7},{7,6},{8,9},{9,8},{10,11... | collective-permute-start | bytes 221192 | tf_op jit(solution)/shard_map/ppermute | solution.py:86
  348.6 17.4 %all-to-all-start.3 = ((bf16[4,72,576]{2,1,0:T(8,128)(2,1)}), bf16[4,72,576]{2,1,0:T(8,128)(2,1)}, u32[]{:S(2)}, u32[]{:S(2)}) async-start(bf16[4,72,576]{2,1,0:T(8,128)(2,1)} %bitcast.70), calls=%async_computation.7 | async-start | bytes 737280 | tf_op jit(solution)/shard_map/all_to_all | solution.py:65
  352.7 44.6 %reduce-scatter.11.cloned.1.call-start = ((), (), s32[]{:S(2)}) async-start(), calls=%async_computation.13 | async-start | bytes 1105920 | tf_op jit(solution)/shard_map/reduce_scatter | solution.py:74
  353.8 16.8 %collective-permute-start.13 = (f32[16,1152]{1,0:T(8,128)S(1)}, f32[16,1152]{1,0:T(8,128)S(1)}, u32[]{:S(2)}, u32[]{:S(2)}) collective-permute-start(f32[16,1152]{1,0:T(8,128)S(1)} %fusion.66), channel_id=1, source_target_pairs={{0,2},{2,0},{4,6},{6,4},{1,3},{3,1},{5,7},{7,5},{8,10},{10,8},{12,... | collective-permute-start | bytes 221192 | tf_op jit(solution)/shard_map/ppermute | solution.py:86
  370.7 5.6 %collective-permute-start.14 = (f32[16,1152]{1,0:T(8,128)S(1)}, f32[16,1152]{1,0:T(8,128)S(1)}, u32[]{:S(2)}, u32[]{:S(2)}) collective-permute-start(f32[16,1152]{1,0:T(8,128)S(1)} %add.356), channel_id=1, source_target_pairs={{0,4},{2,6},{4,0},{6,2},{1,5},{3,7},{5,1},{7,3},{8,12},{10,14},{12... | collective-permute-start | bytes 221192 | tf_op jit(solution)/shard_map/ppermute | solution.py:86
  376.4 4.4 %collective-permute-start.15 = (f32[16,1152]{1,0:T(8,128)S(1)}, f32[16,1152]{1,0:T(8,128)S(1)}, u32[]{:S(2)}, u32[]{:S(2)}) collective-permute-start(f32[16,1152]{1,0:T(8,128)S(1)} %add.357), channel_id=1, source_target_pairs={{0,8},{8,0},{16,24},{24,16},{1,9},{9,1},{17,25},{25,17},{2,10},{10... | collective-permute-start | bytes 221192 | tf_op jit(solution)/shard_map/ppermute | solution.py:86
  380.8 4.4 %collective-permute-start.16 = (f32[16,1152]{1,0:T(8,128)S(1)}, f32[16,1152]{1,0:T(8,128)S(1)}, u32[]{:S(2)}, u32[]{:S(2)}) collective-permute-start(f32[16,1152]{1,0:T(8,128)S(1)} %add.358), channel_id=1, source_target_pairs={{0,16},{8,24},{16,0},{24,8},{1,17},{9,25},{17,1},{25,9},{2,18},{10... | collective-permute-start | bytes 221192 | tf_op jit(solution)/shard_map/ppermute | solution.py:86
  (30 other events, 256.7 us)
Sparse Core Ops, SparseCore 0:
  75.2 25.4 all-gather.4
Sparse Core Ops, SparseCore 1:
  137.4 25.0 reduce-scatter.4
  211.0 24.4 reduce-scatter.6
  297.9 25.9 reduce-scatter.8
  375.6 21.6 reduce-scatter.10

commit v6 on v0

--- a/solution.py
+++ b/solution.py
@@ -418,9 +418,12 @@
     )(branch_all, w_first, qkv, za, attended)
 
 
-def first_kernel(core_ref, w_ref, grad_ref, x_ref, mean_ref, inv_ref, gain_ref, theirs_ref, mine_ref, sum_ref):
-    n_row, rows, tokens = theirs_ref.shape
-    width = rows - 16
+def first_kernel(
+    core_ref, w_ref, grad_ref, x_ref, mean_ref, inv_ref, gain_ref, far_ref, near_ref, theirs_ref, mine_ref, sum_ref
+):
+    n_row, width, tokens = far_ref.shape
+    theirs_ref[:, width + 16 :] = far_ref[...]
+    mine_ref[:, width + 16 :] = near_ref[...]
     first = jnp.zeros((1, tokens), jnp.float32)
     second = jnp.zeros((1, tokens), jnp.float32)
     blocks = []
@@ -443,23 +446,23 @@
             def _(core=core, ref=ref):
                 for row in range(n_row):
                     ref[row, :width] = blocks[core * n_row + row]
-                    ref[row, width:] = sums
-
-
-def first_back(core, w_mixed, qkv_grad, x_all, x_mean, inverse, gain, width, n_row):
-    tokens = x_all.shape[1]
+                    ref[row, width : width + 16] = sums
+
+
+def first_back(core, w_mixed, qkv_grad, x_all, x_mean, inverse, gain, far, near):
+    n_row, width, tokens = far.shape
     return pl.pallas_call(
         first_kernel,
-        in_specs=[SMEM] + [VMEM] * 6,
+        in_specs=[SMEM] + [VMEM] * 8,
         out_specs=[VMEM] * 3,
         out_shape=(
-            jax.ShapeDtypeStruct((n_row, width + 16, tokens), LOW),
-            jax.ShapeDtypeStruct((n_row, width + 16, tokens), LOW),
+            jax.ShapeDtypeStruct((n_row, 2 * width + 16, tokens), LOW),
+            jax.ShapeDtypeStruct((n_row, 2 * width + 16, tokens), LOW),
             jax.ShapeDtypeStruct((D, 2), jnp.float32),
         ),
         compiler_params=BIG,
         name="first_back",
-    )(core, w_mixed, qkv_grad, x_all, x_mean, inverse, gain)
+    )(core, w_mixed, qkv_grad, x_all, x_mean, inverse, gain, far, near)
 
 
 def adam_update(weights, moment_one, second, gradient, step_rate, weight_decay):
@@ -589,30 +592,30 @@
     two_grad = sum_over_rows(pair)
 
     middle_mixed = dot(order, middle.astype(LOW), 1, 1, LOW)
-    rest_grad, theirs, mine = behind(
+    rest_grad, far, near = behind(
         place, pair, zb, hidden_grad, cot_tokens, active, down_mixed, middle_mixed, n_dp
     )
-    result = mine.astype(jnp.float32) + swap_cores(theirs).astype(jnp.float32)
 
     scaled = two_grad * gain_two
     first_sum = jnp.sum(scaled, axis=1, keepdims=True) / D
     second_sum = jnp.sum(scaled * normed_two, axis=1, keepdims=True) / D
-    middle_grad = cot_mine + inverse_two * (scaled - first_sum - normed_two * second_sum)
+    middle_grad = cot_mine + zero_of(far) + inverse_two * (scaled - first_sum - normed_two * second_sum)
     middle_grad = middle_grad.astype(LOW)
     branch_rows = lax.all_gather(middle_grad, "row", axis=0, tiled=True)
     later = zero_of(branch_rows)
-    result = sum_over_rows(result + later) + down_bias[:, None]
-    result = result.astype(LOW)[:, :tokens].T
     branch_all = both_cores(branch_rows)
 
     qkv_grad, bias_sums, first_grad = attend_back(
         branch_all, w_first, qkv, za, attended, n_dp
     )
     theirs, mine, one_sums = first_back(
-        core_of, qkv_mixed, qkv_grad, x_all, x_mean, inverse_one, gain_one[:, None], width, n_row
+        core_of, qkv_mixed, qkv_grad, x_all, x_mean, inverse_one, gain_one[:, None],
+        far.reshape(n_row, width, padded), near.reshape(n_row, width, padded),
     )
     pair = (mine.astype(jnp.float32) + swap_cores(theirs).astype(jnp.float32)).astype(LOW)
     one_grad = sum_over_rows(pair.reshape(-1, padded))
+    result = one_grad[width + 16 :] + down_bias[:, None]
+    result = result.astype(LOW)[:, :tokens].T
     first_rows = sum_blocks(first_grad, "dp", 0.0)
     rest_rows = sum_blocks(rest_grad, "dp", later)
 
@@ -661,10 +664,16 @@
         ]
     )
 
-    rest_new = adam(
+    first_new = adam(
         pair,
-        returned(rest_rows),
-        (0.03, 0.02),
+        returned(jnp.concatenate([first_rows, rest_rows], axis=1)),
+        (0.03, 0.12, 0.03, 0.02),
+        qkv_master,
+        qkv_first,
+        qkv_second,
+        flat(out_master),
+        flat(out_first),
+        flat(out_second),
         up_master,
         up_first,
         up_second,
@@ -672,17 +681,7 @@
         flat(down_first),
         flat(down_second),
     )
-    first_new = adam(
-        pair,
-        returned(first_rows),
-        (0.03, 0.12),
-        qkv_master,
-        qkv_first,
-        qkv_second,
-        flat(out_master),
-        flat(out_first),
-        flat(out_second),
-    )
+    first_new, rest_new = first_new[:6], first_new[6:]
     g_new = adam_update(norm_gains, gain_first, gain_second, gain_total, 0.5, 0.0)
     b_new = adam_update(biases, bias_first, bias_second, bias_total, 0.5, 0.0)
     return (

time: 353 us -> 369 us (1.045)
  starting transfers between devices: 56.3 us -> 36.5 us
  waiting for transfers between devices: 50.3 us -> 68.5 us
  local copies, waits for them, and re-layouts: 23.7 us -> 41 us
    reduce_scatter x4 -> x3, waiting for transfers between devices: 4.79 us -> 19.1 us  [sum_over_rows(): lax.psum_scatter(half.astype(LOW), 'row', scatter_dimension=0, tiled=True)]
    reduce_scatter x4 -> x3, starting transfers between devices: 12.2 us -> 0.54 us  [sum_over_rows(): lax.psum_scatter(half.astype(LOW), 'row', scatter_dimension=0, tiled=True)]
    all_to_all x4 -> x3, waiting for transfers between devices: 17.6 us -> 25.9 us  [exchange_rows(): return lax.all_to_all(blocks, 'row', 0, 0)]
    another operation x7, local copies, waits for them, and re-layouts: 0.09 us -> 7.09 us  [shards(): jnp.stack([one_sums[:, 0], one_sums[:, 1], jnp.sum(two_grad * normed_two,...]
    ppermute x5, starting transfers between devices: 10 us -> 4.04 us  [all_sum(): lax.ppermute(vector, axis, [(i, i ^ step) for i in range(size)])]
    all_to_all x2, waiting for transfers between devices: 10 us -> 5.62 us  [sum_blocks(): blocks = lax.all_to_all(blocks, axis, 0, 0)]
    pallas_call x2 -> x1, Pallas kernels: 12 us -> 8.79 us  [adam(): pl.pallas_call(partial(adam_kernel, rates), in_specs=[ANY] + [VMEM] * (1...]
    all_to_all x4 -> x3, starting transfers between devices: 17.6 us -> 15.4 us  [exchange_rows(): return lax.all_to_all(blocks, 'row', 0, 0)]
  transfers between devices with their start and end apart: 26 -> 23, of which waited for: 10 -> 9; matrix products, arithmetic and copies ran while one was open for 17% -> 20% of each run, Pallas kernels for 16% -> 10%
where the time goes in v6:
time: 369 us; the launch traced here: 363 us
  Pallas kernels  79.3 us (21%)
  blocking collectives  71.9 us (19%)
  waiting for transfers between devices  68.5 us (19%)
  local copies, waits for them, and re-layouts  41 us (11%)
  other arithmetic  37.8 us (10%)
  starting transfers between devices  36.5 us (10%)
  between operations  20 us (5%)
  matrix products  8.52 us (2%)
    all_to_all x3, waiting for transfers between devices, exchange_rows(): return lax.all_to_all(blocks, 'row', 0, 0)  25.9 us
    all_gather x1, blocking collectives, shards(): x_rows = lax.all_gather(x_after, 'row', axis=0, tiled=True)  19.2 us
    reduce_scatter x3, waiting for transfers between devices, sum_over_rows(): lax.psum_scatter(half.astype(LOW), 'row', scatter_dimension=0, tiled=True)  19.1 us
    all_gather x1, blocking collectives, shards(): zb_rows = lax.all_gather(zb, 'row', axis=0, tiled=True)  18.8 us
    all_gather x1, blocking collectives, shards(): branch_rows = lax.all_gather(middle_grad, 'row', axis=0, tiled=True)  18.7 us
    all_to_all x3, starting transfers between devices, exchange_rows(): return lax.all_to_all(blocks, 'row', 0, 0)  15.4 us
    all_gather x6, blocking collectives, both_cores(): lax.all_gather(piece, 'col', axis=0)  15.2 us
    ppermute x5, waiting for transfers between devices, all_sum(): lax.ppermute(vector, axis, [(i, i ^ step) for i in range(size)])  12.7 us
  transfers between devices with their start and end apart: 23, of which 9 were waited for; matrix products, arithmetic and copies ran while one was open for 20% of the time, Pallas kernels for 10%

profile of v6, /device:TPU:0, one launch (start us, length us, event | category | flops | bytes accessed | tf_op | source)
XLA Modules:
  0.0 363.4 jit_solution(17632510986664219640)
XLA Ops:
  8.6 2.6 prepare.2
  11.2 6.4 %all-to-all-start = ((bf16[4,72,576]{2,1,0:T(8,128)(2,1)}), bf16[4,72,576]{2,1,0:T(8,128)(2,1)S(1)}, u32[]{:S(2)}, u32[]{:S(2)}) async-start(bf16[4,72,576]{2,1,0:T(8,128)(2,1)} %prepare.2), calls=%async_computation | async-start | bytes 737280 | tf_op jit(solution)/shard_map/all_to_all | solution.py:65
  21.6 7.2 %all-to-all-done = bf16[4,72,576]{2,1,0:T(8,128)(2,1)S(1)} async-done(((bf16[4,72,576]{2,1,0:T(8,128)(2,1)}), bf16[4,72,576]{2,1,0:T(8,128)(2,1)S(1)}, u32[]{:S(2)}, u32[]{:S(2)}) %all-to-all-start) | async-done | bytes 331808 | tf_op jit(solution)/shard_map/all_to_all | solution.py:65
  30.1 19.2 %all_gather.51.after_ref = bf16[576,768]{1,0:T(8,128)(2,1)} all-gather(bf16[144,768]{1,0:T(8,128)(2,1)S(1)} %pad_add_fusion.1), channel_id=1, replica_groups=mesh['dp'=4,'row'=4,'col'=2] {'row'}, dimensions={0}, use_global_device_ids=true | all-gather | bytes 1105920 | tf_op jit(solution)/shard_map/all_gather | solution.py:540
  49.3 3.5 prepare.3
  52.8 4.2 %all-to-all-start.1 = ((bf16[4,72,1076]{2,1,0:T(8,128)(2,1)}), bf16[4,72,1076]{2,1,0:T(8,128)(2,1)}, u32[]{:S(2)}, u32[]{:S(2)}) async-start(bf16[4,72,1076]{2,1,0:T(8,128)(2,1)} %prepare.3), calls=%async_computation.1 | async-start | bytes 1327104 | tf_op jit(solution)/shard_map/all_to_all | solution.py:65
  75.8 2.9 all-gather
  79.7 4.1 %fusion.3.za_ref = bf16[1152,768]{1,0:T(8,128)(2,1)} fusion(bf16[1152,1152]{1,0:T(8,128)(2,1)S(1)} %fusion.order_ref, bf16[1152,768]{1,0:T(8,128)(2,1)S(1)} %bitcast.61, f32[1152]{0:T(1024)S(1)} %copy-done.29, f32[1152]{0:T(1024)S(1)} %copy-done.28, f32[768]{0:T(1024)S(1)} %add_rsqrt_fusion, f32[768]{0:T(1024)S(1)} %broadcast_multiply_fusion), kind=kOutput, calls=%fused_computation.9 | convolution fusion | flops 2043740160 | bytes 6208512 | tf_op jit(solution)/shard_map/dot_general | solution.py:24
  83.8 9.1 %attend.1 = (bf16[1152,576]{1,0:T(8,128)(2,1)}, bf16[2,3,72,768]{3,2,1,0:T(8,128)(2,1)}, bf16[768,144]{1,0:T(8,128)(2,1)}, bf16[384,1152]{1,0:T(8,128)(2,1)}, bf16[384,1152]{1,0:T(8,128)(2,1)}) custom-call(s32[3]{0:T(128)} %pad_add_fusion.2.after_ref.place_ref, bf16[288,1076]{1,0:T(8,128)(2,1)} %bitcast.8.after_ref.refs_0_, bf16[1152,768]{1,0:T(8,128)(2,1)} %fusion.3.za_ref, ...), custom_call_target="tpu_custom_call" | custom-call | tf_op jit(solution)/shard_map/attend/pallas_call | solution.py:202
  93.1 2.5 collective-permute-done.3
  104.5 9.3 %beside.1 = (bf16[768,1152]{1,0:T(8,128)(2,1)}, bf16[1152,432]{1,0:T(8,128)(2,1)}, f32[96,1152]{1,0:T(8,128)}) custom-call(s32[3]{0:T(128)} %pad_add_fusion.2.after_ref.place_ref, bf16[384,1152]{1,0:T(8,128)(2,1)} %add_convert_fusion.4.after_ref, bf16[1152,1152]{1,0:T(8,128)(2,1)} %copy-done, bf16[8,144,768]{2,1,0:T(8,128)(2,1)} %bitcast.81, ...), custom_call_target="tpu_custom_call" | custom-call | tf_op jit(solution)/shard_map/beside/pallas_call | solution.py:238
  113.8 10.4 %reduce-scatter.4.cloned.1.call-done = bf16[96,1152]{1,0:T(8,128)(2,1)} async-done(((bf16[384,1152]{1,0:T(8,128)(2,1)}), bf16[96,1152]{1,0:T(8,128)(2,1)}) %reduce-scatter.4.cloned.1.call-update) | async-done | bytes 221200 | tf_op jit(solution)/shard_map/reduce_scatter | solution.py:74
  125.8 18.8 %all_gather.58.after_ref = bf16[384,1152]{1,0:T(8,128)(2,1)S(1)} all-gather(bf16[96,1152]{1,0:T(8,128)(2,1)S(1)} %add_convert_fusion.5), channel_id=1, replica_groups=mesh['dp'=4,'row'=4,'col'=2] {'row'}, dimensions={0}, use_global_device_ids=true | all-gather | bytes 1105920 | tf_op jit(solution)/shard_map/all_gather | solution.py:583
  152.1 8.8 %before.1 = (bf16[1152,538]{1,0:T(8,128)(2,1)}, f32[768,538]{1,0:T(8,128)}, bf16[1152,538]{1,0:T(8,128)(2,1)}) custom-call(s32[3]{0:T(128)} %pad_add_fusion.2.after_ref.place_ref, bf16[384,1152]{1,0:T(8,128)(2,1)} %copy-done.5, bf16[1152,1152]{1,0:T(8,128)(2,1)} %copy-done, bf16[768,1152]{1,0:T(8,128)(2,1)} %get-tuple-element.61.cot_ref, ...), custom_call_target="tpu_custom_call" | custom-call | tf_op jit(solution)/shard_map/before/pallas_call | solution.py:265
  160.9 9.4 %mlp.1 = (bf16[768,538]{1,0:T(8,128)(2,1)}, bf16[768,538]{1,0:T(8,128)(2,1)}, bf16[384,1152]{1,0:T(8,128)(2,1)}, bf16[384,1152]{1,0:T(8,128)(2,1)}, f32[1,538]{1,0:T(1,128)}) custom-call(s32[1]{0:T(128)} %bitcast.core_ref, bf16[768,1152]{1,0:T(8,128)(2,1)} %bitcast.66, bf16[1152,538]{1,0:T(8,128)(2,1)} %get-tuple-element.63.up_ref, ...), custom_call_target="tpu_custom_call" | custom-call | tf_op jit(solution)/shard_map/mlp/pallas_call | solution.py:351
  170.5 2.5 collective-permute-done.7
  179.4 10.2 %behind.1 = (bf16[4,288,1076]{2,1,0:T(8,128)(2,1)}, bf16[576,768]{1,0:T(8,128)(2,1)}, bf16[576,768]{1,0:T(8,128)(2,1)}) custom-call(s32[3]{0:T(128)} %pad_add_fusion.2.after_ref.place_ref, bf16[384,1152]{1,0:T(8,128)(2,1)} %add_convert_fusion.3.after_ref, bf16[768,1152]{1,0:T(8,128)(2,1)} %bitcast.67, bf16[768,538]{1,0:T(8,128)(2,1)} %get-tuple-element.67.hid_ref, ...), custom_call_target="tpu_custom_call" | custom-call | tf_op jit(solution)/shard_map/behind/pallas_call | solution.py:297
  191.4 8.7 %reduce-scatter.6.cloned.1.call-done = bf16[96,1152]{1,0:T(8,128)(2,1)} async-done(((bf16[384,1152]{1,0:T(8,128)(2,1)}), bf16[96,1152]{1,0:T(8,128)(2,1)}) %reduce-scatter.6.cloned.1.call-update) | async-done | bytes 221200 | tf_op jit(solution)/shard_map/reduce_scatter | solution.py:74
  203.7 18.7 %all_gather.63 = bf16[384,1152]{1,0:T(8,128)(2,1)S(1)} all-gather(bf16[96,1152]{1,0:T(8,128)(2,1)S(1)} %get-tuple-element.113), channel_id=1, replica_groups=mesh['dp'=4,'row'=4,'col'=2] {'row'}, dimensions={0}, use_global_device_ids=true | all-gather | bytes 1105920 | tf_op jit(solution)/shard_map/all_gather | solution.py:604
  225.0 2.6 all-gather.6
  228.9 10.7 %attend_back.1 = (bf16[432,768]{1,0:T(8,128)(2,1)}, f32[432,1]{1,0:T(8,128)}, bf16[4,288,576]{2,1,0:T(8,128)(2,1)}) custom-call(bf16[768,1152]{1,0:T(8,128)(2,1)} %bitcast.64, bf16[1152,576]{1,0:T(8,128)(2,1)} %get-tuple-element.59.w_ref, bf16[2,3,72,768]{3,2,1,0:T(8,128)(2,1)} %get-tuple-element.71.qkv_ref, bf16[1152,768]{1,0:T(8,128)(2,1)} %fusion.3.za_ref, ...), custom_call_target="tpu_custom_call" | custom-call | tf_op jit(solution)/shard_map/attend_back/pallas_call | solution.py:407
  239.7 6.7 %first_back.1 = (bf16[4,304,768]{2,1,0:T(8,128)(2,1)}, bf16[4,304,768]{2,1,0:T(8,128)(2,1)}, f32[1152,2]{1,0:T(8,128)}) custom-call(s32[1]{0:T(128)} %bitcast.core_ref, bf16[1152,432]{1,0:T(8,128)(2,1)} %get-tuple-element.60.w_ref, bf16[432,768]{1,0:T(8,128)(2,1)} %get-tuple-element.73.grad_ref, bf16[1152,768]{1,0:T(8,128)(2,1)} %bitcast.63, ...), custom_call_target="tpu_custom_call" | custom-call | tf_op jit(solution)/shard_map/first_back/pallas_call | solution.py:454
  246.4 4.5 %all-to-all-start.3 = ((bf16[4,288,1076]{2,1,0:T(8,128)(2,1)}), bf16[4,288,1076]{2,1,0:T(8,128)(2,1)}, u32[]{:S(2)}, u32[]{:S(2)}) async-start(bf16[4,288,1076]{2,1,0:T(8,128)(2,1)} %get-tuple-element.78), calls=%async_computation.6 | async-start | bytes 5308416 | tf_op jit(solution)/shard_map/all_to_all | solution.py:69
  270.3 2.6 add_convert_fusion.after_ref
  277.2 5.6 %all-to-all-done.3 = bf16[4,288,1076]{2,1,0:T(8,128)(2,1)} async-done(((bf16[4,288,1076]{2,1,0:T(8,128)(2,1)}), bf16[4,288,1076]{2,1,0:T(8,128)(2,1)}, u32[]{:S(2)}, u32[]{:S(2)}) %all-to-all-start.3) | async-done | bytes 2479136 | tf_op jit(solution)/shard_map/all_to_all | solution.py:69
  282.8 4.6 %all-to-all-start.2 = ((bf16[4,288,576]{2,1,0:T(8,128)(2,1)}), bf16[4,288,576]{2,1,0:T(8,128)(2,1)}, u32[]{:S(2)}, u32[]{:S(2)}) async-start(bf16[4,288,576]{2,1,0:T(8,128)(2,1)} %get-tuple-element.77), calls=%async_computation.5 | async-start | bytes 2949120 | tf_op jit(solution)/shard_map/all_to_all | solution.py:69
  290.3 5.8 %collective-permute-done.10 = f32[16,1152]{1,0:T(8,128)S(1)} collective-permute-done((f32[16,1152]{1,0:T(8,128)S(1)}, f32[16,1152]{1,0:T(8,128)S(1)}, u32[]{:S(2)}, u32[]{:S(2)}) %collective-permute-start.10) | collective-permute-done | bytes 73760 | tf_op jit(solution)/shard_map/ppermute | solution.py:86
  296.2 2.9 fusion.23
  300.3 6.9 %collective-permute-done.11 = f32[16,1152]{1,0:T(8,128)S(1)} collective-permute-done((f32[16,1152]{1,0:T(8,128)S(1)}, f32[16,1152]{1,0:T(8,128)S(1)}, u32[]{:S(2)}, u32[]{:S(2)}) %collective-permute-start.11) | collective-permute-done | bytes 73760 | tf_op jit(solution)/shard_map/ppermute | solution.py:86
  315.9 4.8 %all-to-all-start.4 = ((bf16[4,72,1652]{2,1,0:T(8,128)(2,1)}), bf16[4,72,1652]{2,1,0:T(8,128)(2,1)S(1)}, u32[]{:S(2)}, u32[]{:S(2)}) async-start(bf16[4,72,1652]{2,1,0:T(8,128)(2,1)} %pad_maximum_fusion.3), calls=%async_computation.7 | async-start | bytes 1916928 | tf_op jit(solution)/shard_map/all_to_all | solution.py:65
  324.2 18.7 %all-to-all-done.4.blocks_ref = bf16[4,72,1652]{2,1,0:T(8,128)(2,1)S(1)} async-done(((bf16[4,72,1652]{2,1,0:T(8,128)(2,1)}), bf16[4,72,1652]{2,1,0:T(8,128)(2,1)S(1)}, u32[]{:S(2)}, u32[]{:S(2)}) %all-to-all-start.4) | async-done | bytes 951584 | tf_op jit(solution)/shard_map/all_to_all | solution.py:65
  343.8 8.8 %adam.1 = (f32[72,1,1728]{2,1,0:T(1,128)}, f32[72,1,1728]{2,1,0:T(1,128)}, f32[72,1,1728]{2,1,0:T(1,128)}, f32[72,1,576]{2,1,0:T(1,128)}, f32[72,1,576]{2,1,0:T(...) custom-call(bf16[4,304,768]{2,1,0:T(8,128)(2,1)} %copy-done.2, ...), custom_call_target="tpu_custom_call" | custom-call | tf_op jit(solution)/shard_map/adam/pallas_call | solution.py:138
  (227 shorter events, 99.7 us)
Async XLA Ops:
  11.2 18.8 %copy-start.11 = (bf16[729,144]{0,1:T(8,128)(2,1)S(1)}, bf16[729,144]{0,1:T(8,128)(2,1)}, u32[]{:S(2)}) copy-start(bf16[729,144]{0,1:T(8,128)(2,1)} %param.20) | copy-start | bytes 629860
  11.2 17.6 %all-to-all-start = ((bf16[4,72,576]{2,1,0:T(8,128)(2,1)}), bf16[4,72,576]{2,1,0:T(8,128)(2,1)S(1)}, u32[]{:S(2)}, u32[]{:S(2)}) async-start(bf16[4,72,576]{2,1,0:T(8,128)(2,1)} %prepare.2), calls=%async_computation | async-start | bytes 737280 | tf_op jit(solution)/shard_map/all_to_all | solution.py:65
  18.2 61.5 %copy-start = (bf16[1152,1152]{1,0:T(8,128)(2,1)}, bf16[1152,1152]{1,0:T(8,128)(2,1)S(1)}, u32[]{:S(2)}) copy-start(bf16[1152,1152]{1,0:T(8,128)(2,1)S(1)} %fusion.order_ref) | copy-start | bytes 7962628
  28.8 20.5 %copy-start.10 = (bf16[4,72,576]{2,1,0:T(8,128)(2,1)}, bf16[4,72,576]{2,1,0:T(8,128)(2,1)S(1)}, u32[]{:S(2)}) copy-start(bf16[4,72,576]{2,1,0:T(8,128)(2,1)S(1)} %all-to-all-done) | copy-start | bytes 995332
  49.3 9.4 %copy-start.21 = (f32[2,1152]{1,0:T(2,128)S(1)}, f32[2,1152]{1,0:T(2,128)}, u32[]{:S(2)}) copy-start(f32[2,1152]{1,0:T(2,128)} %param.34) | copy-start | bytes 27652
  49.3 19.7 %copy-start.4 = (bf16[576,768]{1,0:T(8,128)(2,1)S(1)}, bf16[576,768]{1,0:T(8,128)(2,1)}, u32[]{:S(2)}) copy-start(bf16[576,768]{1,0:T(8,128)(2,1)} %all_gather.51.after_ref) | copy-start | bytes 2654212
  52.8 19.4 %all-to-all-start.1 = ((bf16[4,72,1076]{2,1,0:T(8,128)(2,1)}), bf16[4,72,1076]{2,1,0:T(8,128)(2,1)}, u32[]{:S(2)}, u32[]{:S(2)}) async-start(bf16[4,72,1076]{2,1,0:T(8,128)(2,1)} %prepare.3), calls=%async_computation.1 | async-start | bytes 1327104 | tf_op jit(solution)/shard_map/all_to_all | solution.py:65
  57.0 47.5 %all-gather.9.cloned.1.call-start = ((), (), s32[]{:S(2)}) async-start(), calls=%async_computation.11 | async-start | bytes 1990656 | tf_op jit(solution)/shard_map/all_gather | solution.py:547
  65.5 18.3 %collective-permute-start = (bf16[288,576]{1,0:T(8,128)(2,1)}, bf16[288,576]{1,0:T(8,128)(2,1)}, u32[]{:S(2)}, u32[]{:S(2)}) collective-permute-start(bf16[288,576]{1,0:T(8,128)(2,1)} %bitcast.83), channel_id=1, source_target_pairs={{0,8},{8,0},{16,24},{24,16},{1,9},{9,1},{17,25},{25,17},{2,10},{10... | collective-permute-start | bytes 995336 | tf_op jit(solution)/shard_map/ppermute | solution.py:55
  67.0 16.8 %collective-permute-start.1 = (bf16[288,576]{1,0:T(8,128)(2,1)}, bf16[288,576]{1,0:T(8,128)(2,1)}, u32[]{:S(2)}, u32[]{:S(2)}) collective-permute-start(bf16[288,576]{1,0:T(8,128)(2,1)} %bitcast.84), channel_id=1, source_target_pairs={{0,16},{8,24},{16,0},{24,8},{1,17},{9,25},{17,1},{25,9},{2,18},{10... | collective-permute-start | bytes 995336 | tf_op jit(solution)/shard_map/ppermute | solution.py:55
  68.5 15.3 %collective-permute-start.2 = (bf16[288,576]{1,0:T(8,128)(2,1)}, bf16[288,576]{1,0:T(8,128)(2,1)}, u32[]{:S(2)}, u32[]{:S(2)}) collective-permute-start(bf16[288,576]{1,0:T(8,128)(2,1)} %bitcast.85), channel_id=1, source_target_pairs={{0,24},{8,16},{16,8},{24,0},{1,25},{9,17},{17,9},{25,1},{2,26},{10... | collective-permute-start | bytes 995336 | tf_op jit(solution)/shard_map/ppermute | solution.py:55
  75.8 48.4 %reduce-scatter.4.cloned.1.call-start = ((), (), s32[]{:S(2)}) async-start(), calls=%async_computation.8 | async-start | bytes 1105920 | tf_op jit(solution)/shard_map/reduce_scatter | solution.py:74
  93.0 2.7 collective-permute-start.3
  98.1 102.0 %reduce-scatter.6.cloned.1.call-start = ((), (), s32[]{:S(2)}) async-start(), calls=%async_computation.9 | async-start | bytes 1105920 | tf_op jit(solution)/shard_map/reduce_scatter | solution.py:74
  101.0 49.9 %collective-permute-start.4 = (bf16[288,1076]{1,0:T(8,128)(2,1)}, bf16[288,1076]{1,0:T(8,128)(2,1)S(1)}, u32[]{:S(2)}, u32[]{:S(2)}) collective-permute-start(bf16[288,1076]{1,0:T(8,128)(2,1)} %bitcast.8.after_ref.refs_0_), channel_id=1, source_target_pairs={{0,8},{8,0},{16,24},{24,16},{1,9},{9,1},{17,25},{25,17},{2,10},{10... | collective-permute-start | bytes 1859336 | tf_op jit(solution)/shard_map/ppermute | solution.py:55
  102.4 48.5 %collective-permute-start.5 = (bf16[288,1076]{1,0:T(8,128)(2,1)}, bf16[288,1076]{1,0:T(8,128)(2,1)S(1)}, u32[]{:S(2)}, u32[]{:S(2)}) collective-permute-start(bf16[288,1076]{1,0:T(8,128)(2,1)} %bitcast.8.after_ref.refs_0_), channel_id=1, source_target_pairs={{0,16},{8,24},{16,0},{24,8},{1,17},{9,25},{17,1},{25,9},{2,18},{10... | collective-permute-start | bytes 1859336 | tf_op jit(solution)/shard_map/ppermute | solution.py:55
  103.9 47.0 %collective-permute-start.6 = (bf16[288,1076]{1,0:T(8,128)(2,1)}, bf16[288,1076]{1,0:T(8,128)(2,1)S(1)}, u32[]{:S(2)}, u32[]{:S(2)}) collective-permute-start(bf16[288,1076]{1,0:T(8,128)(2,1)} %bitcast.8.after_ref.refs_0_), channel_id=1, source_target_pairs={{0,24},{8,16},{16,8},{24,0},{1,25},{9,17},{17,9},{25,1},{2,26},{10... | collective-permute-start | bytes 1859336 | tf_op jit(solution)/shard_map/ppermute | solution.py:55
  170.4 2.7 collective-permute-start.7
  246.4 23.9 %collective-permute-start.8 = (bf16[4,304,768]{2,1,0:T(8,128)(2,1)}, bf16[4,304,768]{2,1,0:T(8,128)(2,1)}, u32[]{:S(2)}, u32[]{:S(2)}) collective-permute-start(bf16[4,304,768]{2,1,0:T(8,128)(2,1)} %get-tuple-element.76), channel_id=1, source_target_pairs={{0,1},{1,0},{2,3},{3,2},{4,5},{5,4},{6,7},{7,6},{8,9},{9,8},{10,11... | collective-permute-start | bytes 5603336 | tf_op jit(solution)/shard_map/ppermute | solution.py:39
  246.4 36.3 %all-to-all-start.3 = ((bf16[4,288,1076]{2,1,0:T(8,128)(2,1)}), bf16[4,288,1076]{2,1,0:T(8,128)(2,1)}, u32[]{:S(2)}, u32[]{:S(2)}) async-start(bf16[4,288,1076]{2,1,0:T(8,128)(2,1)} %get-tuple-element.78), calls=%async_computation.6 | async-start | bytes 5308416 | tf_op jit(solution)/shard_map/all_to_all | solution.py:69
  251.0 101.6 %reduce-scatter.8.cloned.1.call-start = ((), (), s32[]{:S(2)}) async-start(), calls=%async_computation.10 | async-start | bytes 2334720 | tf_op jit(solution)/shard_map/reduce_scatter | solution.py:74
  275.9 11.4 %collective-permute-start.9 = (f32[16,1152]{1,0:T(8,128)}, f32[16,1152]{1,0:T(8,128)}, u32[]{:S(2)}, u32[]{:S(2)}) collective-permute-start(f32[16,1152]{1,0:T(8,128)} %fusion.29), channel_id=1, source_target_pairs={{0,1},{1,0},{2,3},{3,2},{4,5},{5,4},{6,7},{7,6},{8,9},{9,8},{10,11... | collective-permute-start | bytes 221192 | tf_op jit(solution)/shard_map/ppermute | solution.py:86
  282.8 28.5 %all-to-all-start.2 = ((bf16[4,288,576]{2,1,0:T(8,128)(2,1)}), bf16[4,288,576]{2,1,0:T(8,128)(2,1)}, u32[]{:S(2)}, u32[]{:S(2)}) async-start(bf16[4,288,576]{2,1,0:T(8,128)(2,1)} %get-tuple-element.77), calls=%async_computation.5 | async-start | bytes 2949120 | tf_op jit(solution)/shard_map/all_to_all | solution.py:69
  288.3 7.8 %collective-permute-start.10 = (f32[16,1152]{1,0:T(8,128)S(1)}, f32[16,1152]{1,0:T(8,128)S(1)}, u32[]{:S(2)}, u32[]{:S(2)}) collective-permute-start(f32[16,1152]{1,0:T(8,128)S(1)} %fusion.71), channel_id=1, source_target_pairs={{0,2},{2,0},{4,6},{6,4},{1,3},{3,1},{5,7},{7,5},{8,10},{10,8},{12,... | collective-permute-start | bytes 221192 | tf_op jit(solution)/shard_map/ppermute | solution.py:86
  296.2 11.1 %collective-permute-start.11 = (f32[16,1152]{1,0:T(8,128)S(1)}, f32[16,1152]{1,0:T(8,128)S(1)}, u32[]{:S(2)}, u32[]{:S(2)}) collective-permute-start(f32[16,1152]{1,0:T(8,128)S(1)} %add.316), channel_id=1, source_target_pairs={{0,4},{2,6},{4,0},{6,2},{1,5},{3,7},{5,1},{7,3},{8,12},{10,14},{12... | collective-permute-start | bytes 221192 | tf_op jit(solution)/shard_map/ppermute | solution.py:86
  307.2 5.8 %collective-permute-start.12 = (f32[16,1152]{1,0:T(8,128)S(1)}, f32[16,1152]{1,0:T(8,128)S(1)}, u32[]{:S(2)}, u32[]{:S(2)}) collective-permute-start(f32[16,1152]{1,0:T(8,128)S(1)} %add.317), channel_id=1, source_target_pairs={{0,8},{8,0},{16,24},{24,16},{1,9},{9,1},{17,25},{25,17},{2,10},{10... | collective-permute-start | bytes 221192 | tf_op jit(solution)/shard_map/ppermute | solution.py:86
  313.1 7.6 %collective-permute-start.13 = (f32[16,1152]{1,0:T(8,128)S(1)}, f32[16,1152]{1,0:T(8,128)S(1)}, u32[]{:S(2)}, u32[]{:S(2)}) collective-permute-start(f32[16,1152]{1,0:T(8,128)S(1)} %add.318), channel_id=1, source_target_pairs={{0,16},{8,24},{16,0},{24,8},{1,17},{9,25},{17,1},{25,9},{2,18},{10... | collective-permute-start | bytes 221192 | tf_op jit(solution)/shard_map/ppermute | solution.py:86
  315.8 7.0 %copy-start.27 = (f32[2,1152]{1,0:T(2,128)S(1)}, f32[2,1152]{1,0:T(2,128)}, u32[]{:S(2)}) copy-start(f32[2,1152]{1,0:T(2,128)} %param.36) | copy-start | bytes 27652
  315.9 7.6 %copy-start.17 = (f32[11216]{0:T(1024)S(1)}, f32[11216]{0:T(1024)}, u32[]{:S(2)}) copy-start(f32[11216]{0:T(1024)} %param.37) | copy-start | bytes 134596
  315.9 7.6 %copy-start.18 = (f32[11216]{0:T(1024)S(1)}, f32[11216]{0:T(1024)}, u32[]{:S(2)}) copy-start(f32[11216]{0:T(1024)} %param.38) | copy-start | bytes 134596
  315.9 7.6 %copy-start.19 = (f32[11216]{0:T(1024)S(1)}, f32[11216]{0:T(1024)}, u32[]{:S(2)}) copy-start(f32[11216]{0:T(1024)} %param.39) | copy-start | bytes 134596
  315.9 27.0 %all-to-all-start.4 = ((bf16[4,72,1652]{2,1,0:T(8,128)(2,1)}), bf16[4,72,1652]{2,1,0:T(8,128)(2,1)S(1)}, u32[]{:S(2)}, u32[]{:S(2)}) async-start(bf16[4,72,1652]{2,1,0:T(8,128)(2,1)} %pad_maximum_fusion.3), calls=%async_computation.7 | async-start | bytes 1916928 | tf_op jit(solution)/shard_map/all_to_all | solution.py:65
  (22 other events, 73.9 us)
Sparse Core Ops, SparseCore 0:
  75.9 27.7 all-gather.8
Sparse Core Ops, SparseCore 1:
  98.2 25.9 reduce-scatter.3
  175.7 24.4 reduce-scatter.5
  277.3 43.0 reduce-scatter.7

commit v7 on v6

--- a/solution.py
+++ b/solution.py
@@ -379,7 +379,8 @@
     )(core, zb, w_up, up_bias, active_grad)
 
 
-def back_kernel(bg_ref, w_ref, qkv_ref, za_ref, att_ref, grad_ref, sum_ref, wg_ref):
+def back_kernel(after_ref, bg_ref, w_ref, qkv_ref, za_ref, att_ref, grad_ref, sum_ref, wg_ref):
+    del after_ref
     heads = qkv_ref.shape[0]
     attended_grad = dot(bg_ref[...], w_ref[:, heads * 3 * HEAD :], 1, 0).T
     scale = HEAD ** (-0.5)
@@ -402,11 +403,11 @@
     wg_ref[...] = jnp.concatenate([qkv_part, out_part], axis=1).reshape(wg_ref.shape)
 
 
-def attend_back(branch_all, w_first, qkv, za, attended, n_dp):
+def attend_back(after, branch_all, w_first, qkv, za, attended, n_dp):
     tokens, width = attended.shape
     return pl.pallas_call(
         back_kernel,
-        in_specs=[VMEM] * 5,
+        in_specs=[ANY] + [VMEM] * 5,
         out_specs=[VMEM] * 3,
         out_shape=(
             jax.ShapeDtypeStruct((3 * width, tokens), LOW),
@@ -415,7 +416,7 @@
         ),
         compiler_params=BIG,
         name="attend_back",
-    )(branch_all, w_first, qkv, za, attended)
+    )(after, branch_all, w_first, qkv, za, attended)
 
 
 def first_kernel(
@@ -604,9 +605,10 @@
     branch_rows = lax.all_gather(middle_grad, "row", axis=0, tiled=True)
     later = zero_of(branch_rows)
     branch_all = both_cores(branch_rows)
+    rest_rows = sum_blocks(rest_grad, "dp", later)
 
     qkv_grad, bias_sums, first_grad = attend_back(
-        branch_all, w_first, qkv, za, attended, n_dp
+        rest_rows, branch_all, w_first, qkv, za, attended, n_dp
     )
     theirs, mine, one_sums = first_back(
         core_of, qkv_mixed, qkv_grad, x_all, x_mean, inverse_one, gain_one[:, None],
@@ -617,7 +619,6 @@
     result = one_grad[width + 16 :] + down_bias[:, None]
     result = result.astype(LOW)[:, :tokens].T
     first_rows = sum_blocks(first_grad, "dp", 0.0)
-    rest_rows = sum_blocks(rest_grad, "dp", later)
 
     own_gain = lax.dynamic_slice_in_dim(norm_gains[0], feature_start, width)[:, None]
     own_normed = (x_own.astype(jnp.float32) - x_mean) * inverse_one
@@ -631,19 +632,19 @@
     input_grad = input_grad.astype(LOW)[:, :tokens].T
 
     later = zero_of(pair)
-    bias_sums = bias_sums.reshape(heads, 3, HEAD)
+    bias_sums = (bias_sums + later).reshape(heads, 3, HEAD)
     all_rows = jnp.stack(
         [
-            one_sums[:, 0],
-            one_sums[:, 1],
-            jnp.sum(two_grad * normed_two, axis=0),
-            jnp.sum(two_grad, axis=0),
-            jnp.sum(middle_grad, axis=0, dtype=jnp.float32),
-            jnp.sum(cot_mine, axis=0),
+            one_sums[:, 0] + later,
+            one_sums[:, 1] + later,
+            jnp.sum(two_grad * normed_two + later, axis=0),
+            jnp.sum(two_grad + later, axis=0),
+            jnp.sum(middle_grad.astype(jnp.float32) + later, axis=0),
+            jnp.sum(cot_mine + later, axis=0),
         ]
     )
     own_row = jnp.concatenate(
-        [bias_sums[:, 0].reshape(width), bias_sums[:, 2].reshape(width), up_sums[0]]
+        [bias_sums[:, 0].reshape(width), bias_sums[:, 2].reshape(width), up_sums[0] + later]
     )
     own_row = jnp.pad(own_row, (0, D - own_row.shape[0]))
     own_rows = jnp.where(jnp.arange(group)[:, None] == own, own_row[None, :], 0.0)

time: 369 us -> 348 us (0.943)
  local copies, waits for them, and re-layouts: 41 us -> 22.7 us
  other arithmetic: 37.8 us -> 31.7 us
  waiting for transfers between devices: 68.5 us -> 72.2 us
    another operation x7 -> x5, local copies, waits for them, and re-layouts: 7.09 us -> 0.08 us  [shards(): jnp.stack([one_sums[:, 0] + later, one_sums[:, 1] + later, jnp.sum(two_gr...]
    all_to_all x2, waiting for transfers between devices: 5.62 us -> 0.01 us  [sum_blocks(): blocks = lax.all_to_all(blocks, axis, 0, 0)]
    all_to_all x3, waiting for transfers between devices: 25.9 us -> 31.3 us  [exchange_rows(): return lax.all_to_all(blocks, 'row', 0, 0)]
    reduce_scatter x3, waiting for transfers between devices: 19.1 us -> 15.1 us  [sum_over_rows(): lax.psum_scatter(half.astype(LOW), 'row', scatter_dimension=0, tiled=True)]
    ppermute x3, waiting for transfers between devices: 5.04 us -> 8.99 us  [swap_cores(): lax.ppermute(array, 'col', [(i, (i + 1) % n_col) for i in range(n_col)])]
    ppermute x5, waiting for transfers between devices: 12.7 us -> 16.7 us  [all_sum(): lax.ppermute(vector, axis, [(i, i ^ step) for i in range(size)])]
  transfers between devices with their start and end apart: 23 -> 23, of which waited for: 9 -> 9; matrix products, arithmetic and copies ran while one was open for 20% -> 13% of each run, Pallas kernels for 10% -> 11%
where the time goes in v7:
time: 348 us; the launch traced here: 342 us
  Pallas kernels  79.3 us (23%)
  waiting for transfers between devices  72.2 us (21%)
  blocking collectives  71.9 us (21%)
  starting transfers between devices  35.9 us (10%)
  other arithmetic  31.7 us (9%)
  local copies, waits for them, and re-layouts  22.7 us (7%)
  between operations  20.1 us (6%)
  matrix products  8.57 us (2%)
    all_to_all x3, waiting for transfers between devices, exchange_rows(): return lax.all_to_all(blocks, 'row', 0, 0)  31.3 us
    all_gather x1, blocking collectives, shards(): x_rows = lax.all_gather(x_after, 'row', axis=0, tiled=True)  19.2 us
    all_gather x1, blocking collectives, shards(): branch_rows = lax.all_gather(middle_grad, 'row', axis=0, tiled=True)  18.8 us
    all_gather x1, blocking collectives, shards(): zb_rows = lax.all_gather(zb, 'row', axis=0, tiled=True)  18.7 us
    ppermute x5, waiting for transfers between devices, all_sum(): lax.ppermute(vector, axis, [(i, i ^ step) for i in range(size)])  16.7 us
    all_gather x6, blocking collectives, both_cores(): lax.all_gather(piece, 'col', axis=0)  15.2 us
    reduce_scatter x3, waiting for transfers between devices, sum_over_rows(): lax.psum_scatter(half.astype(LOW), 'row', scatter_dimension=0, tiled=True)  15.1 us
    all_to_all x3, starting transfers between devices, exchange_rows(): return lax.all_to_all(blocks, 'row', 0, 0)  14.7 us
  transfers between devices with their start and end apart: 23, of which 9 were waited for; matrix products, arithmetic and copies ran while one was open for 13% of the time, Pallas kernels for 11%

profile of v7, /device:TPU:0, one launch (start us, length us, event | category | flops | bytes accessed | tf_op | source)
XLA Modules:
  0.0 342.4 jit_solution(12136929922669070481)
XLA Ops:
  8.6 2.6 prepare.2
  11.2 6.4 %all-to-all-start = ((bf16[4,72,576]{2,1,0:T(8,128)(2,1)}), bf16[4,72,576]{2,1,0:T(8,128)(2,1)S(1)}, u32[]{:S(2)}, u32[]{:S(2)}) async-start(bf16[4,72,576]{2,1,0:T(8,128)(2,1)} %prepare.2), calls=%async_computation | async-start | bytes 737280 | tf_op jit(solution)/shard_map/all_to_all | solution.py:65
  19.7 9.1 %all-to-all-done = bf16[4,72,576]{2,1,0:T(8,128)(2,1)S(1)} async-done(((bf16[4,72,576]{2,1,0:T(8,128)(2,1)}), bf16[4,72,576]{2,1,0:T(8,128)(2,1)S(1)}, u32[]{:S(2)}, u32[]{:S(2)}) %all-to-all-start) | async-done | bytes 331808 | tf_op jit(solution)/shard_map/all_to_all | solution.py:65
  30.1 19.2 %all_gather.51.after_ref = bf16[576,768]{1,0:T(8,128)(2,1)} all-gather(bf16[144,768]{1,0:T(8,128)(2,1)S(1)} %pad_add_fusion.1), channel_id=1, replica_groups=mesh['dp'=4,'row'=4,'col'=2] {'row'}, dimensions={0}, use_global_device_ids=true | all-gather | bytes 1105920 | tf_op jit(solution)/shard_map/all_gather | solution.py:541
  49.3 3.5 %prepare.3 = bf16[4,72,1076]{2,1,0:T(8,128)(2,1)} custom-call(bf16[576,768]{1,0:T(8,128)(2,1)} %all_gather.51.after_ref, f32[72,1,2152]{2,1,0:T(1,128)} %refs_6_.1, f32[72,1,2152]{2,1,0:T(1,128)} %bitcast.79), custom_call_target="tpu_custom_call" | custom-call | tf_op jit(solution)/shard_map/prepare/pallas_call | solution.py:111
  52.8 4.2 %all-to-all-start.1 = ((bf16[4,72,1076]{2,1,0:T(8,128)(2,1)}), bf16[4,72,1076]{2,1,0:T(8,128)(2,1)}, u32[]{:S(2)}, u32[]{:S(2)}) async-start(bf16[4,72,1076]{2,1,0:T(8,128)(2,1)} %prepare.3), calls=%async_computation.1 | async-start | bytes 1327104 | tf_op jit(solution)/shard_map/all_to_all | solution.py:65
  75.1 2.9 all-gather
  79.1 4.1 %fusion.3.za_ref = bf16[1152,768]{1,0:T(8,128)(2,1)} fusion(bf16[1152,1152]{1,0:T(8,128)(2,1)S(1)} %fusion.order_ref, bf16[1152,768]{1,0:T(8,128)(2,1)S(1)} %bitcast.61, f32[1152]{0:T(1024)S(1)} %copy-done.32, f32[1152]{0:T(1024)S(1)} %copy-done.33, f32[768]{0:T(1024)S(1)} %add_rsqrt_fusion, f32[768]{0:T(1024)S(1)} %broadcast_multiply_fusion), kind=kOutput, calls=%fused_computation.9 | convolution fusion | flops 2043740160 | bytes 6208512 | tf_op jit(solution)/shard_map/dot_general | solution.py:24
  83.2 9.2 %attend.1 = (bf16[1152,576]{1,0:T(8,128)(2,1)}, bf16[2,3,72,768]{3,2,1,0:T(8,128)(2,1)}, bf16[768,144]{1,0:T(8,128)(2,1)}, bf16[384,1152]{1,0:T(8,128)(2,1)}, bf16[384,1152]{1,0:T(8,128)(2,1)}) custom-call(s32[3]{0:T(128)} %pad_add_fusion.2.after_ref.place_ref, bf16[288,1076]{1,0:T(8,128)(2,1)} %bitcast.8.after_ref.refs_0_, bf16[1152,768]{1,0:T(8,128)(2,1)} %fusion.3.za_ref, ...), custom_call_target="tpu_custom_call" | custom-call | tf_op jit(solution)/shard_map/attend/pallas_call | solution.py:202
  92.5 2.5 collective-permute-done.3
  103.2 9.3 %beside.1 = (bf16[768,1152]{1,0:T(8,128)(2,1)}, bf16[1152,432]{1,0:T(8,128)(2,1)}, f32[96,1152]{1,0:T(8,128)}) custom-call(s32[3]{0:T(128)} %pad_add_fusion.2.after_ref.place_ref, bf16[384,1152]{1,0:T(8,128)(2,1)} %add_convert_fusion.4.after_ref, bf16[1152,1152]{1,0:T(8,128)(2,1)} %copy-done, bf16[8,144,768]{2,1,0:T(8,128)(2,1)} %bitcast.81, ...), custom_call_target="tpu_custom_call" | custom-call | tf_op jit(solution)/shard_map/beside/pallas_call | solution.py:238
  112.5 10.9 %reduce-scatter.4.cloned.1.call-done = bf16[96,1152]{1,0:T(8,128)(2,1)} async-done(((bf16[384,1152]{1,0:T(8,128)(2,1)}), bf16[96,1152]{1,0:T(8,128)(2,1)}) %reduce-scatter.4.cloned.1.call-update) | async-done | bytes 221200 | tf_op jit(solution)/shard_map/reduce_scatter | solution.py:74
  125.1 18.7 %all_gather.58.after_ref = bf16[384,1152]{1,0:T(8,128)(2,1)S(1)} all-gather(bf16[96,1152]{1,0:T(8,128)(2,1)S(1)} %add_convert_fusion.5), channel_id=1, replica_groups=mesh['dp'=4,'row'=4,'col'=2] {'row'}, dimensions={0}, use_global_device_ids=true | all-gather | bytes 1105920 | tf_op jit(solution)/shard_map/all_gather | solution.py:584
  151.4 8.8 %before.1 = (bf16[1152,538]{1,0:T(8,128)(2,1)}, f32[768,538]{1,0:T(8,128)}, bf16[1152,538]{1,0:T(8,128)(2,1)}) custom-call(s32[3]{0:T(128)} %pad_add_fusion.2.after_ref.place_ref, bf16[384,1152]{1,0:T(8,128)(2,1)} %copy-done.5, bf16[1152,1152]{1,0:T(8,128)(2,1)} %copy-done, bf16[768,1152]{1,0:T(8,128)(2,1)} %get-tuple-element.62.cot_ref, ...), custom_call_target="tpu_custom_call" | custom-call | tf_op jit(solution)/shard_map/before/pallas_call | solution.py:265
  160.2 9.5 %mlp.1 = (bf16[768,538]{1,0:T(8,128)(2,1)}, bf16[768,538]{1,0:T(8,128)(2,1)}, bf16[384,1152]{1,0:T(8,128)(2,1)}, bf16[384,1152]{1,0:T(8,128)(2,1)}, f32[1,538]{1,0:T(1,128)}) custom-call(s32[1]{0:T(128)} %bitcast.core_ref, bf16[768,1152]{1,0:T(8,128)(2,1)} %bitcast.66, bf16[1152,538]{1,0:T(8,128)(2,1)} %get-tuple-element.63.up_ref, ...), custom_call_target="tpu_custom_call" | custom-call | tf_op jit(solution)/shard_map/mlp/pallas_call | solution.py:351
  169.8 2.5 collective-permute-done.7
  178.6 10.2 %behind.1 = (bf16[4,288,1076]{2,1,0:T(8,128)(2,1)}, bf16[576,768]{1,0:T(8,128)(2,1)}, bf16[576,768]{1,0:T(8,128)(2,1)}) custom-call(s32[3]{0:T(128)} %pad_add_fusion.2.after_ref.place_ref, bf16[384,1152]{1,0:T(8,128)(2,1)} %add_convert_fusion.3.after_ref, bf16[768,1152]{1,0:T(8,128)(2,1)} %bitcast.67, bf16[768,538]{1,0:T(8,128)(2,1)} %get-tuple-element.67.hid_ref, ...), custom_call_target="tpu_custom_call" | custom-call | tf_op jit(solution)/shard_map/behind/pallas_call | solution.py:297
  188.9 4.6 %all-to-all-start.2 = ((bf16[4,288,1076]{2,1,0:T(8,128)(2,1)}), bf16[4,288,1076]{2,1,0:T(8,128)(2,1)}, u32[]{:S(2)}, u32[]{:S(2)}) async-start(bf16[4,288,1076]{2,1,0:T(8,128)(2,1)} %get-tuple-element.70), calls=%async_computation.3 | async-start | bytes 5308416 | tf_op jit(solution)/shard_map/all_to_all | solution.py:69
  195.3 4.2 %reduce-scatter.6.cloned.1.call-done = bf16[96,1152]{1,0:T(8,128)(2,1)} async-done(((bf16[384,1152]{1,0:T(8,128)(2,1)}), bf16[96,1152]{1,0:T(8,128)(2,1)}) %reduce-scatter.6.cloned.1.call-update) | async-done | bytes 221200 | tf_op jit(solution)/shard_map/reduce_scatter | solution.py:74
  201.9 18.8 %all_gather.63 = bf16[384,1152]{1,0:T(8,128)(2,1)S(1)} all-gather(bf16[96,1152]{1,0:T(8,128)(2,1)S(1)} %fusion.12), channel_id=1, replica_groups=mesh['dp'=4,'row'=4,'col'=2] {'row'}, dimensions={0}, use_global_device_ids=true | all-gather | bytes 1105920 | tf_op jit(solution)/shard_map/all_gather | solution.py:605
  224.4 2.6 all-gather.5
  228.3 3.4 add_reduce_fusion.after_ref
  231.7 10.7 %attend_back.1 = (bf16[432,768]{1,0:T(8,128)(2,1)}, f32[432,1]{1,0:T(8,128)}, bf16[4,288,576]{2,1,0:T(8,128)(2,1)}) custom-call(bf16[288,1076]{1,0:T(8,128)(2,1)} %add_reduce_fusion.after_ref, bf16[768,1152]{1,0:T(8,128)(2,1)} %bitcast.64, bf16[1152,576]{1,0:T(8,128)(2,1)} %get-tuple-element.59.w_ref, bf16[2,3,72,768]{3,2,1,0:T(8,128)(2,1)} %get-tuple-element.72.qkv_ref, ...), custom_call_target="tpu_custom_call" | custom-call | tf_op jit(solution)/shard_map/attend_back/pallas_call | solution.py:408
  242.4 6.7 %first_back.1 = (bf16[4,304,768]{2,1,0:T(8,128)(2,1)}, bf16[4,304,768]{2,1,0:T(8,128)(2,1)}, f32[1152,2]{1,0:T(8,128)}) custom-call(s32[1]{0:T(128)} %bitcast.core_ref, bf16[1152,432]{1,0:T(8,128)(2,1)} %get-tuple-element.60.w_ref, bf16[432,768]{1,0:T(8,128)(2,1)} %get-tuple-element.74.grad_ref, bf16[1152,768]{1,0:T(8,128)(2,1)} %bitcast.63, ...), custom_call_target="tpu_custom_call" | custom-call | tf_op jit(solution)/shard_map/first_back/pallas_call | solution.py:455
  249.2 4.0 %collective-permute-done.8 = bf16[4,304,768]{2,1,0:T(8,128)(2,1)S(1)} collective-permute-done((bf16[4,304,768]{2,1,0:T(8,128)(2,1)}, bf16[4,304,768]{2,1,0:T(8,128)(2,1)S(1)}, u32[]{:S(2)}, u32[]{:S(2)}) %collective-permute-start.8) | collective-permute-done | bytes 1867808 | tf_op jit(solution)/shard_map/ppermute | solution.py:39
  259.4 4.7 %all-to-all-start.3 = ((bf16[4,288,576]{2,1,0:T(8,128)(2,1)}), bf16[4,288,576]{2,1,0:T(8,128)(2,1)}, u32[]{:S(2)}, u32[]{:S(2)}) async-start(bf16[4,288,576]{2,1,0:T(8,128)(2,1)} %get-tuple-element.78), calls=%async_computation.6 | async-start | bytes 2949120 | tf_op jit(solution)/shard_map/all_to_all | solution.py:69
  265.1 6.6 %collective-permute-done.10 = f32[16,1152]{1,0:T(8,128)S(1)} collective-permute-done((f32[16,1152]{1,0:T(8,128)S(1)}, f32[16,1152]{1,0:T(8,128)S(1)}, u32[]{:S(2)}, u32[]{:S(2)}) %collective-permute-start.10) | collective-permute-done | bytes 73760 | tf_op jit(solution)/shard_map/ppermute | solution.py:86
  272.6 10.1 %collective-permute-done.11 = f32[16,1152]{1,0:T(8,128)S(1)} collective-permute-done((f32[16,1152]{1,0:T(8,128)S(1)}, f32[16,1152]{1,0:T(8,128)S(1)}, u32[]{:S(2)}, u32[]{:S(2)}) %collective-permute-start.11) | collective-permute-done | bytes 73760 | tf_op jit(solution)/shard_map/ppermute | solution.py:86
  284.6 2.9 fusion.26
  292.2 4.0 %all-to-all-start.4 = ((bf16[4,72,1652]{2,1,0:T(8,128)(2,1)}), bf16[4,72,1652]{2,1,0:T(8,128)(2,1)S(1)}, u32[]{:S(2)}, u32[]{:S(2)}) async-start(bf16[4,72,1652]{2,1,0:T(8,128)(2,1)} %pad_maximum_fusion.3), calls=%async_computation.7 | async-start | bytes 1916928 | tf_op jit(solution)/shard_map/all_to_all | solution.py:65
  299.7 22.2 %all-to-all-done.4.blocks_ref = bf16[4,72,1652]{2,1,0:T(8,128)(2,1)S(1)} async-done(((bf16[4,72,1652]{2,1,0:T(8,128)(2,1)}), bf16[4,72,1652]{2,1,0:T(8,128)(2,1)S(1)}, u32[]{:S(2)}, u32[]{:S(2)}) %all-to-all-start.4) | async-done | bytes 951584 | tf_op jit(solution)/shard_map/all_to_all | solution.py:65
  322.9 8.8 %adam.1 = (f32[72,1,1728]{2,1,0:T(1,128)}, f32[72,1,1728]{2,1,0:T(1,128)}, f32[72,1,1728]{2,1,0:T(1,128)}, f32[72,1,576]{2,1,0:T(1,128)}, f32[72,1,576]{2,1,0:T(...) custom-call(bf16[4,304,768]{2,1,0:T(8,128)(2,1)} %copy-done.2, ...), custom_call_target="tpu_custom_call" | custom-call | tf_op jit(solution)/shard_map/adam/pallas_call | solution.py:138
  (238 shorter events, 74.5 us)
Async XLA Ops:
  11.2 7.0 %copy-start.20 = (f32[11216]{0:T(1024)S(1)}, f32[11216]{0:T(1024)}, u32[]{:S(2)}) copy-start(f32[11216]{0:T(1024)} %param.37) | copy-start | bytes 134596
  11.2 18.8 %copy-start.14 = (bf16[729,144]{0,1:T(8,128)(2,1)S(1)}, bf16[729,144]{0,1:T(8,128)(2,1)}, u32[]{:S(2)}) copy-start(bf16[729,144]{0,1:T(8,128)(2,1)} %param.20) | copy-start | bytes 629860
  11.2 17.6 %all-to-all-start = ((bf16[4,72,576]{2,1,0:T(8,128)(2,1)}), bf16[4,72,576]{2,1,0:T(8,128)(2,1)S(1)}, u32[]{:S(2)}, u32[]{:S(2)}) async-start(bf16[4,72,576]{2,1,0:T(8,128)(2,1)} %prepare.2), calls=%async_computation | async-start | bytes 737280 | tf_op jit(solution)/shard_map/all_to_all | solution.py:65
  18.2 60.9 %copy-start = (bf16[1152,1152]{1,0:T(8,128)(2,1)}, bf16[1152,1152]{1,0:T(8,128)(2,1)S(1)}, u32[]{:S(2)}) copy-start(bf16[1152,1152]{1,0:T(8,128)(2,1)S(1)} %fusion.order_ref) | copy-start | bytes 7962628
  28.8 20.5 %copy-start.13 = (bf16[4,72,576]{2,1,0:T(8,128)(2,1)}, bf16[4,72,576]{2,1,0:T(8,128)(2,1)S(1)}, u32[]{:S(2)}) copy-start(bf16[4,72,576]{2,1,0:T(8,128)(2,1)S(1)} %all-to-all-done) | copy-start | bytes 995332
  49.3 7.8 %copy-start.25 = (f32[2,1152]{1,0:T(2,128)S(1)}, f32[2,1152]{1,0:T(2,128)}, u32[]{:S(2)}) copy-start(f32[2,1152]{1,0:T(2,128)} %param.34) | copy-start | bytes 27652
  49.3 19.0 %copy-start.4 = (bf16[576,768]{1,0:T(8,128)(2,1)S(1)}, bf16[576,768]{1,0:T(8,128)(2,1)}, u32[]{:S(2)}) copy-start(bf16[576,768]{1,0:T(8,128)(2,1)} %all_gather.51.after_ref) | copy-start | bytes 2654212
  52.8 18.7 %all-to-all-start.1 = ((bf16[4,72,1076]{2,1,0:T(8,128)(2,1)}), bf16[4,72,1076]{2,1,0:T(8,128)(2,1)}, u32[]{:S(2)}, u32[]{:S(2)}) async-start(bf16[4,72,1076]{2,1,0:T(8,128)(2,1)} %prepare.3), calls=%async_computation.1 | async-start | bytes 1327104 | tf_op jit(solution)/shard_map/all_to_all | solution.py:65
  57.0 46.2 %all-gather.9.cloned.1.call-start = ((), (), s32[]{:S(2)}) async-start(), calls=%async_computation.11 | async-start | bytes 1990656 | tf_op jit(solution)/shard_map/all_gather | solution.py:548
  64.8 18.4 %collective-permute-start = (bf16[288,576]{1,0:T(8,128)(2,1)}, bf16[288,576]{1,0:T(8,128)(2,1)}, u32[]{:S(2)}, u32[]{:S(2)}) collective-permute-start(bf16[288,576]{1,0:T(8,128)(2,1)} %bitcast.83), channel_id=1, source_target_pairs={{0,8},{8,0},{16,24},{24,16},{1,9},{9,1},{17,25},{25,17},{2,10},{10... | collective-permute-start | bytes 995336 | tf_op jit(solution)/shard_map/ppermute | solution.py:55
  66.3 16.9 %collective-permute-start.1 = (bf16[288,576]{1,0:T(8,128)(2,1)}, bf16[288,576]{1,0:T(8,128)(2,1)}, u32[]{:S(2)}, u32[]{:S(2)}) collective-permute-start(bf16[288,576]{1,0:T(8,128)(2,1)} %bitcast.84), channel_id=1, source_target_pairs={{0,16},{8,24},{16,0},{24,8},{1,17},{9,25},{17,1},{25,9},{2,18},{10... | collective-permute-start | bytes 995336 | tf_op jit(solution)/shard_map/ppermute | solution.py:55
  67.8 15.4 %collective-permute-start.2 = (bf16[288,576]{1,0:T(8,128)(2,1)}, bf16[288,576]{1,0:T(8,128)(2,1)}, u32[]{:S(2)}, u32[]{:S(2)}) collective-permute-start(bf16[288,576]{1,0:T(8,128)(2,1)} %bitcast.85), channel_id=1, source_target_pairs={{0,24},{8,16},{16,8},{24,0},{1,25},{9,17},{17,9},{25,1},{2,26},{10... | collective-permute-start | bytes 995336 | tf_op jit(solution)/shard_map/ppermute | solution.py:55
  75.1 48.4 %reduce-scatter.4.cloned.1.call-start = ((), (), s32[]{:S(2)}) async-start(), calls=%async_computation.8 | async-start | bytes 1105920 | tf_op jit(solution)/shard_map/reduce_scatter | solution.py:74
  92.4 2.6 collective-permute-start.3
  97.4 102.0 %reduce-scatter.6.cloned.1.call-start = ((), (), s32[]{:S(2)}) async-start(), calls=%async_computation.9 | async-start | bytes 1105920 | tf_op jit(solution)/shard_map/reduce_scatter | solution.py:74
  99.7 50.3 %collective-permute-start.4 = (bf16[288,1076]{1,0:T(8,128)(2,1)}, bf16[288,1076]{1,0:T(8,128)(2,1)S(1)}, u32[]{:S(2)}, u32[]{:S(2)}) collective-permute-start(bf16[288,1076]{1,0:T(8,128)(2,1)} %bitcast.8.after_ref.refs_0_), channel_id=1, source_target_pairs={{0,8},{8,0},{16,24},{24,16},{1,9},{9,1},{17,25},{25,17},{2,10},{10... | collective-permute-start | bytes 1859336 | tf_op jit(solution)/shard_map/ppermute | solution.py:55
  101.2 48.9 %collective-permute-start.5 = (bf16[288,1076]{1,0:T(8,128)(2,1)}, bf16[288,1076]{1,0:T(8,128)(2,1)S(1)}, u32[]{:S(2)}, u32[]{:S(2)}) collective-permute-start(bf16[288,1076]{1,0:T(8,128)(2,1)} %bitcast.8.after_ref.refs_0_), channel_id=1, source_target_pairs={{0,16},{8,24},{16,0},{24,8},{1,17},{9,25},{17,1},{25,9},{2,18},{10... | collective-permute-start | bytes 1859336 | tf_op jit(solution)/shard_map/ppermute | solution.py:55
  102.7 47.4 %collective-permute-start.6 = (bf16[288,1076]{1,0:T(8,128)(2,1)}, bf16[288,1076]{1,0:T(8,128)(2,1)S(1)}, u32[]{:S(2)}, u32[]{:S(2)}) collective-permute-start(bf16[288,1076]{1,0:T(8,128)(2,1)} %bitcast.8.after_ref.refs_0_), channel_id=1, source_target_pairs={{0,24},{8,16},{16,8},{24,0},{1,25},{9,17},{17,9},{25,1},{2,26},{10... | collective-permute-start | bytes 1859336 | tf_op jit(solution)/shard_map/ppermute | solution.py:55
  169.7 2.7 collective-permute-start.7
  188.9 39.5 %all-to-all-start.2 = ((bf16[4,288,1076]{2,1,0:T(8,128)(2,1)}), bf16[4,288,1076]{2,1,0:T(8,128)(2,1)}, u32[]{:S(2)}, u32[]{:S(2)}) async-start(bf16[4,288,1076]{2,1,0:T(8,128)(2,1)} %get-tuple-element.70), calls=%async_computation.3 | async-start | bytes 5308416 | tf_op jit(solution)/shard_map/all_to_all | solution.py:69
  193.4 138.3 %reduce-scatter.8.cloned.1.call-start = ((), (), s32[]{:S(2)}) async-start(), calls=%async_computation.10 | async-start | bytes 2334720 | tf_op jit(solution)/shard_map/reduce_scatter | solution.py:74
  249.1 4.0 %collective-permute-start.8 = (bf16[4,304,768]{2,1,0:T(8,128)(2,1)}, bf16[4,304,768]{2,1,0:T(8,128)(2,1)S(1)}, u32[]{:S(2)}, u32[]{:S(2)}) collective-permute-start(bf16[4,304,768]{2,1,0:T(8,128)(2,1)} %get-tuple-element.77), channel_id=1, source_target_pairs={{0,1},{1,0},{2,3},{3,2},{4,5},{5,4},{6,7},{7,6},{8,9},{9,8},{10,11... | collective-permute-start | bytes 5603336 | tf_op jit(solution)/shard_map/ppermute | solution.py:39
  259.1 5.0 %collective-permute-start.9 = (f32[16,1152]{1,0:T(8,128)S(1)}, f32[16,1152]{1,0:T(8,128)S(1)}, u32[]{:S(2)}, u32[]{:S(2)}) collective-permute-start(f32[16,1152]{1,0:T(8,128)S(1)} %fusion.32), channel_id=1, source_target_pairs={{0,1},{1,0},{2,3},{3,2},{4,5},{5,4},{6,7},{7,6},{8,9},{9,8},{10,11... | collective-permute-start | bytes 221192 | tf_op jit(solution)/shard_map/ppermute | solution.py:86
  259.3 12.4 %copy-start.15 = (bf16[729,144]{0,1:T(8,128)(2,1)S(1)}, bf16[729,144]{0,1:T(8,128)(2,1)}, u32[]{:S(2)}) copy-start(bf16[729,144]{0,1:T(8,128)(2,1)} %param.20) | copy-start | bytes 629860
  259.4 28.2 %all-to-all-start.3 = ((bf16[4,288,576]{2,1,0:T(8,128)(2,1)}), bf16[4,288,576]{2,1,0:T(8,128)(2,1)}, u32[]{:S(2)}, u32[]{:S(2)}) async-start(bf16[4,288,576]{2,1,0:T(8,128)(2,1)} %get-tuple-element.78), calls=%async_computation.6 | async-start | bytes 2949120 | tf_op jit(solution)/shard_map/all_to_all | solution.py:69
  264.1 7.6 %collective-permute-start.10 = (f32[16,1152]{1,0:T(8,128)S(1)}, f32[16,1152]{1,0:T(8,128)S(1)}, u32[]{:S(2)}, u32[]{:S(2)}) collective-permute-start(f32[16,1152]{1,0:T(8,128)S(1)} %fusion.73), channel_id=1, source_target_pairs={{0,2},{2,0},{4,6},{6,4},{1,3},{3,1},{5,7},{7,5},{8,10},{10,8},{12,... | collective-permute-start | bytes 221192 | tf_op jit(solution)/shard_map/ppermute | solution.py:86
  271.7 11.0 %collective-permute-start.11 = (f32[16,1152]{1,0:T(8,128)S(1)}, f32[16,1152]{1,0:T(8,128)S(1)}, u32[]{:S(2)}, u32[]{:S(2)}) collective-permute-start(f32[16,1152]{1,0:T(8,128)S(1)} %add.394), channel_id=1, source_target_pairs={{0,4},{2,6},{4,0},{6,2},{1,5},{3,7},{5,1},{7,3},{8,12},{10,14},{12... | collective-permute-start | bytes 221192 | tf_op jit(solution)/shard_map/ppermute | solution.py:86
  282.7 8.2 %copy-start.6 = (bf16[288,1076]{1,0:T(8,128)(2,1)S(1)}, bf16[288,1076]{1,0:T(8,128)(2,1)}, u32[]{:S(2)}) copy-start(bf16[288,1076]{1,0:T(8,128)(2,1)} %add_reduce_fusion.after_ref) | copy-start | bytes 1859332
  282.7 6.7 %collective-permute-start.12 = (f32[16,1152]{1,0:T(8,128)S(1)}, f32[16,1152]{1,0:T(8,128)S(1)}, u32[]{:S(2)}, u32[]{:S(2)}) collective-permute-start(f32[16,1152]{1,0:T(8,128)S(1)} %add.395), channel_id=1, source_target_pairs={{0,8},{8,0},{16,24},{24,16},{1,9},{9,1},{17,25},{25,17},{2,10},{10... | collective-permute-start | bytes 221192 | tf_op jit(solution)/shard_map/ppermute | solution.py:86
  289.4 6.9 %collective-permute-start.13 = (f32[16,1152]{1,0:T(8,128)S(1)}, f32[16,1152]{1,0:T(8,128)S(1)}, u32[]{:S(2)}, u32[]{:S(2)}) collective-permute-start(f32[16,1152]{1,0:T(8,128)S(1)} %add.396), channel_id=1, source_target_pairs={{0,16},{8,24},{16,0},{24,8},{1,17},{9,25},{17,1},{25,9},{2,18},{10... | collective-permute-start | bytes 221192 | tf_op jit(solution)/shard_map/ppermute | solution.py:86
  292.1 6.9 %copy-start.22 = (f32[11216]{0:T(1024)S(1)}, f32[11216]{0:T(1024)}, u32[]{:S(2)}) copy-start(f32[11216]{0:T(1024)} %param.38) | copy-start | bytes 134596
  292.2 29.7 %all-to-all-start.4 = ((bf16[4,72,1652]{2,1,0:T(8,128)(2,1)}), bf16[4,72,1652]{2,1,0:T(8,128)(2,1)S(1)}, u32[]{:S(2)}, u32[]{:S(2)}) async-start(bf16[4,72,1652]{2,1,0:T(8,128)(2,1)} %pad_maximum_fusion.3), calls=%async_computation.7 | async-start | bytes 1916928 | tf_op jit(solution)/shard_map/all_to_all | solution.py:65
  (26 other events, 92.6 us)
Sparse Core Ops, SparseCore 0:
  75.2 27.7 all-gather.8
Sparse Core Ops, SparseCore 1:
  97.5 25.9 reduce-scatter.3
  174.9 24.4 reduce-scatter.5
  259.4 46.8 reduce-scatter.7

commit v8 on v7

--- a/solution.py
+++ b/solution.py
@@ -648,7 +648,7 @@
     )
     own_row = jnp.pad(own_row, (0, D - own_row.shape[0]))
     own_rows = jnp.where(jnp.arange(group)[:, None] == own, own_row[None, :], 0.0)
-    total = all_sum(jnp.concatenate([jnp.pad(all_rows, ((0, 2), (0, 0))), own_rows]) + later)
+    total = all_sum(jnp.concatenate([jnp.pad(all_rows, ((0, 2), (0, 0))), own_rows]) + zero_of(first_rows))
     one_rows = total[:2].reshape(2, n_col, n_row, width).transpose(0, 2, 1, 3).reshape(2, D)
     two_rows = total[2:6].reshape(4, n_dp, D // n_dp).transpose(0, 2, 1).reshape(4, D)
     own_rows = total[8:]

time: 348 us -> 371 us (1.066)
  starting transfers between devices: 35.9 us -> 46.9 us
  waiting for transfers between devices: 72.2 us -> 82.4 us
    all_to_all x2, waiting for transfers between devices: 0.01 us -> 18.9 us  [sum_blocks(): blocks = lax.all_to_all(blocks, axis, 0, 0)]
    reduce_scatter x3, waiting for transfers between devices: 15.1 us -> 3.26 us  [sum_over_rows(): lax.psum_scatter(half.astype(LOW), 'row', scatter_dimension=0, tiled=True)]
    reduce_scatter x3, starting transfers between devices: 0.66 us -> 12 us  [sum_over_rows(): lax.psum_scatter(half.astype(LOW), 'row', scatter_dimension=0, tiled=True)]
    all_to_all x3, waiting for transfers between devices: 31.3 us -> 40.3 us  [exchange_rows(): return lax.all_to_all(blocks, 'row', 0, 0)]
    ppermute x3, waiting for transfers between devices: 8.99 us -> 5.02 us  [swap_cores(): lax.ppermute(array, 'col', [(i, (i + 1) % n_col) for i in range(n_col)])]
  transfers between devices with their start and end apart: 23 -> 23, of which waited for: 9 -> 11; matrix products, arithmetic and copies ran while one was open for 13% -> 13% of each run, Pallas kernels for 11% -> 10%
where the time goes in v8:
time: 371 us; the launch traced here: 367 us
  waiting for transfers between devices  82.4 us (22%)
  Pallas kernels  79.2 us (21%)
  blocking collectives  74.1 us (20%)
  starting transfers between devices  46.9 us (13%)
  other arithmetic  32.1 us (9%)
  local copies, waits for them, and re-layouts  23.9 us (6%)
  between operations  20.8 us (6%)
  matrix products  7.73 us (2%)
    all_to_all x3, waiting for transfers between devices, exchange_rows(): return lax.all_to_all(blocks, 'row', 0, 0)  40.3 us
    all_gather x1, blocking collectives, shards(): zb_rows = lax.all_gather(zb, 'row', axis=0, tiled=True)  20.5 us
    all_gather x1, blocking collectives, shards(): x_rows = lax.all_gather(x_after, 'row', axis=0, tiled=True)  19.2 us
    all_to_all x2, waiting for transfers between devices, sum_blocks(): blocks = lax.all_to_all(blocks, axis, 0, 0)  18.9 us
    all_gather x1, blocking collectives, shards(): branch_rows = lax.all_gather(middle_grad, 'row', axis=0, tiled=True)  18.8 us
    all_gather x6, blocking collectives, both_cores(): lax.all_gather(piece, 'col', axis=0)  15.6 us
    ppermute x5, waiting for transfers between devices, all_sum(): lax.ppermute(vector, axis, [(i, i ^ step) for i in range(size)])  14.9 us
    all_to_all x3, starting transfers between devices, exchange_rows(): return lax.all_to_all(blocks, 'row', 0, 0)  14.3 us
  transfers between devices with their start and end apart: 23, of which 11 were waited for; matrix products, arithmetic and copies ran while one was open for 13% of the time, Pallas kernels for 10%

profile of v8, /device:TPU:0, one launch (start us, length us, event | category | flops | bytes accessed | tf_op | source)
XLA Modules:
  0.0 367.1 jit_solution(2693197632701593384)
XLA Ops:
  8.6 2.6 prepare.2
  11.2 6.4 %all-to-all-start = ((bf16[4,72,576]{2,1,0:T(8,128)(2,1)}), bf16[4,72,576]{2,1,0:T(8,128)(2,1)S(1)}, u32[]{:S(2)}, u32[]{:S(2)}) async-start(bf16[4,72,576]{2,1,0:T(8,128)(2,1)} %prepare.2), calls=%async_computation | async-start | bytes 737280 | tf_op jit(solution)/shard_map/all_to_all | solution.py:65
  19.7 9.1 %all-to-all-done = bf16[4,72,576]{2,1,0:T(8,128)(2,1)S(1)} async-done(((bf16[4,72,576]{2,1,0:T(8,128)(2,1)}), bf16[4,72,576]{2,1,0:T(8,128)(2,1)S(1)}, u32[]{:S(2)}, u32[]{:S(2)}) %all-to-all-start) | async-done | bytes 331808 | tf_op jit(solution)/shard_map/all_to_all | solution.py:65
  30.1 19.2 %all_gather.51.after_ref = bf16[576,768]{1,0:T(8,128)(2,1)} all-gather(bf16[144,768]{1,0:T(8,128)(2,1)S(1)} %pad_add_fusion.1), channel_id=1, replica_groups=mesh['dp'=4,'row'=4,'col'=2] {'row'}, dimensions={0}, use_global_device_ids=true | all-gather | bytes 1105920 | tf_op jit(solution)/shard_map/all_gather | solution.py:541
  49.3 3.5 prepare.3
  52.8 4.2 %all-to-all-start.1 = ((bf16[4,72,1076]{2,1,0:T(8,128)(2,1)}), bf16[4,72,1076]{2,1,0:T(8,128)(2,1)}, u32[]{:S(2)}, u32[]{:S(2)}) async-start(bf16[4,72,1076]{2,1,0:T(8,128)(2,1)} %prepare.3), calls=%async_computation.1 | async-start | bytes 1327104 | tf_op jit(solution)/shard_map/all_to_all | solution.py:65
  74.5 3.0 all-gather
  78.6 4.0 %fusion.3.za_ref = bf16[1152,768]{1,0:T(8,128)(2,1)} fusion(bf16[1152,1152]{1,0:T(8,128)(2,1)S(1)} %fusion.order_ref, bf16[1152,768]{1,0:T(8,128)(2,1)S(1)} %bitcast.62, f32[1152]{0:T(1024)S(1)} %copy-done.31, f32[1152]{0:T(1024)S(1)} %copy-done.32, f32[768]{0:T(1024)S(1)} %add_rsqrt_fusion, f32[768]{0:T(1024)S(1)} %broadcast_multiply_fusion), kind=kOutput, calls=%fused_computation.9 | convolution fusion | flops 2043740160 | bytes 6208512 | tf_op jit(solution)/shard_map/dot_general | solution.py:24
  82.6 9.1 %attend.1 = (bf16[1152,576]{1,0:T(8,128)(2,1)}, bf16[2,3,72,768]{3,2,1,0:T(8,128)(2,1)}, bf16[768,144]{1,0:T(8,128)(2,1)}, bf16[384,1152]{1,0:T(8,128)(2,1)}, bf16[384,1152]{1,0:T(8,128)(2,1)}) custom-call(s32[3]{0:T(128)} %pad_add_fusion.2.after_ref.place_ref, bf16[288,1076]{1,0:T(8,128)(2,1)} %bitcast.8.after_ref.refs_0_, bf16[1152,768]{1,0:T(8,128)(2,1)} %fusion.3.za_ref, ...), custom_call_target="tpu_custom_call" | custom-call | tf_op jit(solution)/shard_map/attend/pallas_call | solution.py:202
  91.9 2.5 collective-permute-done.3
  96.8 11.7 %reduce-scatter.6.cloned.1.call-start = ((), (), s32[]{:S(2)}) async-start(), calls=%async_computation.9 | async-start | bytes 1105920 | tf_op jit(solution)/shard_map/reduce_scatter | solution.py:74
  114.5 9.2 %beside.1 = (bf16[768,1152]{1,0:T(8,128)(2,1)}, bf16[1152,432]{1,0:T(8,128)(2,1)}, f32[96,1152]{1,0:T(8,128)}) custom-call(s32[3]{0:T(128)} %pad_add_fusion.2.after_ref.place_ref, bf16[384,1152]{1,0:T(8,128)(2,1)} %add_convert_fusion.4.after_ref, bf16[1152,1152]{1,0:T(8,128)(2,1)} %copy-done, bf16[8,144,768]{2,1,0:T(8,128)(2,1)} %bitcast.82, ...), custom_call_target="tpu_custom_call" | custom-call | tf_op jit(solution)/shard_map/beside/pallas_call | solution.py:238
  125.3 20.5 %all_gather.58.after_ref = bf16[384,1152]{1,0:T(8,128)(2,1)S(1)} all-gather(bf16[96,1152]{1,0:T(8,128)(2,1)S(1)} %add_convert_fusion.5), channel_id=1, replica_groups=mesh['dp'=4,'row'=4,'col'=2] {'row'}, dimensions={0}, use_global_device_ids=true | all-gather | bytes 1105920 | tf_op jit(solution)/shard_map/all_gather | solution.py:584
  153.5 8.8 %before.1 = (bf16[1152,538]{1,0:T(8,128)(2,1)}, f32[768,538]{1,0:T(8,128)}, bf16[1152,538]{1,0:T(8,128)(2,1)}) custom-call(s32[3]{0:T(128)} %pad_add_fusion.2.after_ref.place_ref, bf16[384,1152]{1,0:T(8,128)(2,1)} %copy-done.5, bf16[1152,1152]{1,0:T(8,128)(2,1)} %copy-done, bf16[768,1152]{1,0:T(8,128)(2,1)} %get-tuple-element.62.cot_ref, ...), custom_call_target="tpu_custom_call" | custom-call | tf_op jit(solution)/shard_map/before/pallas_call | solution.py:265
  162.3 9.5 %mlp.1 = (bf16[768,538]{1,0:T(8,128)(2,1)}, bf16[768,538]{1,0:T(8,128)(2,1)}, bf16[384,1152]{1,0:T(8,128)(2,1)}, bf16[384,1152]{1,0:T(8,128)(2,1)}, f32[1,538]{1,0:T(1,128)}) custom-call(s32[1]{0:T(128)} %bitcast.core_ref, bf16[768,1152]{1,0:T(8,128)(2,1)} %bitcast.67, bf16[1152,538]{1,0:T(8,128)(2,1)} %get-tuple-element.63.up_ref, ...), custom_call_target="tpu_custom_call" | custom-call | tf_op jit(solution)/shard_map/mlp/pallas_call | solution.py:351
  171.9 2.5 collective-permute-done.7
  180.6 10.3 %behind.1 = (bf16[4,288,1076]{2,1,0:T(8,128)(2,1)}, bf16[576,768]{1,0:T(8,128)(2,1)}, bf16[576,768]{1,0:T(8,128)(2,1)}) custom-call(s32[3]{0:T(128)} %pad_add_fusion.2.after_ref.place_ref, bf16[384,1152]{1,0:T(8,128)(2,1)} %add_convert_fusion.3.after_ref, bf16[768,1152]{1,0:T(8,128)(2,1)} %bitcast.68, bf16[768,538]{1,0:T(8,128)(2,1)} %get-tuple-element.67.hid_ref, ...), custom_call_target="tpu_custom_call" | custom-call | tf_op jit(solution)/shard_map/behind/pallas_call | solution.py:297
  190.9 4.6 %all-to-all-start.2 = ((bf16[4,288,1076]{2,1,0:T(8,128)(2,1)}), bf16[4,288,1076]{2,1,0:T(8,128)(2,1)}, u32[]{:S(2)}, u32[]{:S(2)}) async-start(bf16[4,288,1076]{2,1,0:T(8,128)(2,1)} %get-tuple-element.70), calls=%async_computation.3 | async-start | bytes 5308416 | tf_op jit(solution)/shard_map/all_to_all | solution.py:69
  197.3 3.2 reduce-scatter.6.cloned.1.call-done
  203.0 18.8 %all_gather.63 = bf16[384,1152]{1,0:T(8,128)(2,1)S(1)} all-gather(bf16[96,1152]{1,0:T(8,128)(2,1)S(1)} %fusion.12), channel_id=1, replica_groups=mesh['dp'=4,'row'=4,'col'=2] {'row'}, dimensions={0}, use_global_device_ids=true | all-gather | bytes 1105920 | tf_op jit(solution)/shard_map/all_gather | solution.py:605
  225.5 2.8 all-gather.5
  229.7 3.3 add_reduce_fusion.after_ref
  233.0 10.7 %attend_back.1 = (bf16[432,768]{1,0:T(8,128)(2,1)}, f32[432,1]{1,0:T(8,128)}, bf16[4,288,576]{2,1,0:T(8,128)(2,1)}) custom-call(bf16[288,1076]{1,0:T(8,128)(2,1)} %add_reduce_fusion.after_ref, bf16[768,1152]{1,0:T(8,128)(2,1)} %bitcast.65, bf16[1152,576]{1,0:T(8,128)(2,1)} %get-tuple-element.59.w_ref, bf16[2,3,72,768]{3,2,1,0:T(8,128)(2,1)} %get-tuple-element.72.qkv_ref, ...), custom_call_target="tpu_custom_call" | custom-call | tf_op jit(solution)/shard_map/attend_back/pallas_call | solution.py:408
  243.8 6.7 %first_back.1 = (bf16[4,304,768]{2,1,0:T(8,128)(2,1)}, bf16[4,304,768]{2,1,0:T(8,128)(2,1)}, f32[1152,2]{1,0:T(8,128)}) custom-call(s32[1]{0:T(128)} %bitcast.core_ref, bf16[1152,432]{1,0:T(8,128)(2,1)} %get-tuple-element.60.w_ref, bf16[432,768]{1,0:T(8,128)(2,1)} %get-tuple-element.74.grad_ref, bf16[1152,768]{1,0:T(8,128)(2,1)} %bitcast.64, ...), custom_call_target="tpu_custom_call" | custom-call | tf_op jit(solution)/shard_map/first_back/pallas_call | solution.py:455
  250.6 4.3 %all-to-all-start.3 = ((bf16[4,288,576]{2,1,0:T(8,128)(2,1)}), bf16[4,288,576]{2,1,0:T(8,128)(2,1)}, u32[]{:S(2)}, u32[]{:S(2)}) async-start(bf16[4,288,576]{2,1,0:T(8,128)(2,1)} %get-tuple-element.78), calls=%async_computation.6 | async-start | bytes 2949120 | tf_op jit(solution)/shard_map/all_to_all | solution.py:69
  255.1 18.9 %all-to-all-done.3 = bf16[4,288,576]{2,1,0:T(8,128)(2,1)} async-done(((bf16[4,288,576]{2,1,0:T(8,128)(2,1)}), bf16[4,288,576]{2,1,0:T(8,128)(2,1)}, u32[]{:S(2)}, u32[]{:S(2)}) %all-to-all-start.3) | async-done | bytes 1327136 | tf_op jit(solution)/shard_map/all_to_all | solution.py:69
  278.4 2.6 add_convert_fusion.after_ref
  287.7 2.9 collective-permute-done.10
  291.7 9.9 %collective-permute-done.11 = f32[16,1152]{1,0:T(8,128)S(1)} collective-permute-done((f32[16,1152]{1,0:T(8,128)S(1)}, f32[16,1152]{1,0:T(8,128)S(1)}, u32[]{:S(2)}, u32[]{:S(2)}) %collective-permute-start.11) | collective-permute-done | bytes 73760 | tf_op jit(solution)/shard_map/ppermute | solution.py:86
  308.9 3.7 %all-to-all-start.4 = ((bf16[4,72,1652]{2,1,0:T(8,128)(2,1)}), bf16[4,72,1652]{2,1,0:T(8,128)(2,1)S(1)}, u32[]{:S(2)}, u32[]{:S(2)}) async-start(bf16[4,72,1652]{2,1,0:T(8,128)(2,1)} %pad_maximum_fusion.3), calls=%async_computation.7 | async-start | bytes 1916928 | tf_op jit(solution)/shard_map/all_to_all | solution.py:65
  316.1 30.5 %all-to-all-done.4.blocks_ref = bf16[4,72,1652]{2,1,0:T(8,128)(2,1)S(1)} async-done(((bf16[4,72,1652]{2,1,0:T(8,128)(2,1)}), bf16[4,72,1652]{2,1,0:T(8,128)(2,1)S(1)}, u32[]{:S(2)}, u32[]{:S(2)}) %all-to-all-start.4) | async-done | bytes 951584 | tf_op jit(solution)/shard_map/all_to_all | solution.py:65
  347.6 8.8 %adam.1 = (f32[72,1,1728]{2,1,0:T(1,128)}, f32[72,1,1728]{2,1,0:T(1,128)}, f32[72,1,1728]{2,1,0:T(1,128)}, f32[72,1,576]{2,1,0:T(1,128)}, f32[72,1,576]{2,1,0:T(...) custom-call(bf16[4,304,768]{2,1,0:T(8,128)(2,1)} %copy-done.2, ...), custom_call_target="tpu_custom_call" | custom-call | tf_op jit(solution)/shard_map/adam/pallas_call | solution.py:138
  (241 shorter events, 78.2 us)
Async XLA Ops:
  11.2 18.8 %copy-start.13 = (bf16[729,144]{0,1:T(8,128)(2,1)S(1)}, bf16[729,144]{0,1:T(8,128)(2,1)}, u32[]{:S(2)}) copy-start(bf16[729,144]{0,1:T(8,128)(2,1)} %param.20) | copy-start | bytes 629860
  11.2 17.6 %all-to-all-start = ((bf16[4,72,576]{2,1,0:T(8,128)(2,1)}), bf16[4,72,576]{2,1,0:T(8,128)(2,1)S(1)}, u32[]{:S(2)}, u32[]{:S(2)}) async-start(bf16[4,72,576]{2,1,0:T(8,128)(2,1)} %prepare.2), calls=%async_computation | async-start | bytes 737280 | tf_op jit(solution)/shard_map/all_to_all | solution.py:65
  18.2 60.3 %copy-start = (bf16[1152,1152]{1,0:T(8,128)(2,1)}, bf16[1152,1152]{1,0:T(8,128)(2,1)S(1)}, u32[]{:S(2)}) copy-start(bf16[1152,1152]{1,0:T(8,128)(2,1)S(1)} %fusion.order_ref) | copy-start | bytes 7962628
  28.8 20.5 %copy-start.11 = (bf16[4,72,576]{2,1,0:T(8,128)(2,1)}, bf16[4,72,576]{2,1,0:T(8,128)(2,1)S(1)}, u32[]{:S(2)}) copy-start(bf16[4,72,576]{2,1,0:T(8,128)(2,1)S(1)} %all-to-all-done) | copy-start | bytes 995332
  49.3 17.8 %copy-start.4 = (bf16[576,768]{1,0:T(8,128)(2,1)S(1)}, bf16[576,768]{1,0:T(8,128)(2,1)}, u32[]{:S(2)}) copy-start(bf16[576,768]{1,0:T(8,128)(2,1)} %all_gather.51.after_ref) | copy-start | bytes 2654212
  52.8 18.1 %all-to-all-start.1 = ((bf16[4,72,1076]{2,1,0:T(8,128)(2,1)}), bf16[4,72,1076]{2,1,0:T(8,128)(2,1)}, u32[]{:S(2)}, u32[]{:S(2)}) async-start(bf16[4,72,1076]{2,1,0:T(8,128)(2,1)} %prepare.3), calls=%async_computation.1 | async-start | bytes 1327104 | tf_op jit(solution)/shard_map/all_to_all | solution.py:65
  57.0 57.5 %all-gather.9.cloned.1.call-start = ((), (), s32[]{:S(2)}) async-start(), calls=%async_computation.11 | async-start | bytes 1990656 | tf_op jit(solution)/shard_map/all_gather | solution.py:548
  63.6 19.1 %collective-permute-start = (bf16[288,576]{1,0:T(8,128)(2,1)}, bf16[288,576]{1,0:T(8,128)(2,1)}, u32[]{:S(2)}, u32[]{:S(2)}) collective-permute-start(bf16[288,576]{1,0:T(8,128)(2,1)} %bitcast.84), channel_id=1, source_target_pairs={{0,8},{8,0},{16,24},{24,16},{1,9},{9,1},{17,25},{25,17},{2,10},{10... | collective-permute-start | bytes 995336 | tf_op jit(solution)/shard_map/ppermute | solution.py:55
  65.0 17.6 %collective-permute-start.1 = (bf16[288,576]{1,0:T(8,128)(2,1)}, bf16[288,576]{1,0:T(8,128)(2,1)}, u32[]{:S(2)}, u32[]{:S(2)}) collective-permute-start(bf16[288,576]{1,0:T(8,128)(2,1)} %bitcast.85), channel_id=1, source_target_pairs={{0,16},{8,24},{16,0},{24,8},{1,17},{9,25},{17,1},{25,9},{2,18},{10... | collective-permute-start | bytes 995336 | tf_op jit(solution)/shard_map/ppermute | solution.py:55
  66.6 16.1 %collective-permute-start.2 = (bf16[288,576]{1,0:T(8,128)(2,1)}, bf16[288,576]{1,0:T(8,128)(2,1)}, u32[]{:S(2)}, u32[]{:S(2)}) collective-permute-start(bf16[288,576]{1,0:T(8,128)(2,1)} %bitcast.86), channel_id=1, source_target_pairs={{0,24},{8,16},{16,8},{24,0},{1,25},{9,17},{17,9},{25,1},{2,26},{10... | collective-permute-start | bytes 995336 | tf_op jit(solution)/shard_map/ppermute | solution.py:55
  74.4 49.3 %reduce-scatter.4.cloned.1.call-start = ((), (), s32[]{:S(2)}) async-start(), calls=%async_computation.8 | async-start | bytes 1105920 | tf_op jit(solution)/shard_map/reduce_scatter | solution.py:74
  91.8 16.8 %copy-start.27 = (f32[1152]{0:T(1024)S(1)}, f32[1152]{0:T(1024)}, u32[]{:S(2)}) copy-start(f32[1152]{0:T(1024)} %get-tuple-element.128) | copy-start | bytes 13828
  91.8 2.6 collective-permute-start.3
  94.4 14.5 %copy-start.26 = (f32[1152]{0:T(1024)S(1)}, f32[1152]{0:T(1024)}, u32[]{:S(2)}) copy-start(f32[1152]{0:T(1024)} %get-tuple-element.127) | copy-start | bytes 13828
  94.4 14.8 %copy-start.28 = (f32[1152]{0:T(1024)S(1)}, f32[1152]{0:T(1024)}, u32[]{:S(2)}) copy-start(f32[1152]{0:T(1024)} %get-tuple-element.102) | copy-start | bytes 13828
  96.8 103.8 %reduce-scatter.6.cloned.1.call-start = ((), (), s32[]{:S(2)}) async-start(), calls=%async_computation.9 | async-start | bytes 1105920 | tf_op jit(solution)/shard_map/reduce_scatter | solution.py:74
  111.0 41.1 %collective-permute-start.4 = (bf16[288,1076]{1,0:T(8,128)(2,1)}, bf16[288,1076]{1,0:T(8,128)(2,1)S(1)}, u32[]{:S(2)}, u32[]{:S(2)}) collective-permute-start(bf16[288,1076]{1,0:T(8,128)(2,1)} %bitcast.8.after_ref.refs_0_), channel_id=1, source_target_pairs={{0,8},{8,0},{16,24},{24,16},{1,9},{9,1},{17,25},{25,17},{2,10},{10... | collective-permute-start | bytes 1859336 | tf_op jit(solution)/shard_map/ppermute | solution.py:55
  112.5 39.6 %collective-permute-start.5 = (bf16[288,1076]{1,0:T(8,128)(2,1)}, bf16[288,1076]{1,0:T(8,128)(2,1)S(1)}, u32[]{:S(2)}, u32[]{:S(2)}) collective-permute-start(bf16[288,1076]{1,0:T(8,128)(2,1)} %bitcast.8.after_ref.refs_0_), channel_id=1, source_target_pairs={{0,16},{8,24},{16,0},{24,8},{1,17},{9,25},{17,1},{25,9},{2,18},{10... | collective-permute-start | bytes 1859336 | tf_op jit(solution)/shard_map/ppermute | solution.py:55
  114.0 38.1 %collective-permute-start.6 = (bf16[288,1076]{1,0:T(8,128)(2,1)}, bf16[288,1076]{1,0:T(8,128)(2,1)S(1)}, u32[]{:S(2)}, u32[]{:S(2)}) collective-permute-start(bf16[288,1076]{1,0:T(8,128)(2,1)} %bitcast.8.after_ref.refs_0_), channel_id=1, source_target_pairs={{0,24},{8,16},{16,8},{24,0},{1,25},{9,17},{17,9},{25,1},{2,26},{10... | collective-permute-start | bytes 1859336 | tf_op jit(solution)/shard_map/ppermute | solution.py:55
  171.7 2.7 collective-permute-start.7
  190.9 38.8 %all-to-all-start.2 = ((bf16[4,288,1076]{2,1,0:T(8,128)(2,1)}), bf16[4,288,1076]{2,1,0:T(8,128)(2,1)}, u32[]{:S(2)}, u32[]{:S(2)}) async-start(bf16[4,288,1076]{2,1,0:T(8,128)(2,1)} %get-tuple-element.70), calls=%async_computation.3 | async-start | bytes 5308416 | tf_op jit(solution)/shard_map/all_to_all | solution.py:69
  250.5 27.8 %collective-permute-start.8 = (bf16[4,304,768]{2,1,0:T(8,128)(2,1)}, bf16[4,304,768]{2,1,0:T(8,128)(2,1)}, u32[]{:S(2)}, u32[]{:S(2)}) collective-permute-start(bf16[4,304,768]{2,1,0:T(8,128)(2,1)} %get-tuple-element.77), channel_id=1, source_target_pairs={{0,1},{1,0},{2,3},{3,2},{4,5},{5,4},{6,7},{7,6},{8,9},{9,8},{10,11... | collective-permute-start | bytes 5603336 | tf_op jit(solution)/shard_map/ppermute | solution.py:39
  250.6 23.5 %all-to-all-start.3 = ((bf16[4,288,576]{2,1,0:T(8,128)(2,1)}), bf16[4,288,576]{2,1,0:T(8,128)(2,1)}, u32[]{:S(2)}, u32[]{:S(2)}) async-start(bf16[4,288,576]{2,1,0:T(8,128)(2,1)} %get-tuple-element.78), calls=%async_computation.6 | async-start | bytes 2949120 | tf_op jit(solution)/shard_map/all_to_all | solution.py:69
  254.9 101.5 %reduce-scatter.8.cloned.1.call-start = ((), (), s32[]{:S(2)}) async-start(), calls=%async_computation.10 | async-start | bytes 2334720 | tf_op jit(solution)/shard_map/reduce_scatter | solution.py:74
  284.8 1.3 collective-permute-start.9
  286.2 4.4 %collective-permute-start.10 = (f32[16,1152]{1,0:T(8,128)S(1)}, f32[16,1152]{1,0:T(8,128)S(1)}, u32[]{:S(2)}, u32[]{:S(2)}) collective-permute-start(f32[16,1152]{1,0:T(8,128)S(1)} %fusion.73), channel_id=1, source_target_pairs={{0,2},{2,0},{4,6},{6,4},{1,3},{3,1},{5,7},{7,5},{8,10},{10,8},{12,... | collective-permute-start | bytes 221192 | tf_op jit(solution)/shard_map/ppermute | solution.py:86
  287.7 19.9 %copy-start.6 = (bf16[288,1076]{1,0:T(8,128)(2,1)S(1)}, bf16[288,1076]{1,0:T(8,128)(2,1)}, u32[]{:S(2)}) copy-start(bf16[288,1076]{1,0:T(8,128)(2,1)} %add_reduce_fusion.after_ref) | copy-start | bytes 1859332
  287.7 19.9 %copy-start.12 = (bf16[288,576]{1,0:T(8,128)(2,1)S(1)}, bf16[288,576]{1,0:T(8,128)(2,1)}, u32[]{:S(2)}) copy-start(bf16[288,576]{1,0:T(8,128)(2,1)} %reduce_sum.118) | copy-start | bytes 995332
  290.6 11.0 %collective-permute-start.11 = (f32[16,1152]{1,0:T(8,128)S(1)}, f32[16,1152]{1,0:T(8,128)S(1)}, u32[]{:S(2)}, u32[]{:S(2)}) collective-permute-start(f32[16,1152]{1,0:T(8,128)S(1)} %add.394), channel_id=1, source_target_pairs={{0,4},{2,6},{4,0},{6,2},{1,5},{3,7},{5,1},{7,3},{8,12},{10,14},{12... | collective-permute-start | bytes 221192 | tf_op jit(solution)/shard_map/ppermute | solution.py:86
  301.6 4.4 %collective-permute-start.12 = (f32[16,1152]{1,0:T(8,128)S(1)}, f32[16,1152]{1,0:T(8,128)S(1)}, u32[]{:S(2)}, u32[]{:S(2)}) collective-permute-start(f32[16,1152]{1,0:T(8,128)S(1)} %add.395), channel_id=1, source_target_pairs={{0,8},{8,0},{16,24},{24,16},{1,9},{9,1},{17,25},{25,17},{2,10},{10... | collective-permute-start | bytes 221192 | tf_op jit(solution)/shard_map/ppermute | solution.py:86
  306.0 6.5 %collective-permute-start.13 = (f32[16,1152]{1,0:T(8,128)S(1)}, f32[16,1152]{1,0:T(8,128)S(1)}, u32[]{:S(2)}, u32[]{:S(2)}) collective-permute-start(f32[16,1152]{1,0:T(8,128)S(1)} %add.396), channel_id=1, source_target_pairs={{0,16},{8,24},{16,0},{24,8},{1,17},{9,25},{17,1},{25,9},{2,18},{10... | collective-permute-start | bytes 221192 | tf_op jit(solution)/shard_map/ppermute | solution.py:86
  308.9 37.8 %all-to-all-start.4 = ((bf16[4,72,1652]{2,1,0:T(8,128)(2,1)}), bf16[4,72,1652]{2,1,0:T(8,128)(2,1)S(1)}, u32[]{:S(2)}, u32[]{:S(2)}) async-start(bf16[4,72,1652]{2,1,0:T(8,128)(2,1)} %pad_maximum_fusion.3), calls=%async_computation.7 | async-start | bytes 1916928 | tf_op jit(solution)/shard_map/all_to_all | solution.py:65
  (27 other events, 110.2 us)
Sparse Core Ops, SparseCore 0:
  74.6 27.1 all-gather.8
Sparse Core Ops, SparseCore 1:
  96.9 25.3 reduce-scatter.3
  176.9 23.6 reduce-scatter.5
  285.0 48.8 reduce-scatter.7
